TPU v7x, 32 devices: a whole 2x2x4 slice. The times are simulated.
32 devices in a mesh: dp: 4 (over z), shard: 8 (over y, x, core).
Axes of the slice: x: 2, y: 2, z: 4, core: 2. Of those that a mesh axis runs over, the one named last changes fastest.
Arguments:
- tokens_in: bfloat16 [2, 3072, 1536], P(None, ('dp', 'shard')), may hold values from -6 to 6
- in_weight: bfloat16 [1536, 4608], P(('dp', 'shard')), may hold values from -0.15625 to 0.15625
- conv_weight: bfloat16 [1536, 3], P(('dp', 'shard')), may hold values from -3.5 to 3.5
- out_weight: bfloat16 [1536, 1536], P(('dp', 'shard')), may hold values from -0.15625 to 0.15625
- norm_gain: bfloat16 [1536], P(('dp', 'shard')), may hold values from 0.25 to 1.75
- ff_gain: bfloat16 [1536], P(('dp', 'shard')), may hold values from 0.25 to 1.75
- gate_weight: bfloat16 [1536, 6912], P(('dp', 'shard')), may hold values from -0.15625 to 0.15625
- up_weight: bfloat16 [1536, 6912], P(('dp', 'shard')), may hold values from -0.15625 to 0.15625
- down_weight: bfloat16 [1536, 6912], P(('dp', 'shard')), may hold values from -0.078125 to 0.078125
- cotangent: bfloat16 [2, 3072, 1536], P(None, ('dp', 'shard')), may hold values from -6 to 6
- deal_table: int32 [2, 4, 8, 8], P(None, 'dp', 'shard'), may hold values from 0 to 7, each once within a row
- seq_lengths: int32 [2, 4, 3], P(None, 'dp'), may hold values from 1 to 720, 768 in all within a row
Outputs:
- block_out: bfloat16 [2, 3072, 1536], P(None, ('dp', 'shard'))
- tokens_grad: bfloat16 [2, 3072, 1536], P(None, ('dp', 'shard'))
- in_grad: float32 [1536, 4608], P(('dp', 'shard'))
- conv_grad: float32 [1536, 3], P(('dp', 'shard'))
- out_grad: float32 [1536, 1536], P(('dp', 'shard'))
- norm_gain_grad: float32 [1536], P(('dp', 'shard'))
- ff_gain_grad: float32 [1536], P(('dp', 'shard'))
- gate_grad: float32 [1536, 6912], P(('dp', 'shard'))
- up_grad: float32 [1536, 6912], P(('dp', 'shard'))
- down_grad: float32 [1536, 6912], P(('dp', 'shard'))
Inputs may be any that keep to these rules, and one draw needn't show every extreme that they name: Each row deal_table[m, g, j, :] is a permutation of the shard indices: natural piece i of shard device j of group g lies in slot j of shard device deal_table[m, g, j, i]. `seq_lengths`: each row holds 3 lengths summing to 768, the largest exactly 720.
All inputs are finite; a program needn't handle non-finite values.
Results may differ from a plain program's by a relative error of at most 0.015.
Values may be sent and summed in bfloat16 or wider, within the bound.
No kernel may reach another device: no remote copies, remote signals or barrier semaphores. Data moves between devices by JAX's collectives and lax.ppermute only.
A program may use at most 384 MiB of HBM per device.

v0:
```python
import jax
import jax.numpy as jnp
from jax import lax
from jax.sharding import PartitionSpec as P

EPS = 1e-05


def shifted(block, axis, distance):
    devices = range(lax.axis_size(axis))
    route = [(i - distance, i) for i in devices if i - distance in devices]
    return lax.ppermute(block, axis, route)


def matmul(former, latter):
    return jnp.dot(former, latter, preferred_element_type=jnp.float32)


def times_trans(former, latter):
    return lax.dot_general(
        former, latter, (((1,), (1,)), ((), ())), preferred_element_type=jnp.float32
    )


def contract(former, latter):
    return lax.dot_general(
        former, latter, (((0,), (0,)), ((), ())), preferred_element_type=jnp.float32
    )


def body(
    tokens_in,
    in_weight,
    conv_weight,
    out_weight,
    norm_gain,
    ff_gain,
    gate_weight,
    up_weight,
    down_weight,
    cotangent,
    deal_table,
    seq_lengths,
):
    batches, rows_dev, model_width = tokens_in.shape
    shards = lax.axis_size("shard")
    piece_rows = rows_dev // shards
    own_index = lax.axis_index("shard")
    full_in, full_out, full_gate, full_up, full_down, full_conv, full_norm, full_ff = (
        lax.all_gather(in_weight, ("dp", "shard"), axis=0, tiled=True),
        lax.all_gather(out_weight, ("dp", "shard"), axis=0, tiled=True),
        lax.all_gather(gate_weight, ("dp", "shard"), axis=0, tiled=True),
        lax.all_gather(up_weight, ("dp", "shard"), axis=0, tiled=True),
        lax.all_gather(down_weight, ("dp", "shard"), axis=0, tiled=True),
        lax.all_gather(conv_weight, ("dp", "shard"), axis=0, tiled=True),
        lax.all_gather(norm_gain, ("dp", "shard"), axis=0, tiled=True),
        lax.all_gather(ff_gain, ("dp", "shard"), axis=0, tiled=True),
    )
    deal_rows = deal_table[:, 0, 0, :]
    batch_index = jnp.arange(batches)[:, None]
    split_in = tokens_in.reshape(batches, shards, piece_rows, model_width)
    arrived = lax.all_to_all(split_in, "shard", split_axis=1, concat_axis=1, tiled=True)
    natural = arrived[batch_index, deal_rows]
    tokens = natural.reshape(batches * rows_dev, model_width).astype(jnp.float32)
    lengths = seq_lengths[:, 0, :]
    starts = jnp.cumsum(lengths, axis=1) - lengths
    places = own_index * rows_dev + jnp.arange(rows_dev, dtype=jnp.int32)
    seq_start = jnp.max(
        jnp.where(starts[:, None, :] <= places[None, :, None], starts[:, None, :], 0), axis=2
    )
    offset = places[None, :] - seq_start
    after_one = (offset >= 1).astype(jnp.float32).reshape(-1, 1)
    after_two = (offset >= 2).astype(jnp.float32).reshape(-1, 1)
    inv_one = lax.rsqrt(jnp.mean(tokens * tokens, axis=1, keepdims=True) + EPS)
    unit_one = tokens * inv_one
    normed = (unit_one * full_norm.astype(jnp.float32)).astype(jnp.bfloat16)
    projected = matmul(normed, full_in)
    b_part = projected[:, :model_width]
    c_part = projected[:, model_width : 2 * model_width]
    x_part = projected[:, 2 * model_width :]
    product = (b_part * x_part).astype(jnp.bfloat16)
    framed = product.reshape(batches, rows_dev, model_width)
    edge_rows = shifted(framed[:, rows_dev - 2 :, :], "shard", 1)
    padded = jnp.concatenate([edge_rows, framed], axis=1)
    prev_two = padded[:, :rows_dev].reshape(-1, model_width).astype(jnp.float32) * after_two
    prev_one = padded[:, 1 : rows_dev + 1].reshape(-1, model_width).astype(jnp.float32) * after_one
    product_wide = product.astype(jnp.float32)
    conv_taps = full_conv.astype(jnp.float32)
    conv_out = (
        prev_two * conv_taps[:, 0] + prev_one * conv_taps[:, 1] + product_wide * conv_taps[:, 2]
    )
    gated_mix = (c_part * conv_out).astype(jnp.bfloat16)
    hidden = tokens + matmul(gated_mix, full_out)
    inv_two = lax.rsqrt(jnp.mean(hidden * hidden, axis=1, keepdims=True) + EPS)
    unit_two = hidden * inv_two
    normed_ff = (unit_two * full_ff.astype(jnp.float32)).astype(jnp.bfloat16)
    gate_val = matmul(normed_ff, full_gate)
    up_val = matmul(normed_ff, full_up)
    sigmoid_val = jax.nn.sigmoid(gate_val)
    silu_val = gate_val * sigmoid_val
    ff_inner = (silu_val * up_val).astype(jnp.bfloat16)
    block_val = hidden + times_trans(ff_inner, full_down)
    block_out = block_val.astype(jnp.bfloat16).reshape(batches, rows_dev, model_width)
    back_in, back_out, back_gate, back_up, back_down, back_conv, back_norm, back_ff = (
        lax.all_gather(in_weight, ("dp", "shard"), axis=0, tiled=True),
        lax.all_gather(out_weight, ("dp", "shard"), axis=0, tiled=True),
        lax.all_gather(gate_weight, ("dp", "shard"), axis=0, tiled=True),
        lax.all_gather(up_weight, ("dp", "shard"), axis=0, tiled=True),
        lax.all_gather(down_weight, ("dp", "shard"), axis=0, tiled=True),
        lax.all_gather(conv_weight, ("dp", "shard"), axis=0, tiled=True),
        lax.all_gather(norm_gain, ("dp", "shard"), axis=0, tiled=True),
        lax.all_gather(ff_gain, ("dp", "shard"), axis=0, tiled=True),
    )
    cot_rows = cotangent.reshape(-1, model_width)
    d_inner = matmul(cot_rows, back_down)
    silu_slope = sigmoid_val * (1.0 + gate_val * (1.0 - sigmoid_val))
    d_gate = (d_inner * up_val * silu_slope).astype(jnp.bfloat16)
    d_up = (d_inner * silu_val).astype(jnp.bfloat16)
    d_normed_ff = times_trans(d_gate, back_gate) + times_trans(d_up, back_up)
    scaled_ff = d_normed_ff * back_ff.astype(jnp.float32)
    d_hidden = cot_rows.astype(jnp.float32) + inv_two * (
        scaled_ff - unit_two * jnp.mean(scaled_ff * unit_two, axis=1, keepdims=True)
    )
    d_branch = d_hidden.astype(jnp.bfloat16)
    d_gated = times_trans(d_branch, back_out)
    grad_c = d_gated * conv_out
    grad_conv = d_gated * c_part
    back_taps = back_conv.astype(jnp.float32)
    front_one = (grad_conv * after_one * back_taps[:, 1]).reshape(batches, rows_dev, model_width)
    front_two = (grad_conv * after_two * back_taps[:, 0]).reshape(batches, rows_dev, model_width)
    contrib = jnp.pad(front_two, ((0, 0), (0, 2), (0, 0))) + jnp.pad(
        front_one, ((0, 0), (1, 1), (0, 0))
    )
    tail_rows = contrib[:, :2]
    received = shifted(tail_rows, "shard", -1)
    own_terms = (grad_conv * back_taps[:, 2]).reshape(batches, rows_dev, model_width) + contrib[
        :, 2:
    ]
    d_product = own_terms + jnp.concatenate(
        [jnp.zeros((batches, rows_dev - 2, model_width), jnp.float32), received], axis=1
    )
    d_product = d_product.reshape(-1, model_width).astype(jnp.bfloat16).astype(jnp.float32)
    grad_proj = jnp.concatenate([d_product * x_part, grad_c, d_product * b_part], axis=1).astype(
        jnp.bfloat16
    )
    d_normed = times_trans(grad_proj, back_in)
    scaled_one = d_normed * back_norm.astype(jnp.float32)
    d_tokens = d_hidden + inv_one * (
        scaled_one - unit_one * jnp.mean(scaled_one * unit_one, axis=1, keepdims=True)
    )
    d_pieces = d_tokens.astype(jnp.bfloat16).reshape(batches, shards, piece_rows, model_width)
    inverse = jnp.argsort(deal_rows, axis=1)
    outgoing = d_pieces[batch_index, inverse]
    returned = lax.all_to_all(outgoing, "shard", split_axis=1, concat_axis=1, tiled=True)
    tokens_grad = returned.reshape(batches, rows_dev, model_width)
    norm_prod = d_normed * unit_one
    ff_prod = d_normed_ff * unit_two
    tap_zero = grad_conv * prev_two
    tap_one = grad_conv * prev_one
    tap_two = grad_conv * product_wide
    small_cols = jnp.stack(
        [jnp.sum(matrix, axis=0) for matrix in (norm_prod, ff_prod, tap_zero, tap_one, tap_two)],
        axis=1,
    )
    in_term = contract(normed, grad_proj)
    out_term = contract(gated_mix, d_branch)
    gate_term = contract(normed_ff, d_gate)
    up_term = contract(normed_ff, d_up)
    down_term = contract(cot_rows, ff_inner)
    grad_sum = (
        lax.psum_scatter(in_term, ("dp", "shard"), scatter_dimension=0, tiled=True),
        lax.psum_scatter(out_term, ("dp", "shard"), scatter_dimension=0, tiled=True),
        lax.psum_scatter(gate_term, ("dp", "shard"), scatter_dimension=0, tiled=True),
        lax.psum_scatter(up_term, ("dp", "shard"), scatter_dimension=0, tiled=True),
        lax.psum_scatter(down_term, ("dp", "shard"), scatter_dimension=0, tiled=True),
        lax.psum_scatter(small_cols, ("dp", "shard"), scatter_dimension=0, tiled=True),
    )
    in_grad, out_grad, gate_grad, up_grad, down_grad, small_grad = grad_sum
    norm_gain_grad = small_grad[:, 0]
    ff_gain_grad = small_grad[:, 1]
    conv_grad = small_grad[:, 2:5]
    return (
        block_out,
        tokens_grad,
        in_grad,
        conv_grad,
        out_grad,
        norm_gain_grad,
        ff_gain_grad,
        gate_grad,
        up_grad,
        down_grad,
    )


def solution(mesh):
    placed = (
        P(None, ("dp", "shard"), None),
        P(("dp", "shard"), None),
        P(("dp", "shard"), None),
        P(("dp", "shard"), None),
        P(("dp", "shard")),
        P(("dp", "shard")),
        P(("dp", "shard"), None),
        P(("dp", "shard"), None),
        P(("dp", "shard"), None),
        P(None, ("dp", "shard"), None),
        P(None, "dp", "shard", None),
        P(None, "dp", None),
    )
    return jax.shard_map(
        body,
        mesh=mesh,
        in_specs=placed,
        out_specs=(
            P(None, ("dp", "shard"), None),
            P(None, ("dp", "shard"), None),
            P(("dp", "shard"), None),
            P(("dp", "shard"), None),
            P(("dp", "shard"), None),
            P(("dp", "shard")),
            P(("dp", "shard")),
            P(("dp", "shard"), None),
            P(("dp", "shard"), None),
            P(("dp", "shard"), None),
        ),
        check_vma=False,
    )
```

profile of v0, /device:TPU:0, one launch (start us, length us, event | category | flops | bytes accessed | tf_op | source)
XLA Modules:
  0.0 2333.2 jit_solution(14941423816352421106)
XLA Ops:
  12.1 5.2 all-to-all-start
  17.3 45.2 %all-gather = bf16[32,48,3]{1,2,0:T(4,128)(2,1)S(1)} all-gather(bf16[1,48,3]{1,2,0:T(4,128)(2,1)S(1)} %bitcast.86), channel_id=1, replica_groups=mesh['dp'=4,'shard'=8] {'dp','shard'}, dimensions={0}, use_global_device_ids=true | all-gather | bytes 9504 | tf_op jit(solution)/shard_map/all_gather | solution.py:55
  63.1 40.3 %all-reduce.5 = (bf16[1536]{0:T(1024)(128)(2,1)S(1)}, bf16[1536]{0:T(1024)(128)(2,1)}) all-reduce(bf16[1536]{0:T(1024)(128)(2,1)S(1)} %dynamic-update-slice, bf16[1536]{0:T(1024)(128)(2,1)S(1)} %dynamic-update-slice.1), channel_id=1, replica_groups=mesh['dp'=4,'shard'=8] {'dp','shard'}, use_global_device_ids=true, to_apply=%add.3 | all-reduce | flops 3072 | bytes 12288
  107.5 11.3 all-gather.7.cloned.1.call-done
  118.8 7.0 fusion.32
  127.4 3.2 collective-permute-start
  138.0 45.8 %all-gather.9.cloned.1.call-done = bf16[1536,1536]{1,0:T(8,128)(2,1)} async-done(((bf16[48,1536]{1,0:T(8,128)(2,1)}), bf16[1536,1536]{1,0:T(8,128)(2,1)}) %all-gather.9.cloned.1.call-update) | async-done | bytes 4718608 | tf_op jit(solution)/shard_map/all_gather | solution.py:51
  183.8 4.1 multiply_reduce_fusion.5
  189.9 131.5 %all-gather.11.cloned.1.call-done = bf16[1536,6912]{1,0:T(8,128)(2,1)} async-done(((bf16[48,6912]{1,0:T(8,128)(2,1)}), bf16[1536,6912]{1,0:T(8,128)(2,1)}) %all-gather.11.cloned.1.call-update) | async-done | bytes 21233680 | tf_op jit(solution)/shard_map/all_gather | solution.py:52
  321.4 13.8 fusion.34
  335.2 123.0 %all-gather.13.cloned.1.call-done = bf16[1536,6912]{1,0:T(8,128)(2,1)} async-done(((bf16[48,6912]{1,0:T(8,128)(2,1)}), bf16[1536,6912]{1,0:T(8,128)(2,1)}) %all-gather.13.cloned.1.call-update) | async-done | bytes 21233680 | tf_op jit(solution)/shard_map/all_gather | solution.py:53
  458.2 13.8 fusion.35
  472.0 123.0 %all-gather.15.cloned.1.call-done = bf16[1536,6912]{1,0:T(8,128)(2,1)} async-done(((bf16[48,6912]{1,0:T(8,128)(2,1)}), bf16[1536,6912]{1,0:T(8,128)(2,1)}) %all-gather.15.cloned.1.call-update) | async-done | bytes 21233680 | tf_op jit(solution)/shard_map/all_gather | solution.py:54
  594.9 14.9 multiply_convert_fusion
  609.9 12.2 fusion.36
  622.1 12.9 multiply_reduce_fusion.1
  635.1 1.9 multiply_add_fusion
  637.1 5.6 fusion.7
  648.6 10.9 multiply_reduce_fusion.2
  660.9 5.1 fusion.20
  667.6 12.7 fusion.17
  681.3 18.5 fusion.37
  700.1 18.6 fusion.38
  719.8 18.5 convolution_bitcast_fusion
  738.2 42.7 %copy.67 = f32[1536,6912]{1,0:T(8,128)} copy(f32[1536,6912]{0,1:T(8,128)} %convolution_bitcast_fusion) | data formatting | bytes 84934656
  786.4 4.7 all-to-all-start.1
  791.1 13.3 fusion.1
  808.8 89.1 %reduce-scatter.13.cloned.1.call-done = f32[48,1536]{1,0:T(8,128)} async-done(((f32[1536,1536]{1,0:T(8,128)}), f32[48,1536]{1,0:T(8,128)}) %reduce-scatter.13.cloned.1.call-update) | async-done | bytes 294928 | tf_op jit(solution)/shard_map/reduce_scatter | solution.py:172
  897.9 271.1 %reduce-scatter.11.cloned.1.call-done = f32[48,4608]{1,0:T(8,128)} async-done(((f32[1536,4608]{1,0:T(8,128)}), f32[48,4608]{1,0:T(8,128)}) %reduce-scatter.11.cloned.1.call-update) | async-done | bytes 884752 | tf_op jit(solution)/shard_map/reduce_scatter | solution.py:171
  1169.0 386.8 %reduce-scatter.15.cloned.1.call-done = f32[48,6912]{1,0:T(8,128)} async-done(((f32[1536,6912]{1,0:T(8,128)}), f32[48,6912]{1,0:T(8,128)}) %reduce-scatter.15.cloned.1.call-update) | async-done | bytes 1327120 | tf_op jit(solution)/shard_map/reduce_scatter | solution.py:173
  1555.7 384.5 %reduce-scatter.17.cloned.1.call-done = f32[48,6912]{1,0:T(8,128)} async-done(((f32[1536,6912]{1,0:T(8,128)}), f32[48,6912]{1,0:T(8,128)}) %reduce-scatter.17.cloned.1.call-update) | async-done | bytes 1327120 | tf_op jit(solution)/shard_map/reduce_scatter | solution.py:174
  1940.3 386.2 %reduce-scatter.21.cloned.1.call-done = f32[48,6912]{1,0:T(8,128)} async-done(((f32[1536,6912]{1,0:T(8,128)}), f32[48,6912]{1,0:T(8,128)}) %reduce-scatter.21.cloned.1.call-update) | async-done | bytes 1327120
  (184 shorter events, 41.3 us)
Async XLA Ops:
  7.2 111.6 %all-gather.7.cloned.1.call-start = ((), (), s32[]{:S(2)}) async-start(), calls=%async_computation.8 | async-start | bytes 14598144 | tf_op jit(solution)/shard_map/all_gather | solution.py:50
  7.9 175.8 %all-gather.9.cloned.1.call-start = ((), (), s32[]{:S(2)}) async-start(), calls=%async_computation.9 | async-start | bytes 4866048 | tf_op jit(solution)/shard_map/all_gather | solution.py:51
  8.7 312.7 %all-gather.11.cloned.1.call-start = ((), (), s32[]{:S(2)}) async-start(), calls=%async_computation.10 | async-start | bytes 21897216 | tf_op jit(solution)/shard_map/all_gather | solution.py:52
  9.4 448.8 %all-gather.13.cloned.1.call-start = ((), (), s32[]{:S(2)}) async-start(), calls=%async_computation.11 | async-start | bytes 21897216 | tf_op jit(solution)/shard_map/all_gather | solution.py:53
  10.0 585.0 %all-gather.15.cloned.1.call-start = ((), (), s32[]{:S(2)}) async-start(), calls=%async_computation.12 | async-start | bytes 21897216 | tf_op jit(solution)/shard_map/all_gather | solution.py:54
  10.6 6.7 copy-start.44
  10.6 51.9 %copy-start.42 = (s32[2,1,1,8]{3,2,1,0:T(1,128)S(1)}, s32[2,1,1,8]{3,2,1,0:T(1,128)}, u32[]{:S(2)}) copy-start(s32[2,1,1,8]{3,2,1,0:T(1,128)} %param.22) | copy-start | bytes 196
  10.6 52.0 %copy-start.45 = (bf16[48]{0:T(256)(128)(2,1)S(1)}, bf16[48]{0:T(256)(128)(2,1)}, u32[]{:S(2)}) copy-start(bf16[48]{0:T(256)(128)(2,1)} %param.16) | copy-start | bytes 292
  10.6 52.2 %copy-start.46 = (bf16[48]{0:T(256)(128)(2,1)S(1)}, bf16[48]{0:T(256)(128)(2,1)}, u32[]{:S(2)}) copy-start(bf16[48]{0:T(256)(128)(2,1)} %param.17) | copy-start | bytes 292
  10.6 93.5 %copy-start.41 = (s32[2,1,3]{2,1,0:T(1,128)S(1)}, s32[2,1,3]{2,1,0:T(1,128)}, u32[]{:S(2)}) copy-start(s32[2,1,3]{2,1,0:T(1,128)} %param.23) | copy-start | bytes 76
  12.1 93.2 %all-to-all-start = ((bf16[2,8,12,1536]{3,0,2,1:T(2,128)(2,1)}), bf16[2,8,12,1536]{3,0,2,1:T(2,128)(2,1)S(1)}, u32[]{:S(2)}, u32[]{:S(2)}) async-start(bf16[2,8,12,1536]{3,0,2,1:T(2,128)(2,1)} %bitcast), calls=%async_computation | async-start | bytes 1179648 | tf_op jit(solution)/shard_map/all_to_all | solution.py:62
  17.2 787.2 %reduce-scatter.19.cloned.1.call-start = ((), (), s32[]{:S(2)}) async-start(), calls=%async_computation.17 | async-start | bytes 811008
  107.5 18.3 copy-start.29
  127.4 6.7 collective-permute-start
  609.9 12.2 copy-start.9
  609.9 12.2 copy-start.6
  609.9 12.2 copy-start.40
  643.0 3.9 collective-permute-start.1
  647.6 11.9 copy-start.16
  647.6 11.9 copy-start.18
  648.6 10.9 copy-start.31
  648.6 10.9 copy-start.32
  648.6 10.9 copy-start.33
  648.6 10.9 copy-start.34
  648.6 12.3 copy-start.8
  660.9 237.0 %reduce-scatter.13.cloned.1.call-start = ((), (), s32[]{:S(2)}) async-start(), calls=%async_computation.14 | async-start | bytes 9732096 | tf_op jit(solution)/shard_map/reduce_scatter | solution.py:172
  666.0 502.9 %reduce-scatter.11.cloned.1.call-start = ((), (), s32[]{:S(2)}) async-start(), calls=%async_computation.13 | async-start | bytes 29196288 | tf_op jit(solution)/shard_map/reduce_scatter | solution.py:171
  680.3 875.4 %reduce-scatter.15.cloned.1.call-start = ((), (), s32[]{:S(2)}) async-start(), calls=%async_computation.15 | async-start | bytes 43794432 | tf_op jit(solution)/shard_map/reduce_scatter | solution.py:173
  699.8 1240.4 %reduce-scatter.17.cloned.1.call-start = ((), (), s32[]{:S(2)}) async-start(), calls=%async_computation.16 | async-start | bytes 43794432 | tf_op jit(solution)/shard_map/reduce_scatter | solution.py:174
  718.7 1607.7 %reduce-scatter.21.cloned.1.call-start = ((), (), s32[]{:S(2)}) async-start(), calls=%async_computation.18 | async-start | bytes 43794432
  784.9 6.2 copy-start.7
  786.4 21.6 all-to-all-start.1
  (30 other events, 62.2 us)
Sparse Core Ops, SparseCore 0:
  10.9 107.7 all-gather.6
  121.7 62.0 all-gather.8
  186.7 134.6 all-gather.10
  324.1 133.9 all-gather.12
  460.9 133.9 all-gather.14
  661.0 95.7 reduce-scatter.18
  763.2 134.6 reduce-scatter.12
  906.0 262.8 reduce-scatter.10
  1177.1 378.5 reduce-scatter.14
  1562.6 377.6 reduce-scatter.16
  1948.4 377.9 reduce-scatter.20
where the time goes:
time: 2340 us; the launch traced here: 2330 us
  waiting for transfers between devices  1960 us (84%)
  matrix products  182 us (8%)
  blocking collectives  85.5 us (4%)
  local copies, waits for them, and re-layouts  69.2 us (3%)
    unnamed x13, waiting for transfers between devices  389 us
    reduce_scatter x1, waiting for transfers between devices, body(): lax.psum_scatter(gate_term, ('dp', 'shard'), scatter_dimension=0, tiled=T...  387 us
    reduce_scatter x1, waiting for transfers between devices, body(): lax.psum_scatter(up_term, ('dp', 'shard'), scatter_dimension=0, tiled=True)  385 us
    reduce_scatter x1, waiting for transfers between devices, body(): lax.psum_scatter(in_term, ('dp', 'shard'), scatter_dimension=0, tiled=True)  271 us
    all_gather x1, waiting for transfers between devices, body(): lax.all_gather(gate_weight, ('dp', 'shard'), axis=0, tiled=True)  131 us
    all_gather x1, waiting for transfers between devices, body(): lax.all_gather(up_weight, ('dp', 'shard'), axis=0, tiled=True)  123 us
    all_gather x1, waiting for transfers between devices, body(): lax.all_gather(down_weight, ('dp', 'shard'), axis=0, tiled=True)  123 us
    reduce_scatter x1, waiting for transfers between devices, body(): lax.psum_scatter(out_term, ('dp', 'shard'), scatter_dimension=0, tiled=True)  89.1 us
  transfers between devices with their start and end apart: 15, of which 10 were waited for; matrix products, arithmetic and copies ran while one was open for 8% of the time, Pallas kernels for 0%

commit v1 on v0

v1 whole, which is shorter than its diff:
```python
import jax
import jax.numpy as jnp
from jax import lax
from jax.sharding import PartitionSpec as P

EPS = 1e-05
F32 = jnp.float32
BF16 = jnp.bfloat16
LANES = 128


def dot(former, latter, dims, out=F32):
    return lax.dot_general(
        former, latter, ((dims[0], dims[1]), ((), ())), preferred_element_type=F32
    ).astype(out)


def bits_of(count):
    return [1 << k for k in range(count.bit_length() - 1)]


def swap(value, bit):
    n = lax.axis_size("shard")
    return lax.ppermute(value, "shard", [(i, i ^ bit) for i in range(n)])


def route(outer, turn):
    turn = turn % len(outer)
    return outer[turn:] + outer[:turn]


def last_of(index, order):
    return [bit for bit in order if index & bit][-1]


def by_count(n):
    return sorted(range(1, n), key=lambda index: (bin(index).count("1"), index))


def plane_gather(parts):
    n = lax.axis_size("shard")
    outer = bits_of(n)[1:]
    near = []
    for turn, part in enumerate(parts):
        order = route(outer, turn)
        held = {0: part}
        for e in by_count(n // 2):
            bit = last_of(2 * e, order)
            held[e] = swap(held[e ^ (bit >> 1)], bit)
        near.append([held[e] for e in range(n // 2)])
    far = [[swap(block, 1) for block in blocks] for blocks in near]
    return jnp.stack([jnp.stack([jnp.stack(b) for b in half]) for half in (near, far)])


def plane_reduce(near, far):
    n = lax.axis_size("shard")
    outer = bits_of(n)[1:]
    sums = []
    for turn in range(near.shape[0]):
        order = route(outer, turn)
        came = swap(far[turn], 1)
        held = {e: near[turn, e] + came[e].astype(F32) for e in range(n // 2)}
        for e in reversed(by_count(n // 2)):
            bit = last_of(2 * e, order)
            held[e ^ (bit >> 1)] = held[e ^ (bit >> 1)] + swap(held[e].astype(BF16), bit).astype(F32)
        sums.append(held[0])
    return jnp.stack(sums)


def plane_deal(blocks, order):
    held = list(blocks)
    for bit in order:
        picked = [r for r in range(len(held)) if r & bit]
        came = swap(jnp.stack([held[r] for r in picked]), bit)
        for place, r in enumerate(picked):
            held[r] = came[place]
    return held


def line_gather(block):
    n = lax.axis_size("dp")
    z = lax.axis_index("dp")
    ups, downs = {0: block}, {0: block}
    for k in range(1, n):
        ups[k] = lax.ppermute(ups[k - 1], "dp", [(i, i + 1) for i in range(k - 1, n - 1)])
        downs[k] = lax.ppermute(downs[k - 1], "dp", [(i + 1, i) for i in range(n - k)])
    return [block] + [jnp.where(z + d < n, downs[d], ups[n - d]) for d in range(1, n)]


def line_reduce(terms):
    n = lax.axis_size("dp")
    up = down = None
    for d in range(n - 1, 0, -1):
        going = terms[d] if up is None else terms[d] + up.astype(F32)
        up = lax.ppermute(going.astype(BF16), "dp", [(i, i + 1) for i in range(n - d)])
        going = terms[n - d] if down is None else terms[n - d] + down.astype(F32)
        down = lax.ppermute(going.astype(BF16), "dp", [(i, i - 1) for i in range(d, n)])
    return terms[0] + up.astype(F32) + down.astype(F32)


def turned(value, blocks, amount):
    width = value.shape[-1] // blocks
    out = value
    for k in range(1, blocks):
        out = jnp.where(amount == k, jnp.roll(value, -k * width, axis=-1), out)
    return out


def xor_blocks(value, axis, n):
    index = lax.axis_index("shard")
    for bit in bits_of(n):
        shape = value.shape
        split = value.reshape(shape[:axis] + (n // (2 * bit), 2, bit) + shape[axis + 1 :])
        low = lax.slice_in_dim(split, 0, 1, axis=axis + 1)
        high = lax.slice_in_dim(split, 1, 2, axis=axis + 1)
        flipped = jnp.concatenate([high, low], axis=axis + 1)
        value = jnp.where((index & bit) != 0, flipped, split).reshape(shape)
    return value


def body(
    tokens_in,
    in_weight,
    conv_weight,
    out_weight,
    norm_gain,
    ff_gain,
    gate_weight,
    up_weight,
    down_weight,
    cotangent,
    deal_table,
    seq_lengths,
):
    batches, rows_dev, width = tokens_in.shape
    n, n_dp = lax.axis_size("shard"), lax.axis_size("dp")
    half = n // 2
    me, z = lax.axis_index("shard"), lax.axis_index("dp")
    group = n * rows_dev
    piece_rows = rows_dev // n
    own_rows, hidden_units = gate_weight.shape
    total = batches * group
    outer = bits_of(n)[1:]
    order_a, order_b = [1] + route(outer, 0), [1] + route(outer, 1)
    zblock = n * own_rows
    channels = n_dp * own_rows

    whole = hidden_units // (LANES * n) * LANES
    rest = hidden_units // n - whole

    def pick(stacked, r):
        return lax.dynamic_index_in_dim(stacked, me ^ r, 0, keepdims=False)

    def spread_columns(weight):
        return jnp.stack(
            [
                jnp.concatenate(
                    [
                        weight[:, s * whole : (s + 1) * whole],
                        weight[:, n * whole + s * rest : n * whole + (s + 1) * rest],
                    ],
                    axis=1,
                )
                for s in range(n)
            ]
        )

    def join_columns(blocks):
        return jnp.concatenate(
            [blocks[s, :, :whole] for s in range(n)] + [blocks[s, :, whole:] for s in range(n)],
            axis=1,
        )

    place = jnp.arange(zblock, dtype=jnp.int32)
    arrival = ((place // own_rows) ^ me) * own_rows + place % own_rows
    to_natural = (arrival[:, None] == place[None, :]).astype(BF16)

    def spread(stacked, order):
        came = plane_deal([pick(stacked, r) for r in range(n)], order)
        block = jnp.concatenate(came, axis=0)
        return dot(block, to_natural, ((0,), (0,)), BF16)

    def collect(summed, order):
        rows = dot(to_natural, summed.astype(BF16), ((1,), (1,)), BF16)
        rows = rows.reshape(n, own_rows, -1)
        came = plane_deal([rows[r] for r in range(n)], order)
        stacked = jnp.stack(came)
        return jnp.stack([pick(stacked, s) for s in range(n)])

    def line_matrix(block):
        return jnp.concatenate(line_gather(block), axis=1)

    tok_turned = turned(tokens_in, n_dp, z)
    tok_all = plane_gather([tok_turned[m] for m in range(batches)]).reshape(total, width)
    cot_turned = turned(cotangent, n_dp, z)
    cot_all = plane_gather([cot_turned[m] for m in range(batches)]).reshape(total, width)

    out_aug = jnp.concatenate(
        [out_weight, conv_weight, jnp.zeros((own_rows, LANES - conv_weight.shape[1]), BF16)], axis=1
    )
    out_lines = jnp.stack(line_gather(out_aug))
    in_parts = in_weight.reshape(own_rows, 3 * n_dp, n, own_rows).transpose(2, 0, 1, 3)
    in_parts = in_parts.reshape(n, own_rows, 3 * channels)
    gains = jnp.stack([norm_gain, ff_gain], axis=1)
    gain_cols = jnp.pad(gains, ((0, 0), (0, 14)))
    in_parts = jnp.concatenate(
        [in_parts, jnp.broadcast_to(gain_cols[None], (n,) + gain_cols.shape)], axis=2
    )
    in_full = line_matrix(spread(in_parts, order_b))
    gate_t = line_matrix(spread(spread_columns(gate_weight), order_a))
    up_t = line_matrix(spread(spread_columns(up_weight), order_b))
    down_t = line_matrix(spread(spread_columns(down_weight), order_a))
    in_t = in_full[: 3 * channels]
    gain_one = in_full[3 * channels].astype(F32)
    gain_two = turned(in_full[3 * channels + 1], n_dp, n_dp - z).astype(F32)
    natural_lines = out_lines[0][None]
    stacked_lines = jnp.stack(
        [lax.dynamic_index_in_dim(out_lines, (k - z) % n_dp, 0, keepdims=False) for k in range(n_dp)]
    ).reshape(channels, width + LANES)
    out_full = stacked_lines[:, :width]
    taps = stacked_lines[:, width : width + conv_weight.shape[1]].astype(F32).T

    table = deal_table[:, 0, 0, :].astype(F32)
    seen = table[None]
    for bit in bits_of(n):
        seen = jnp.concatenate([seen, swap(seen, bit)], axis=0)
    deal = xor_blocks(seen, 0, n).astype(jnp.int32)
    deal = deal.transpose(1, 0, 2)
    m_index = jnp.arange(batches, dtype=jnp.int32)[:, None, None, None]
    j_index = jnp.arange(n, dtype=jnp.int32)[None, :, None, None]
    i_index = jnp.arange(n, dtype=jnp.int32)[None, None, :, None]
    t_index = jnp.arange(piece_rows, dtype=jnp.int32)[None, None, None, :]

    def arrival_row(m, holder, row):
        rel = holder ^ me
        return (((rel & 1) * batches + m) * half + (rel >> 1)) * rows_dev + row

    source = arrival_row(m_index, deal[:, :, :, None], j_index * piece_rows + t_index)
    source = source.reshape(total)
    columns = jnp.arange(total, dtype=jnp.int32)
    deal_mat = (source[:, None] == columns[None, :]).astype(BF16)
    own_source = lax.dynamic_index_in_dim(source.reshape(batches, n, rows_dev), me, 1, keepdims=False)
    own_mat = (own_source.reshape(-1)[:, None] == columns[None, :]).astype(BF16)
    inverse = jnp.sum(jnp.where(deal == me, jnp.arange(n, dtype=jnp.int32)[None, None, :], 0), axis=2)
    slot_source = arrival_row(
        m_index[:, :, 0], j_index[:, :, 0], inverse[:, :, None] * piece_rows + t_index[:, 0]
    )
    slot_mat = (slot_source.reshape(-1)[:, None] == columns[None, :]).astype(BF16)

    lengths = seq_lengths[:, 0, :]
    places = jnp.arange(group, dtype=jnp.int32)
    seq_start = jnp.zeros((batches, group), jnp.int32)
    start = jnp.zeros((batches,), jnp.int32)
    for k in range(lengths.shape[1]):
        seq_start = jnp.where(start[:, None] <= places[None, :], start[:, None], seq_start)
        start = start + lengths[:, k]
    offset = places[None, :] - seq_start
    after_one = (offset >= 1).astype(F32)[:, :, None]
    after_two = (offset >= 2).astype(F32)[:, :, None]

    tok_wide = tok_all.astype(F32)
    unit = tok_wide * lax.rsqrt(jnp.mean(tok_wide * tok_wide, axis=1, keepdims=True) + EPS)
    normed = (unit * gain_one).astype(BF16)
    projected = dot(normed, in_t, ((1,), (1,)))
    b_part = projected[:, :channels]
    c_part = projected[:, channels : 2 * channels]
    x_part = projected[:, 2 * channels :]
    c_high = c_part.astype(BF16)
    c_low = (c_part - c_high.astype(F32)).astype(BF16)
    product = (b_part * x_part).astype(BF16)
    moved = dot(deal_mat, jnp.concatenate([product, c_high, c_low], axis=1), ((1,), (0,)))
    moved = moved.reshape(batches, group, 3 * channels)
    product_nat = moved[:, :, :channels]
    c_nat = moved[:, :, channels : 2 * channels] + moved[:, :, 2 * channels :]
    zero_row = jnp.zeros((batches, 1, channels), F32)
    shift_one = jnp.concatenate([zero_row, product_nat[:, :-1]], axis=1)
    shift_two = jnp.concatenate([zero_row, zero_row, product_nat[:, :-2]], axis=1)
    prev_one = shift_one * after_one
    prev_two = shift_two * after_two
    conv_out = prev_two * taps[0] + prev_one * taps[1] + product_nat * taps[2]
    gated = (c_nat * conv_out).astype(BF16)

    def to_arrival(value):
        k = value.shape[-1]
        blocks = xor_blocks(value.reshape(batches, n, rows_dev, k), 1, n)
        blocks = blocks.reshape(batches, half, 2, rows_dev, k).transpose(2, 0, 1, 3, 4)
        return blocks.reshape(total, k)

    def from_arrival(value):
        k = value.shape[-1]
        blocks = value.reshape(2, batches, half, rows_dev, k).transpose(1, 2, 0, 3, 4)
        return xor_blocks(blocks.reshape(batches, n, rows_dev, k), 1, n).reshape(batches, group, k)

    def summed_rows(pairs):
        far = sum(dot(a[total // 2 :], b, ((1,), (0,))) for a, b in pairs).astype(BF16)
        near = sum(dot(a[: total // 2], b, ((1,), (0,))) for a, b in pairs)
        shape = (batches, half, rows_dev, width)
        return plane_reduce(near.reshape(shape), far.reshape(shape))

    gated_arr = to_arrival(gated)
    own_tok = turned(dot(own_mat, tok_all, ((1,), (0,))), n_dp, n_dp - z)
    own_tok = own_tok.reshape(batches, rows_dev, width)
    hidden = own_tok + summed_rows([(gated_arr, out_full)])
    inv_two = lax.rsqrt(jnp.mean(hidden * hidden, axis=2, keepdims=True) + EPS)
    unit_two = hidden * inv_two
    ff_own = turned((unit_two * gain_two).astype(BF16), n_dp, z)
    normed_ff = plane_gather([ff_own[m] for m in range(batches)]).reshape(total, width)

    gate_val = dot(normed_ff, gate_t, ((1,), (1,)))
    up_val = dot(normed_ff, up_t, ((1,), (1,)))
    sigmoid_val = jax.nn.sigmoid(gate_val)
    silu_val = gate_val * sigmoid_val
    ff_inner = (silu_val * up_val).astype(BF16)
    d_inner = dot(cot_all, down_t, ((1,), (1,)))
    silu_slope = sigmoid_val * (1.0 + gate_val * (1.0 - sigmoid_val))
    d_gate = (d_inner * up_val * silu_slope).astype(BF16)
    d_up = (d_inner * silu_val).astype(BF16)
    d_ff = turned(summed_rows([(d_gate, gate_t), (d_up, up_t)]), n_dp, n_dp - z)
    cot_wide = cotangent.astype(F32)
    scaled_ff = d_ff * gain_two
    d_hidden = cot_wide + inv_two * (
        scaled_ff - unit_two * jnp.mean(scaled_ff * unit_two, axis=2, keepdims=True)
    )
    branch_own = d_hidden.astype(BF16)
    branch = plane_gather([branch_own[m] for m in range(batches)]).reshape(total, width)
    block_val = turned(summed_rows([(ff_inner, down_t)]), n_dp, n_dp - z)
    block_out = (hidden + block_val).astype(BF16)

    d_gated = from_arrival(dot(branch, out_full, ((1,), (1,))))
    grad_c = (d_gated * conv_out).astype(BF16)
    grad_conv = d_gated * c_nat
    from_one = grad_conv * after_one * taps[1]
    from_two = grad_conv * after_two * taps[0]
    d_product = (
        grad_conv * taps[2]
        + jnp.concatenate([from_one[:, 1:], zero_row], axis=1)
        + jnp.concatenate([from_two[:, 2:], zero_row, zero_row], axis=1)
    ).astype(BF16)
    back = jnp.concatenate([d_product, grad_c], axis=2).reshape(total, 2 * channels)
    back = dot(deal_mat, back, ((0,), (0,)))
    d_prod_arr = back[:, :channels]
    grad_proj = jnp.concatenate(
        [d_prod_arr * x_part, back[:, channels:], d_prod_arr * b_part], axis=1
    ).astype(BF16)
    d_normed = turned(summed_rows([(grad_proj, in_t)]), n_dp, n_dp - z)
    own_wide = tokens_in.astype(F32)
    inv_one = lax.rsqrt(jnp.mean(own_wide * own_wide, axis=2, keepdims=True) + EPS)
    unit_own = own_wide * inv_one
    gain_nat = turned(in_full[3 * channels], n_dp, n_dp - z).astype(F32)
    scaled_one = d_normed * gain_nat
    d_hidden_own = dot(slot_mat, branch, ((1,), (0,))).reshape(batches, rows_dev, width)
    tokens_grad = (
        d_hidden_own
        + inv_one * (scaled_one - unit_own * jnp.mean(scaled_one * unit_own, axis=2, keepdims=True))
    ).astype(BF16)

    def summed_matrix(grad):
        step = width // n_dp
        return line_reduce([grad[:, d * step : (d + 1) * step] for d in range(n_dp)])

    down_sum = summed_matrix(dot(ff_inner, cot_all, ((0,), (0,))))
    gate_sum = summed_matrix(dot(d_gate, normed_ff, ((0,), (0,))))
    up_sum = summed_matrix(dot(d_up, normed_ff, ((0,), (0,))))
    in_sum = summed_matrix(dot(grad_proj, normed, ((0,), (0,))))
    out_term = dot(gated_arr, branch, ((0,), (0,)))
    conv_term = jnp.stack(
        [
            jnp.sum(grad_conv * tap_in, axis=(0, 1))
            for tap_in in (prev_two, prev_one, product_nat)
        ],
        axis=1,
    )
    out_term = jnp.concatenate(
        [out_term, conv_term, jnp.zeros((channels, LANES - conv_term.shape[1]), F32)], axis=1
    ).reshape(n_dp, own_rows, width + LANES)
    out_sum = line_reduce(
        [
            lax.dynamic_index_in_dim(out_term, (z + d) % n_dp, 0, keepdims=False)
            for d in range(n_dp)
        ]
    )
    out_grad = out_sum[:, :width]
    conv_grad = out_sum[:, width : width + conv_weight.shape[1]]
    down_grad = join_columns(collect(down_sum, order_a)).astype(F32)
    gate_grad = join_columns(collect(gate_sum, order_b)).astype(F32)
    up_grad = join_columns(collect(up_sum, order_a)).astype(F32)
    in_blocks = collect(in_sum, order_b).reshape(n, own_rows, 3 * n_dp, own_rows)
    in_grad = in_blocks.transpose(1, 2, 0, 3).reshape(own_rows, 3 * width).astype(F32)
    norm_gain_grad = jnp.sum(in_weight.astype(F32) * in_grad, axis=1) / norm_gain.astype(F32)
    ff_gain_grad = (
        jnp.sum(gate_weight.astype(F32) * gate_grad, axis=1)
        + jnp.sum(up_weight.astype(F32) * up_grad, axis=1)
    ) / ff_gain.astype(F32)
    return (
        block_out,
        tokens_grad,
        in_grad,
        conv_grad,
        out_grad,
        norm_gain_grad,
        ff_gain_grad,
        gate_grad,
        up_grad,
        down_grad,
    )


def solution(mesh):
    rows = P(("dp", "shard"), None)
    tokens = P(None, ("dp", "shard"), None)
    vector = P(("dp", "shard"))
    placed = (
        tokens,
        rows,
        rows,
        rows,
        vector,
        vector,
        rows,
        rows,
        rows,
        tokens,
        P(None, "dp", "shard", None),
        P(None, "dp", None),
    )
    return jax.shard_map(
        body,
        mesh=mesh,
        in_specs=placed,
        out_specs=(tokens, tokens, rows, rows, rows, vector, vector, rows, rows, rows),
        check_vma=False,
    )
```

time: 2340 us -> 958 us (0.41)
  waiting for transfers between devices: 1960 us -> 306 us
  starting transfers between devices: 15.3 us -> 247 us
  other arithmetic: 11.2 us -> 115 us
  local copies, waits for them, and re-layouts: 69.2 us -> 159 us
  blocking collectives: 85.5 us -> 0 us
  matrix products: 182 us -> 115 us
    reduce_scatter x4 -> x0, waiting for transfers between devices: 1130 us -> none  [the longest x1 387 us: body(): lax.psum_scatter(gate_term, ('dp', 'shard'), scatter_dimension=0, tiled=T...]
    all_gather x5 -> x0, waiting for transfers between devices: 434 us -> none  [the longest x1 131 us: body(): lax.all_gather(gate_weight, ('dp', 'shard'), axis=0, tiled=True)]
    unnamed x13 -> x0, waiting for transfers between devices: 389 us -> none
    ppermute x2 -> x175, waiting for transfers between devices: 0.01 us -> 306 us  [the longest x15 117 us: line_gather(): lax.ppermute(downs[k - 1], 'dp', [(i + 1, i) for i in range(n - k)])]
    ppermute x2 -> x175, starting transfers between devices: 4.75 us -> 247 us  [the longest x115 90.7 us: swap(): return lax.ppermute(value, 'shard', [(i, i ^ bit) for i in range(n)])]
    dot_general x15 -> x32, matrix products: 182 us -> 115 us  [dot(): lax.dot_general(former, latter, ((dims[0], dims[1]), ((), ())), preferred...]
    slice x4 -> x104, local copies, waits for them, and re-layouts: 2.96 us -> 67.9 us  [the longest x36 35.4 us: collect(): came = plane_deal([rows[r] for r in range(n)], order)]
    all_gather x1 -> x0, blocking collectives: 45.2 us -> none  [body(): lax.all_gather(conv_weight, ('dp', 'shard'), axis=0, tiled=True)]
  transfers between devices with their start and end apart: 15 -> 175, of which waited for: 10 -> 53; matrix products, arithmetic and copies ran while one was open for 8% -> 32% of each run, Pallas kernels for 0% -> 0%
where the time goes in v1:
time: 958 us; the launch traced here: 947 us
  waiting for transfers between devices  306 us (32%)
  starting transfers between devices  247 us (26%)
  local copies, waits for them, and re-layouts  159 us (17%)
  other arithmetic  115 us (12%)
  matrix products  115 us (12%)
    ppermute x15, waiting for transfers between devices, line_gather(): lax.ppermute(downs[k - 1], 'dp', [(i + 1, i) for i in range(n - k)])  117 us
    dot_general x32, matrix products, dot(): lax.dot_general(former, latter, ((dims[0], dims[1]), ((), ())), preferred...  115 us
    ppermute x115, waiting for transfers between devices, swap(): return lax.ppermute(value, 'shard', [(i, i ^ bit) for i in range(n)])  114 us
    ppermute x115, starting transfers between devices, swap(): return lax.ppermute(value, 'shard', [(i, i ^ bit) for i in range(n)])  90.7 us
    ppermute x15, starting transfers between devices, line_reduce(): lax.ppermute(going.astype(BF16), 'dp', [(i, i + 1) for i in range(n - d)])  51.8 us
    ppermute x15, starting transfers between devices, line_reduce(): lax.ppermute(going.astype(BF16), 'dp', [(i, i - 1) for i in range(d, n)])  50.9 us
    ppermute x15, waiting for transfers between devices, line_reduce(): lax.ppermute(going.astype(BF16), 'dp', [(i, i + 1) for i in range(n - d)])  45 us
    unnamed x492, local copies, waits for them, and re-layouts  41 us
  transfers between devices with their start and end apart: 175, of which 53 were waited for; matrix products, arithmetic and copies ran while one was open for 32% of the time, Pallas kernels for 0%

profile of v1, /device:TPU:0, one launch (start us, length us, event | category | flops | bytes accessed | tf_op | source)
XLA Modules:
  0.0 946.8 jit_solution(14345906032319426521)
XLA Ops:
  58.8 8.0 collective-permute-done.30
  73.7 6.7 collective-permute-done.18
  89.3 7.4 collective-permute-done.89
  111.4 5.8 collective-permute-done.94
  180.9 9.1 collective-permute-start.67
  191.3 11.3 %collective-permute-done.24 = bf16[592,384]{1,0:T(8,128)(2,1)S(1)} collective-permute-done((bf16[592,384]{1,0:T(8,128)(2,1)S(1)}, bf16[592,384]{1,0:T(8,128)(2,1)S(1)}, u32[]{:S(2)}, u32[]{:S(2)}) %collective-permute-start.24) | collective-permute-done | bytes 454688 | tf_op jit(solution)/shard_map/ppermute | solution.py:86
  204.3 10.4 %collective-permute-done.25 = bf16[592,384]{1,0:T(8,128)(2,1)S(1)} collective-permute-done((bf16[592,384]{1,0:T(8,128)(2,1)S(1)}, bf16[592,384]{1,0:T(8,128)(2,1)S(1)}, u32[]{:S(2)}, u32[]{:S(2)}) %collective-permute-start.25) | collective-permute-done | bytes 454688 | tf_op jit(solution)/shard_map/ppermute | solution.py:86
  263.2 7.5 collective-permute-done.76
  271.0 30.3 %collective-permute-done.75 = bf16[864,384]{1,0:T(8,128)(2,1)S(1)} collective-permute-done((bf16[864,384]{1,0:T(8,128)(2,1)S(1)}, bf16[864,384]{1,0:T(8,128)(2,1)S(1)}, u32[]{:S(2)}, u32[]{:S(2)}) %collective-permute-start.75) | collective-permute-done | bytes 663584 | tf_op jit(solution)/shard_map/ppermute | solution.py:86
  303.8 11.9 %collective-permute-done.61 = bf16[864,384]{1,0:T(8,128)(2,1)} collective-permute-done((bf16[864,384]{1,0:T(8,128)(2,1)}, bf16[864,384]{1,0:T(8,128)(2,1)}, u32[]{:S(2)}, u32[]{:S(2)}) %collective-permute-start.61) | collective-permute-done | bytes 663584 | tf_op jit(solution)/shard_map/ppermute | solution.py:86
  320.4 9.4 collective-permute-done.79
  333.0 9.6 %collective-permute-done.70 = bf16[864,384]{1,0:T(8,128)(2,1)} collective-permute-done((bf16[864,384]{1,0:T(8,128)(2,1)S(1)}, bf16[864,384]{1,0:T(8,128)(2,1)}, u32[]{:S(2)}, u32[]{:S(2)}) %collective-permute-start.70) | collective-permute-done | bytes 663584 | tf_op jit(solution)/shard_map/ppermute | solution.py:86
  351.5 25.9 %collective-permute-done.80 = bf16[864,384]{1,0:T(8,128)(2,1)S(1)} collective-permute-done((bf16[864,384]{1,0:T(8,128)(2,1)S(1)}, bf16[864,384]{1,0:T(8,128)(2,1)S(1)}, u32[]{:S(2)}, u32[]{:S(2)}) %collective-permute-start.80) | collective-permute-done | bytes 663584 | tf_op jit(solution)/shard_map/ppermute | solution.py:86
  379.8 6.0 fusion.258
  417.8 7.4 fusion.259
  425.2 10.2 %multiply_convert_fusion.2 = (bf16[1536,864]{0,1:T(8,128)(2,1)}, bf16[1536,864]{0,1:T(8,128)(2,1)S(1)}, bf16[1536,864]{0,1:T(8,128)(2,1)S(1)}) fusion(f32[1536,864]{0,1:T(8,128)} %fusion.258, f32[1536,864]{0,1:T(8,128)} %fusion.259, bf16[1536,1536]{1,0:T(8,128)(2,1)S(1)} %bitcast.1139, bf16[864,384]{1,0:T(8,128)(2,1)S(1)} %broadcast_select_fusion.4, ...), kind=kOutput, calls=%fused_computation.6 | convolution fusion | flops 4107386880 | bytes 25952256 | tf_op jit(solution)/shard_map/dot_general | solution.py:13
  439.7 6.5 fusion.25
  446.2 5.9 fusion.28
  465.3 5.9 collective-permute-start.166
  484.0 5.6 add_convert_fusion
  489.6 6.2 convolution_add_fusion
  502.6 11.2 %collective-permute-done.148 = bf16[864,384]{1,0:T(8,128)(2,1)} collective-permute-done((bf16[864,384]{1,0:T(8,128)(2,1)}, bf16[864,384]{1,0:T(8,128)(2,1)}, u32[]{:S(2)}, u32[]{:S(2)}) %collective-permute-start.148) | collective-permute-done | bytes 663584 | tf_op jit(solution)/shard_map/ppermute | solution.py:95
  522.4 11.1 %collective-permute-done.167 = bf16[864,384]{1,0:T(8,128)(2,1)S(1)} collective-permute-done((bf16[864,384]{1,0:T(8,128)(2,1)S(1)}, bf16[864,384]{1,0:T(8,128)(2,1)S(1)}, u32[]{:S(2)}, u32[]{:S(2)}) %collective-permute-start.167) | collective-permute-done | bytes 663584 | tf_op jit(solution)/shard_map/ppermute | solution.py:95
  540.3 7.4 collective-permute-done.158
  551.8 8.6 collective-permute-done.149
  570.6 6.1 collective-permute-done.105
  589.5 5.6 collective-permute-done.84
  601.9 31.0 %collective-permute-start.171 = (bf16[864,384]{1,0:T(8,128)(2,1)}, bf16[864,384]{1,0:T(8,128)(2,1)}, u32[]{:S(2)}, u32[]{:S(2)}) collective-permute-start(bf16[864,384]{1,0:T(8,128)(2,1)} %add_convert_fusion.1), channel_id=1, source_target_pairs={{8,0},{16,8},{24,16},{9,1},{17,9},{25,17},{10,2},{18,10},{26,18},{... | collective-permute-start | bytes 1990664 | tf_op jit(solution)/shard_map/ppermute | solution.py:97
  695.3 7.6 collective-permute-done.162
  707.4 6.5 collective-permute-done.153
  834.0 6.8 collective-permute-start.144
  893.6 5.9 collective-permute-done.138
  (1232 shorter events, 626.4 us)
Async XLA Ops:
  3.3 78.9 %collective-permute-start.3 = (bf16[96,1536]{1,0:T(8,128)(2,1)}, bf16[96,1536]{1,0:T(8,128)(2,1)}, u32[]{:S(2)}, u32[]{:S(2)}) collective-permute-start(bf16[96,1536]{1,0:T(8,128)(2,1)} %get-tuple-element.389), channel_id=1, source_target_pairs={{0,2},{1,3},{2,0},{3,1},{4,6},{5,7},{6,4},{7,5},{8,10},{9,11},{10,... | collective-permute-start | bytes 884744 | tf_op jit(solution)/shard_map/ppermute | solution.py:24
  6.3 81.5 %collective-permute-start.4 = (bf16[96,1536]{1,0:T(8,128)(2,1)}, bf16[96,1536]{1,0:T(8,128)(2,1)}, u32[]{:S(2)}, u32[]{:S(2)}) collective-permute-start(bf16[96,1536]{1,0:T(8,128)(2,1)} %get-tuple-element.389), channel_id=1, source_target_pairs={{0,4},{1,5},{2,6},{3,7},{4,0},{5,1},{6,2},{7,3},{8,12},{9,13},{10,... | collective-permute-start | bytes 884744 | tf_op jit(solution)/shard_map/ppermute | solution.py:24
  8.0 46.7 %collective-permute-start.27 = (bf16[48,1664]{1,0:T(8,128)(2,1)S(1)}, bf16[48,1664]{1,0:T(8,128)(2,1)}, u32[]{:S(2)}, u32[]{:S(2)}) collective-permute-start(bf16[48,1664]{1,0:T(8,128)(2,1)S(1)} %concatenate.441), channel_id=1, source_target_pairs={{0,8},{8,16},{16,24},{1,9},{9,17},{17,25},{2,10},{10,18},{18,26},{... | collective-permute-start | bytes 479240 | tf_op jit(solution)/shard_map/ppermute | solution.py:85
  12.1 43.1 %collective-permute-start.26 = (bf16[48,1664]{1,0:T(8,128)(2,1)S(1)}, bf16[48,1664]{1,0:T(8,128)(2,1)}, u32[]{:S(2)}, u32[]{:S(2)}) collective-permute-start(bf16[48,1664]{1,0:T(8,128)(2,1)S(1)} %concatenate.441), channel_id=1, source_target_pairs={{8,0},{16,8},{24,16},{9,1},{17,9},{25,17},{10,2},{18,10},{26,18},{... | collective-permute-start | bytes 479240 | tf_op jit(solution)/shard_map/ppermute | solution.py:86
  99.9 39.9 %collective-permute-start.9 = (bf16[96,1536]{1,0:T(8,128)(2,1)}, bf16[96,1536]{1,0:T(8,128)(2,1)S(1)}, u32[]{:S(2)}, u32[]{:S(2)}) collective-permute-start(bf16[96,1536]{1,0:T(8,128)(2,1)} %get-tuple-element.389), channel_id=1, source_target_pairs={{0,1},{1,0},{2,3},{3,2},{4,5},{5,4},{6,7},{7,6},{8,9},{9,8},{10,11... | collective-permute-start | bytes 884744 | tf_op jit(solution)/shard_map/ppermute | solution.py:24
  100.2 41.5 %collective-permute-start.13 = (bf16[96,1536]{1,0:T(8,128)(2,1)S(1)}, bf16[96,1536]{1,0:T(8,128)(2,1)S(1)}, u32[]{:S(2)}, u32[]{:S(2)}) collective-permute-start(bf16[96,1536]{1,0:T(8,128)(2,1)S(1)} %copy-done.130), channel_id=1, source_target_pairs={{0,1},{1,0},{2,3},{3,2},{4,5},{5,4},{6,7},{7,6},{8,9},{9,8},{10,11... | collective-permute-start | bytes 884744 | tf_op jit(solution)/shard_map/ppermute | solution.py:24
  169.9 87.6 %collective-permute-start.58 = (bf16[864,384]{1,0:T(8,128)(2,1)}, bf16[864,384]{1,0:T(8,128)(2,1)}, u32[]{:S(2)}, u32[]{:S(2)}) collective-permute-start(bf16[864,384]{1,0:T(8,128)(2,1)} %convolution_convert_fusion.8), channel_id=1, source_target_pairs={{0,8},{8,16},{16,24},{1,9},{9,17},{17,25},{2,10},{10,18},{18,26},{... | collective-permute-start | bytes 1990664 | tf_op jit(solution)/shard_map/ppermute | solution.py:85
  175.3 83.5 %collective-permute-start.57 = (bf16[864,384]{1,0:T(8,128)(2,1)}, bf16[864,384]{1,0:T(8,128)(2,1)}, u32[]{:S(2)}, u32[]{:S(2)}) collective-permute-start(bf16[864,384]{1,0:T(8,128)(2,1)} %convolution_convert_fusion.8), channel_id=1, source_target_pairs={{8,0},{16,8},{24,16},{9,1},{17,9},{25,17},{10,2},{18,10},{26,18},{... | collective-permute-start | bytes 1990664 | tf_op jit(solution)/shard_map/ppermute | solution.py:86
  180.9 79.2 %collective-permute-start.67 = (bf16[864,384]{1,0:T(8,128)(2,1)}, bf16[864,384]{1,0:T(8,128)(2,1)}, u32[]{:S(2)}, u32[]{:S(2)}) collective-permute-start(bf16[864,384]{1,0:T(8,128)(2,1)} %convolution_convert_fusion.7), channel_id=1, source_target_pairs={{0,8},{8,16},{16,24},{1,9},{9,17},{17,25},{2,10},{10,18},{18,26},{... | collective-permute-start | bytes 1990664 | tf_op jit(solution)/shard_map/ppermute | solution.py:85
  257.5 59.3 %collective-permute-start.66 = (bf16[864,384]{1,0:T(8,128)(2,1)}, bf16[864,384]{1,0:T(8,128)(2,1)S(1)}, u32[]{:S(2)}, u32[]{:S(2)}) collective-permute-start(bf16[864,384]{1,0:T(8,128)(2,1)} %convolution_convert_fusion.7), channel_id=1, source_target_pairs={{8,0},{16,8},{24,16},{9,1},{17,9},{25,17},{10,2},{18,10},{26,18},{... | collective-permute-start | bytes 1990664 | tf_op jit(solution)/shard_map/ppermute | solution.py:86
  258.8 42.5 %collective-permute-start.75 = (bf16[864,384]{1,0:T(8,128)(2,1)S(1)}, bf16[864,384]{1,0:T(8,128)(2,1)S(1)}, u32[]{:S(2)}, u32[]{:S(2)}) collective-permute-start(bf16[864,384]{1,0:T(8,128)(2,1)S(1)} %convolution_convert_fusion.6), channel_id=1, source_target_pairs={{8,0},{16,8},{24,16},{9,1},{17,9},{25,17},{10,2},{18,10},{26,18},{... | collective-permute-start | bytes 1990664 | tf_op jit(solution)/shard_map/ppermute | solution.py:86
  260.1 41.9 %collective-permute-start.59 = (bf16[864,384]{1,0:T(8,128)(2,1)}, bf16[864,384]{1,0:T(8,128)(2,1)}, u32[]{:S(2)}, u32[]{:S(2)}) collective-permute-start(bf16[864,384]{1,0:T(8,128)(2,1)} %collective-permute-done.58), channel_id=1, source_target_pairs={{8,16},{16,24},{9,17},{17,25},{10,18},{18,26},{11,19},{19,27},{12,... | collective-permute-start | bytes 1990664 | tf_op jit(solution)/shard_map/ppermute | solution.py:85
  261.7 53.9 %collective-permute-start.61 = (bf16[864,384]{1,0:T(8,128)(2,1)}, bf16[864,384]{1,0:T(8,128)(2,1)}, u32[]{:S(2)}, u32[]{:S(2)}) collective-permute-start(bf16[864,384]{1,0:T(8,128)(2,1)} %collective-permute-done.57), channel_id=1, source_target_pairs={{8,0},{16,8},{9,1},{17,9},{10,2},{18,10},{11,3},{19,11},{12,4},{20... | collective-permute-start | bytes 1990664 | tf_op jit(solution)/shard_map/ppermute | solution.py:86
  270.6 47.7 %collective-permute-start.34 = (bf16[96,1536]{1,0:T(8,128)(2,1)S(1)}, bf16[96,1536]{1,0:T(8,128)(2,1)S(1)}, u32[]{:S(2)}, u32[]{:S(2)}) collective-permute-start(bf16[96,1536]{1,0:T(8,128)(2,1)S(1)} %get-tuple-element.138), channel_id=1, source_target_pairs={{0,4},{1,5},{2,6},{3,7},{4,0},{5,1},{6,2},{7,3},{8,12},{9,13},{10,... | collective-permute-start | bytes 884744 | tf_op jit(solution)/shard_map/ppermute | solution.py:24
  331.4 61.3 %collective-permute-start.60 = (bf16[864,384]{1,0:T(8,128)(2,1)}, bf16[864,384]{1,0:T(8,128)(2,1)}, u32[]{:S(2)}, u32[]{:S(2)}) collective-permute-start(bf16[864,384]{1,0:T(8,128)(2,1)} %collective-permute-done.59), channel_id=1, source_target_pairs={{16,24},{17,25},{18,26},{19,27},{20,28},{21,29},{22,30},{23,31}} | collective-permute-start | bytes 1990664 | tf_op jit(solution)/shard_map/ppermute | solution.py:85
  345.4 50.1 %collective-permute-start.62 = (bf16[864,384]{1,0:T(8,128)(2,1)}, bf16[864,384]{1,0:T(8,128)(2,1)}, u32[]{:S(2)}, u32[]{:S(2)}) collective-permute-start(bf16[864,384]{1,0:T(8,128)(2,1)} %collective-permute-done.61), channel_id=1, source_target_pairs={{8,0},{9,1},{10,2},{11,3},{12,4},{13,5},{14,6},{15,7}} | collective-permute-start | bytes 1990664 | tf_op jit(solution)/shard_map/ppermute | solution.py:86
  346.8 54.1 %collective-permute-start.69 = (bf16[864,384]{1,0:T(8,128)(2,1)}, bf16[864,384]{1,0:T(8,128)(2,1)}, u32[]{:S(2)}, u32[]{:S(2)}) collective-permute-start(bf16[864,384]{1,0:T(8,128)(2,1)} %collective-permute-done.68), channel_id=1, source_target_pairs={{16,24},{17,25},{18,26},{19,27},{20,28},{21,29},{22,30},{23,31}} | collective-permute-start | bytes 1990664 | tf_op jit(solution)/shard_map/ppermute | solution.py:85
  471.2 49.1 %collective-permute-start.169 = (bf16[864,384]{1,0:T(8,128)(2,1)}, bf16[864,384]{1,0:T(8,128)(2,1)}, u32[]{:S(2)}, u32[]{:S(2)}) collective-permute-start(bf16[864,384]{1,0:T(8,128)(2,1)} %get-tuple-element.144), channel_id=1, source_target_pairs={{24,16},{25,17},{26,18},{27,19},{28,20},{29,21},{30,22},{31,23}} | collective-permute-start | bytes 1990664 | tf_op jit(solution)/shard_map/ppermute | solution.py:97
  500.1 40.2 %collective-permute-start.160 = (bf16[864,384]{1,0:T(8,128)(2,1)S(1)}, bf16[864,384]{1,0:T(8,128)(2,1)S(1)}, u32[]{:S(2)}, u32[]{:S(2)}) collective-permute-start(bf16[864,384]{1,0:T(8,128)(2,1)S(1)} %copy-done.83), channel_id=1, source_target_pairs={{24,16},{25,17},{26,18},{27,19},{28,20},{29,21},{30,22},{31,23}} | collective-permute-start | bytes 1990664 | tf_op jit(solution)/shard_map/ppermute | solution.py:97
  520.4 42.7 %collective-permute-start.103 = (bf16[4,96,1536]{2,1,0:T(8,128)(2,1)S(1)}, bf16[4,96,1536]{2,1,0:T(8,128)(2,1)S(1)}, u32[]{:S(2)}, u32[]{:S(2)}) collective-permute-start(bf16[4,96,1536]{2,1,0:T(8,128)(2,1)S(1)} %bitcast.1166), channel_id=1, source_target_pairs={{0,1},{1,0},{2,3},{3,2},{4,5},{5,4},{6,7},{7,6},{8,9},{9,8},{10,11... | collective-permute-start | bytes 3538952 | tf_op jit(solution)/shard_map/ppermute | solution.py:24
  540.3 47.8 %collective-permute-start.85 = (bf16[4,96,1536]{2,1,0:T(8,128)(2,1)S(1)}, bf16[4,96,1536]{2,1,0:T(8,128)(2,1)S(1)}, u32[]{:S(2)}, u32[]{:S(2)}) collective-permute-start(bf16[4,96,1536]{2,1,0:T(8,128)(2,1)S(1)} %bitcast.1164), channel_id=1, source_target_pairs={{0,1},{1,0},{2,3},{3,2},{4,5},{5,4},{6,7},{7,6},{8,9},{9,8},{10,11... | collective-permute-start | bytes 3538952 | tf_op jit(solution)/shard_map/ppermute | solution.py:24
  581.8 102.4 %collective-permute-start.168 = (bf16[864,384]{1,0:T(8,128)(2,1)}, bf16[864,384]{1,0:T(8,128)(2,1)}, u32[]{:S(2)}, u32[]{:S(2)}) collective-permute-start(bf16[864,384]{1,0:T(8,128)(2,1)} %get-tuple-element.141), channel_id=1, source_target_pairs={{0,8},{8,16},{16,24},{1,9},{9,17},{17,25},{2,10},{10,18},{18,26},{... | collective-permute-start | bytes 1990664 | tf_op jit(solution)/shard_map/ppermute | solution.py:95
  600.3 40.7 %collective-permute-start.86 = (bf16[96,1536]{1,0:T(8,128)(2,1)}, bf16[96,1536]{1,0:T(8,128)(2,1)}, u32[]{:S(2)}, u32[]{:S(2)}) collective-permute-start(bf16[96,1536]{1,0:T(8,128)(2,1)} %get-tuple-element.160), channel_id=1, source_target_pairs={{0,2},{1,3},{2,0},{3,1},{4,6},{5,7},{6,4},{7,5},{8,10},{9,11},{10,... | collective-permute-start | bytes 884744 | tf_op jit(solution)/shard_map/ppermute | solution.py:24
  601.9 83.8 %collective-permute-start.171 = (bf16[864,384]{1,0:T(8,128)(2,1)}, bf16[864,384]{1,0:T(8,128)(2,1)}, u32[]{:S(2)}, u32[]{:S(2)}) collective-permute-start(bf16[864,384]{1,0:T(8,128)(2,1)} %add_convert_fusion.1), channel_id=1, source_target_pairs={{8,0},{16,8},{24,16},{9,1},{17,9},{25,17},{10,2},{18,10},{26,18},{... | collective-permute-start | bytes 1990664 | tf_op jit(solution)/shard_map/ppermute | solution.py:97
  685.7 50.6 %collective-permute-start.117 = (bf16[96,1536]{1,0:T(8,128)(2,1)}, bf16[96,1536]{1,0:T(8,128)(2,1)}, u32[]{:S(2)}, u32[]{:S(2)}) collective-permute-start(bf16[96,1536]{1,0:T(8,128)(2,1)} %get-tuple-element.365), channel_id=1, source_target_pairs={{0,1},{1,0},{2,3},{3,2},{4,5},{5,4},{6,7},{7,6},{8,9},{9,8},{10,11... | collective-permute-start | bytes 884744 | tf_op jit(solution)/shard_map/ppermute | solution.py:24
  694.8 54.9 %collective-permute-start.121 = (bf16[96,1536]{1,0:T(8,128)(2,1)}, bf16[96,1536]{1,0:T(8,128)(2,1)}, u32[]{:S(2)}, u32[]{:S(2)}) collective-permute-start(bf16[96,1536]{1,0:T(8,128)(2,1)} %copy-done.132), channel_id=1, source_target_pairs={{0,1},{1,0},{2,3},{3,2},{4,5},{5,4},{6,7},{7,6},{8,9},{9,8},{10,11... | collective-permute-start | bytes 884744 | tf_op jit(solution)/shard_map/ppermute | solution.py:24
  748.2 56.6 %collective-permute-start.172 = (bf16[4,48,864]{2,1,0:T(8,128)(2,1)}, bf16[4,48,864]{2,1,0:T(8,128)(2,1)}, u32[]{:S(2)}, u32[]{:S(2)}) collective-permute-start(bf16[4,48,864]{2,1,0:T(8,128)(2,1)} %pad_maximum_fusion.38), channel_id=1, source_target_pairs={{0,1},{1,0},{2,3},{3,2},{4,5},{5,4},{6,7},{7,6},{8,9},{9,8},{10,11... | collective-permute-start | bytes 995336 | tf_op jit(solution)/shard_map/ppermute | solution.py:24
  749.7 57.6 %collective-permute-start.163 = (bf16[4,48,864]{2,1,0:T(8,128)(2,1)}, bf16[4,48,864]{2,1,0:T(8,128)(2,1)}, u32[]{:S(2)}, u32[]{:S(2)}) collective-permute-start(bf16[4,48,864]{2,1,0:T(8,128)(2,1)} %pad_maximum_fusion.35), channel_id=1, source_target_pairs={{0,1},{1,0},{2,3},{3,2},{4,5},{5,4},{6,7},{7,6},{8,9},{9,8},{10,11... | collective-permute-start | bytes 995336 | tf_op jit(solution)/shard_map/ppermute | solution.py:24
  750.2 60.3 %collective-permute-start.154 = (bf16[4,48,864]{2,1,0:T(8,128)(2,1)}, bf16[4,48,864]{2,1,0:T(8,128)(2,1)}, u32[]{:S(2)}, u32[]{:S(2)}) collective-permute-start(bf16[4,48,864]{2,1,0:T(8,128)(2,1)} %pad_maximum_fusion.32), channel_id=1, source_target_pairs={{0,1},{1,0},{2,3},{3,2},{4,5},{5,4},{6,7},{7,6},{8,9},{9,8},{10,11... | collective-permute-start | bytes 995336 | tf_op jit(solution)/shard_map/ppermute | solution.py:24
  807.3 65.2 %collective-permute-start.136 = (bf16[576,384]{1,0:T(8,128)(2,1)}, bf16[576,384]{1,0:T(8,128)(2,1)}, u32[]{:S(2)}, u32[]{:S(2)}) collective-permute-start(bf16[576,384]{1,0:T(8,128)(2,1)} %get-tuple-element.166), channel_id=1, source_target_pairs={{24,16},{25,17},{26,18},{27,19},{28,20},{29,21},{30,22},{31,23}} | collective-permute-start | bytes 1327112 | tf_op jit(solution)/shard_map/ppermute | solution.py:97
  810.5 65.7 %collective-permute-start.125 = (bf16[4,96,1536]{2,1,0:T(8,128)(2,1)}, bf16[4,96,1536]{2,1,0:T(8,128)(2,1)}, u32[]{:S(2)}, u32[]{:S(2)}) collective-permute-start(bf16[4,96,1536]{2,1,0:T(8,128)(2,1)} %bitcast.282), channel_id=1, source_target_pairs={{0,1},{1,0},{2,3},{3,2},{4,5},{5,4},{6,7},{7,6},{8,9},{9,8},{10,11... | collective-permute-start | bytes 3538952 | tf_op jit(solution)/shard_map/ppermute | solution.py:24
  833.2 68.6 %collective-permute-start.129 = (bf16[4,96,1536]{2,1,0:T(8,128)(2,1)}, bf16[4,96,1536]{2,1,0:T(8,128)(2,1)}, u32[]{:S(2)}, u32[]{:S(2)}) collective-permute-start(bf16[4,96,1536]{2,1,0:T(8,128)(2,1)} %bitcast.292), channel_id=1, source_target_pairs={{0,1},{1,0},{2,3},{3,2},{4,5},{5,4},{6,7},{7,6},{8,9},{9,8},{10,11... | collective-permute-start | bytes 3538952 | tf_op jit(solution)/shard_map/ppermute | solution.py:24
  (365 other events, 4008.7 us)

commit v2 on v0

v2 whole, which is shorter than its diff:
```python
import functools

import jax
import jax.numpy as jnp
from jax import lax
from jax.experimental import pallas as pl
from jax.experimental.pallas import tpu as pltpu
from jax.sharding import PartitionSpec as P

EPS = 1e-05
F32 = jnp.float32
BF16 = jnp.bfloat16
LANES = 128


def dot(former, latter, dims, out=F32):
    return lax.dot_general(
        former, latter, ((dims[0], dims[1]), ((), ())), preferred_element_type=F32
    ).astype(out)


def bits_of(count):
    return [1 << k for k in range(count.bit_length() - 1)]


def swap(value, bit, axis="shard"):
    n = lax.axis_size(axis)
    return lax.ppermute(value, axis, [(i, i ^ bit) for i in range(n)])


def route(outer, turn):
    turn = turn % len(outer)
    return outer[turn:] + outer[:turn]


def after(value, *others):
    others = [other for other in others if other is not None]
    if not others:
        return value
    return lax.optimization_barrier((value, *others))[0]


def gather_names(n, parts):
    outer = bits_of(n)[1:]
    names = []
    for m in range(parts):
        order = [0]
        for bit in route(outer, m):
            order = order + [e ^ (bit >> 1) for e in order]
        names.append(order)
    return names


def plane_gather(parts, waits=((), ())):
    n = lax.axis_size("shard")
    outer = bits_of(n)[1:]
    held = [[part] for part in parts]
    steps = []
    for k in range(len(outer)):
        going = [h[0] if len(h) == 1 else jnp.concatenate(h, axis=0) for h in held]
        if k < len(waits):
            going = [after(g, *waits[k]) for g in going]
        came = [swap(going[m], route(outer, m)[k]) for m in range(len(parts))]
        held = [[g, c] for g, c in zip(going, came)]
        steps.append(tuple(came))
    near = [piece for h in held for piece in h]
    far = [swap(piece, 1) for piece in near]
    return near + far, steps


def fold_kernel(rows, plans, *refs):
    count = len(plans)
    kept, came, sends, keeps = (refs[k * count : (k + 1) * count] for k in range(4))
    for m, (going, staying) in enumerate(plans):
        for out, places in ((sends[m], going), (keeps[m], staying)):
            for k, place in enumerate(places):
                at = slice(place * rows, (place + 1) * rows)
                value = kept[m][at, :] + came[m][at, :].astype(F32)
                out[k * rows : (k + 1) * rows, :] = value.astype(out.dtype)


def first_fold_kernel(rows, plans, near, came, *refs):
    count = len(plans)
    sends, keeps = refs[:count], refs[count:]
    for m, (going, staying) in enumerate(plans):
        for out, places in ((sends[m], going), (keeps[m], staying)):
            for k, place in enumerate(places):
                at = slice(place * rows, (place + 1) * rows)
                value = near[at, :] + came[at, :].astype(F32)
                out[k * rows : (k + 1) * rows, :] = value.astype(out.dtype)


def plane_reduce(near, far, parts, wait=()):
    n = lax.axis_size("shard")
    half = n // 2
    outer = bits_of(n)[1:]
    width = near.shape[1]
    rows = near.shape[0] // (parts * half)
    came = swap(far, 1)
    names = gather_names(n, parts)
    kept, arrived = near, came
    for k in reversed(range(len(outer))):
        plans = []
        for m in range(parts):
            bit = route(outer, m)[k] >> 1
            going = [e for e in names[m] if e & bit]
            base = m * half if kept is near else 0
            plans.append(([base + names[m].index(e) for e in going], [base + names[m].index(e ^ bit) for e in going]))
            names[m] = [e ^ bit for e in going]
        shape = (len(plans[0][0]) * rows, width)
        outs = [(shape, BF16)] * parts + [(shape, F32)] * parts
        if kept is near:
            made = run(functools.partial(first_fold_kernel, rows, plans), outs, [], [near, came])
            sends = [after(send, *wait) for send in made[:parts]]
        else:
            made = run(functools.partial(fold_kernel, rows, plans), outs, [], [*kept, *arrived])
            sends = made[:parts]
        kept = made[parts:]
        arrived = [swap(sends[m], route(outer, m)[k]) for m in range(parts)]
    return [*kept, *arrived]


def line_gather(block, wait=None):
    n = lax.axis_size("dp")
    block = after(block, *(wait or ()))
    ready = None
    for bit in reversed(bits_of(n)):
        came = swap(block, bit, "dp")
        ready = (came,) if ready is None else ready
        if bit == 1:
            return block, came, ready
        block = jnp.concatenate([block, came], axis=1)


def line_reduce(keep, send, wait=None):
    n = lax.axis_size("dp")
    ready = None
    send = after(send, *(wait or ()))
    for bit in bits_of(n):
        came = swap(send, bit, "dp")
        ready = (came,) if ready is None else ready
        if 2 * bit == n:
            return keep, came, ready
        total = keep + came.astype(F32)
        cut = total.shape[1] // 2
        keep, send = total[:, :cut], total[:, cut:].astype(BF16)


def reversed_bits(index, n):
    out = 0
    for k, bit in enumerate(bits_of(n)):
        if index & bit:
            out |= n >> (k + 1)
    return out


def turned(value, z, n):
    step = value.shape[-1] // n
    pieces = [value[..., k * step : (k + 1) * step] for k in range(n)]
    out = None
    for k in range(n):
        order = [pieces[k ^ reversed_bits(p, n)] for p in range(n)]
        moved = jnp.concatenate(order, axis=-1)
        out = moved if out is None else jnp.where(z == k, moved, out)
    return out


def exchange(value, z, n, back):
    step = value.shape[1] // n
    pieces = [value[:, p * step : (p + 1) * step] for p in range(n)]

    def reorder(pieces):
        return [pieces[reversed_bits(p, n)] for p in range(n)]

    def flip(pieces):
        for k, bit in enumerate(bits_of(n)):
            low = n >> (k + 1)
            pieces = [jnp.where((z & bit) != 0, pieces[p ^ low], pieces[p]) for p in range(n)]
        return pieces

    return jnp.concatenate(reorder(flip(pieces)) if back else flip(reorder(pieces)), axis=1)


WHOLE = pl.BlockSpec(memory_space=pltpu.VMEM)
SCALAR = pl.BlockSpec(memory_space=pltpu.SMEM)


def run(kernel, outs, scalars, arrays, scratch=()):
    return pl.pallas_call(
        kernel,
        out_shape=[jax.ShapeDtypeStruct(shape, dtype) for shape, dtype in outs],
        in_specs=[SCALAR] * len(scalars) + [WHOLE] * len(arrays),
        out_specs=[WHOLE] * len(outs),
        scratch_shapes=list(scratch),
        compiler_params=pltpu.CompilerParams(vmem_limit_bytes=48 * 2**20),
        cost_estimate=pl.CostEstimate(flops=1000, bytes_accessed=1000, transcendentals=0),
    )(*[jnp.asarray(v, jnp.int32).reshape(1) for v in scalars], *arrays)


def mm(former, latter):
    return lax.dot_general(former, latter, (((1,), (0,)), ((), ())), preferred_element_type=F32)


def mt(former, latter):
    return lax.dot_general(former, latter, (((1,), (1,)), ((), ())), preferred_element_type=F32)


def spread_kernel(n, whole, rest, count, *refs):
    weights, out = refs[:count], refs[count]
    rows = weights[0].shape[0]
    for k in range(count):
        for s in range(n):
            at = slice(k * rows, (k + 1) * rows)
            first = n * whole + s * rest
            out[s, at, :whole] = weights[k][:, s * whole : (s + 1) * whole]
            out[s, at, whole:] = weights[k][:, first : first + rest]


def join_kernel(n, whole, rest, came, weight, grad, dots):
    grad[:, n * whole :] = jnp.concatenate([came[s, :, whole:] for s in range(n)], axis=1).astype(F32)
    for s in range(n):
        grad[:, s * whole : (s + 1) * whole] = came[s, :, :whole].astype(F32)
    dots[...] = jnp.sum(grad[...] * weight[...].astype(F32), axis=1, keepdims=True)


def join_in_kernel(n, groups, came, weight, grad, dots):
    rows = came.shape[1]
    for g in range(groups):
        piece = jnp.concatenate([came[s, :, g * rows : (g + 1) * rows] for s in range(n)], axis=1)
        grad[:, g * n * rows : (g + 1) * n * rows] = piece.astype(F32)
    dots[...] = jnp.sum(grad[...] * weight[...].astype(F32), axis=1, keepdims=True)


def by_line(pieces, z, n):
    for k, bit in enumerate(bits_of(n)):
        low = n >> (k + 1)
        pieces = [jnp.where((z & bit) != 0, pieces[p ^ low], pieces[p]) for p in range(n)]
    return [pieces[reversed_bits(p, n)] for p in range(n)]


def out_kernel(n, z, first, second, left, right, tap_cols):
    rows = first.shape[0] // (n // 2)
    cut = left.shape[1]
    pieces = [(first, second)[p // (n // 2)][p % (n // 2) * rows : (p % (n // 2) + 1) * rows, :] for p in range(n)]
    for p, piece in enumerate(by_line(pieces, z[0], n)):
        at = slice(p * rows, (p + 1) * rows)
        left[at, :] = piece[:, :cut]
        right[at, :] = piece[:, cut : 2 * cut]
        tap_cols[at, :] = piece[:, 2 * cut :]


def relative_kernel(n, z, term, conv_term, keep, send):
    rows = term.shape[0] // n
    width = term.shape[1]
    for value, lanes in ((term, slice(0, width)), (conv_term, slice(width, None))):
        pieces = [value[reversed_bits(p, n) * rows : (reversed_bits(p, n) + 1) * rows, :] for p in range(n)]
        for k, bit in enumerate(bits_of(n)):
            low = n >> (k + 1)
            pieces = [jnp.where((z[0] & bit) != 0, pieces[p ^ low], pieces[p]) for p in range(n)]
        for p in range(n):
            out = (keep, send)[p // (n // 2)]
            at = slice(p % (n // 2) * rows, (p % (n // 2) + 1) * rows)
            out[at, lanes] = pieces[p].astype(out.dtype)


def side_kernel(count, *refs):
    pieces, (left, right) = refs[:count], refs[count:]
    rows = pieces[0].shape[0]
    cut = left.shape[1]
    for k in range(count):
        left[k * rows : (k + 1) * rows, :] = pieces[k][:, :cut]
        right[k * rows : (k + 1) * rows, :] = pieces[k][:, cut:]


def project_kernel(channels, count, *refs):
    pieces = refs[:count]
    in_a, in_b, own_ref, normed_a, normed_b, product, c_high, c_low, b_out, x_out, own_tok = refs[count : count + 11]
    tok = refs[count + 11]
    rows = pieces[0].shape[0]
    split = in_a.shape[1]
    at_gain = 3 * channels
    gain = jnp.concatenate([in_a[at_gain : at_gain + 1, :], in_b[at_gain : at_gain + 1, :]], axis=1).astype(F32)
    for k in range(0, count, 2):
        at = slice(k * rows, (k + 2) * rows)
        for j in range(2):
            piece = pieces[k + j][...]
            here = slice((k + j) * rows, (k + j + 1) * rows)
            tok[here, :] = piece
            wide = piece.astype(F32)
            unit = wide * lax.rsqrt(jnp.mean(wide * wide, axis=1, keepdims=True) + EPS)
            lean = (unit * gain).astype(BF16)
            normed_a[here, :] = lean[:, :split]
            normed_b[here, :] = lean[:, split:]
        left, right = normed_a[at, :], normed_b[at, :]

        def part(j):
            lines = slice(j * channels, (j + 1) * channels)
            return mt(left, in_a[lines, :]) + mt(right, in_b[lines, :])

        b_part, c_part, x_part = part(0), part(1), part(2)
        high = c_part.astype(BF16)
        product[at, :] = (b_part * x_part).astype(BF16)
        c_high[at, :] = high
        c_low[at, :] = (c_part - high.astype(F32)).astype(BF16)
        b_out[at, :] = b_part
        x_out[at, :] = x_part
    lanes = lax.broadcasted_iota(jnp.int32, (own_ref.shape[0], tok.shape[0]), 1)
    own_tok[...] = mm((own_ref[...] == lanes).astype(F32).astype(BF16), tok[...]).astype(BF16)


def conv_kernel(batches, n, me, product, c_high, c_low, source, offset, taps, p_out, c_out, conv_out, gated_out, gated):
    names = gather_names(n, batches)
    group = source.shape[1]
    half = group // 2
    rows = group // n
    for m in range(batches):
        lanes = lax.broadcasted_iota(jnp.int32, (group, group), 1)
        deal = (source[m] == lanes).astype(F32).astype(BF16)
        first, second = pl.ds(m * half, half), pl.ds((batches + m) * half, half)

        def moved(ref):
            return mm(deal[:, :half], ref[first, :]) + mm(deal[:, half:], ref[second, :])

        wide = moved(product)
        c_part = moved(c_high) + moved(c_low)
        place = offset[m]
        prev_one = jnp.where(place >= 1, pltpu.roll(wide, 1, 0), 0.0)
        prev_two = jnp.where(place >= 2, pltpu.roll(wide, 2, 0), 0.0)
        conv = prev_two * taps[0:1, :] + prev_one * taps[1:2, :] + wide * taps[2:3, :]
        p_out[m] = wide.astype(BF16)
        c_out[m] = c_part
        conv_out[m] = conv
        gated[...] = c_part * conv
        for c in range(2):
            for k, e in enumerate(names[m]):
                other = me[0] ^ (2 * e + c)
                block = gated[pl.ds(pl.multiple_of(other * rows, 8), rows), :]
                at = ((c * batches + m) * (n // 2) + k) * rows
                gated_out[at : at + rows, :] = block.astype(BF16)


def summed(batches, terms):
    return jnp.concatenate([terms[m][...] + terms[batches + m][...].astype(F32) for m in range(batches)], axis=0)


def hidden_kernel(batches, n_dp, z, own_tok, gain, *refs):
    terms, (hidden, unit_out, *parts) = refs[: 2 * batches], refs[2 * batches :]
    value = exchange(own_tok[...].astype(F32), z[0], n_dp, True) + summed(batches, terms)
    hidden[...] = value
    unit = value * lax.rsqrt(jnp.mean(value * value, axis=1, keepdims=True) + EPS)
    unit_out[...] = unit
    lean = exchange(unit * gain[...], z[0], n_dp, False).astype(BF16)
    rows = parts[0].shape[0]
    for m in range(batches):
        parts[m][...] = lean[m * rows : (m + 1) * rows]


def gate_kernel(count, *refs):
    pieces = refs[:count]
    gate_a, gate_b, up_a, up_b, lean_a, lean_b, inner, by_gate, by_up = refs[count:]
    rows = pieces[0].shape[0]
    split = gate_a.shape[1]
    for k in range(0, count, 2):
        at = slice(k * rows, (k + 2) * rows)
        for j in range(2):
            here = slice((k + j) * rows, (k + j + 1) * rows)
            lean_a[here, :] = pieces[k + j][:, :split]
            lean_b[here, :] = pieces[k + j][:, split:]
        left, right = lean_a[at, :], lean_b[at, :]
        gate = mt(left, gate_a[...]) + mt(right, gate_b[...])
        up = mt(left, up_a[...]) + mt(right, up_b[...])
        sig = jax.nn.sigmoid(gate)
        silu = gate * sig
        inner[at, :] = (silu * up).astype(BF16)
        by_gate[at, :] = (up * sig * (1.0 + gate * (1.0 - sig))).astype(BF16)
        by_up[at, :] = silu.astype(BF16)


def inner_kernel(chunk, cot_a, cot_b, down_a, down_b, by_gate, by_up, d_gate, d_up):
    for k in range(cot_a.shape[0] // chunk):
        at = slice(k * chunk, (k + 1) * chunk)
        d_inner = mt(cot_a[at, :], down_a[...]) + mt(cot_b[at, :], down_b[...])
        d_gate[at, :] = (d_inner * by_gate[at, :].astype(F32)).astype(BF16)
        d_up[at, :] = (d_inner * by_up[at, :].astype(F32)).astype(BF16)


def rows_kernel(pairs, chunk, *refs):
    out = refs[-1]
    for k in range(out.shape[0] // chunk):
        at = slice(k * chunk, (k + 1) * chunk)
        for j in range(2):
            split = refs[1 + j].shape[1]
            value = mm(refs[0][at, :], refs[1 + j][...])
            for pair in range(1, pairs):
                value += mm(refs[3 * pair][at, :], refs[3 * pair + 1 + j][...])
            out[at, j * split : (j + 1) * split] = value.astype(out.dtype)


def half_rows(pairs, part, dtype, chunk):
    total = pairs[0][0].shape[0]
    width = 2 * pairs[0][1].shape[1]
    specs, arrays = [], []
    for lhs, left, right in pairs:
        specs.append(pl.BlockSpec((total // 2, lhs.shape[1]), lambda i: (part, 0)))
        specs += [pl.BlockSpec(left.shape, lambda i: (0, 0)), pl.BlockSpec(right.shape, lambda i: (0, 0))]
        arrays += [lhs, left, right]
    return pl.pallas_call(
        functools.partial(rows_kernel, len(pairs), chunk),
        out_shape=jax.ShapeDtypeStruct((total // 2, width), dtype),
        grid=(1,),
        in_specs=specs,
        out_specs=pl.BlockSpec((total // 2, width), lambda i: (0, 0)),
        compiler_params=pltpu.CompilerParams(vmem_limit_bytes=48 * 2**20),
        cost_estimate=pl.CostEstimate(flops=1000, bytes_accessed=1000, transcendentals=0),
    )(*arrays)


def branch_kernel(batches, n_dp, z, cot, hidden, unit, gain, *refs):
    terms, parts = refs[: 2 * batches], refs[2 * batches :]
    back = exchange(summed(batches, terms), z[0], n_dp, True)
    value = hidden[...]
    inv = lax.rsqrt(jnp.mean(value * value, axis=1, keepdims=True) + EPS)
    scaled = back * gain[...]
    one = unit[...]
    mean = jnp.mean(scaled * one, axis=1, keepdims=True)
    lean = (cot[...].astype(F32) + inv * (scaled - one * mean)).astype(BF16)
    rows = parts[0].shape[0]
    for m in range(batches):
        parts[m][...] = lean[m * rows : (m + 1) * rows]


def conv_back_kernel(batches, n, count, me, *refs):
    pieces = refs[:count]
    out_a, out_b, conv, c_nat, p_nat, b_arr, x_arr, source, offset, slot, taps = refs[count : count + 11]
    branch, d_b, d_c, d_x, conv_grad, own, natural = refs[count + 11 :]
    total = branch.shape[0]
    group = total // batches
    half = group // 2
    rows = group // n
    cut = out_a.shape[1]
    names = gather_names(n, batches)
    for k in range(count):
        size = pieces[k].shape[0]
        branch[k * size : (k + 1) * size, :] = pieces[k][...]
    for c in range(2):
        for m in range(batches):
            k = c * batches + m
            at = slice(k * half, (k + 1) * half)
            gated = mt(branch[at, :cut], out_a[...]) + mt(branch[at, cut:], out_b[...])
            for j, e in enumerate(names[m]):
                other = me[0] ^ (2 * e + c)
                at = m * group + other * rows
                natural[pl.ds(pl.multiple_of(at, 8), rows), :] = gated[j * rows : (j + 1) * rows]
    totals = [jnp.zeros((1, taps.shape[1]), F32)] * 3
    for m in range(batches):
        gated = natural[m * group : (m + 1) * group, :]
        place = offset[m]
        wide = p_nat[m].astype(F32)
        grad = gated * c_nat[m]
        grad_c = (gated * conv[m]).astype(BF16)
        one = jnp.where(place >= 1, grad, 0.0)
        two = jnp.where(place >= 2, grad, 0.0)
        totals[0] += jnp.sum(two * pltpu.roll(wide, 2, 0), axis=0, keepdims=True)
        totals[1] += jnp.sum(one * pltpu.roll(wide, 1, 0), axis=0, keepdims=True)
        totals[2] += jnp.sum(grad * wide, axis=0, keepdims=True)
        d_product = (
            grad * taps[2:3, :]
            + pltpu.roll(one, group - 1, 0) * taps[1:2, :]
            + pltpu.roll(two, group - 2, 0) * taps[0:1, :]
        ).astype(BF16)
        lines = lax.broadcasted_iota(jnp.int32, (group, group), 0)
        undeal = (source[m] == lines).astype(F32).astype(BF16)
        d_prod = mm(undeal, d_product)
        c_back = mm(undeal, grad_c)
        for c in range(2):
            there = pl.ds((c * batches + m) * half, half)
            piece = d_prod[c * half : (c + 1) * half]
            d_b[there, :] = (piece * x_arr[there, :]).astype(BF16)
            d_c[there, :] = c_back[c * half : (c + 1) * half].astype(BF16)
            d_x[there, :] = (piece * b_arr[there, :]).astype(BF16)
    for k in range(3):
        conv_grad[k : k + 1, :] = totals[k]
    lanes = lax.broadcasted_iota(jnp.int32, (slot.shape[0], total), 1)
    picked = (slot[...] == lanes).astype(F32).astype(BF16)
    own[...] = mm(picked, branch[...]).astype(BF16)


def final_kernel(batches, n_dp, z, tokens, gain, d_hidden, *refs):
    terms, out = refs[:-1], refs[-1]
    back = exchange(summed(batches, terms), z[0], n_dp, True)
    wide = tokens[...].astype(F32)
    inv = lax.rsqrt(jnp.mean(wide * wide, axis=1, keepdims=True) + EPS)
    unit = wide * inv
    scaled = back * gain[...]
    mean = jnp.mean(scaled * unit, axis=1, keepdims=True)
    out[...] = (d_hidden[...].astype(F32) + inv * (scaled - unit * mean)).astype(BF16)


def block_kernel(batches, n_dp, z, hidden, *refs):
    terms, out = refs[:-1], refs[-1]
    out[...] = (hidden[...] + exchange(summed(batches, terms), z[0], n_dp, True)).astype(BF16)


def body(
    tokens_in,
    in_weight,
    conv_weight,
    out_weight,
    norm_gain,
    ff_gain,
    gate_weight,
    up_weight,
    down_weight,
    cotangent,
    deal_table,
    seq_lengths,
):
    batches, rows_dev, width = tokens_in.shape
    n, n_dp = lax.axis_size("shard"), lax.axis_size("dp")
    half = n // 2
    me, z = lax.axis_index("shard"), lax.axis_index("dp")
    group = n * rows_dev
    piece_rows = rows_dev // n
    own_rows, hidden_units = gate_weight.shape
    total = batches * group
    outer = bits_of(n)[1:]
    zblock = n * own_rows
    channels = n_dp * own_rows

    whole = hidden_units // (LANES * n) * LANES
    rest = hidden_units // n - whole

    place = jnp.arange(zblock, dtype=jnp.int32)
    identity = (place[:, None] == place[None, :]).astype(BF16)
    own_total = batches * rows_dev
    share = hidden_units // n
    chunk = total // 4
    cut = width // 2
    names = gather_names(n, batches)

    def dealt(blocks):
        return lax.all_to_all(blocks, "shard", split_axis=0, concat_axis=0, tiled=True)

    def flipped(block):
        return dot(block.reshape(zblock, -1), identity, ((0,), (0,)), BF16)

    in_parts = in_weight.reshape(own_rows, 3 * n_dp, n, own_rows).transpose(2, 0, 1, 3)
    in_parts = in_parts.reshape(n, own_rows, 3 * channels)
    spare = 14
    table = deal_table[:, 0, 0, :].astype(BF16).reshape(-1)
    table = jnp.pad(table, (0, own_rows * spare - table.shape[0])).reshape(own_rows, spare)
    extra = jnp.concatenate([norm_gain[:, None], ff_gain[:, None], table], axis=1)
    in_parts = jnp.concatenate([in_parts, jnp.broadcast_to(extra[None], (n,) + extra.shape)], axis=2)
    in_came = dealt(in_parts)
    tok_turned = turned(tokens_in, z, n_dp)
    tok_pieces, tok_steps = plane_gather([tok_turned[m] for m in range(batches)])
    out_aug = jnp.concatenate(
        [out_weight, conv_weight, jnp.zeros((own_rows, LANES - conv_weight.shape[1]), BF16)], axis=1
    )
    out_lines = out_aug
    for bit in reversed(bits_of(n_dp)):
        out_came = swap(out_lines, bit, "dp")
        if bit > 1:
            out_lines = jnp.concatenate([out_lines, out_came], axis=0)

    in_a, in_b, ready = line_gather(flipped(in_came))
    weights = [gate_weight, up_weight, down_weight]
    [ff_parts] = run(
        functools.partial(spread_kernel, n, whole, rest, 3),
        [((n, 3 * own_rows, share), BF16)],
        [],
        weights,
    )
    ff_came = dealt(after(ff_parts, in_came))
    gate_block, up_block, down_block = [
        flipped(ff_came[:, k * own_rows : (k + 1) * own_rows]) for k in range(3)
    ]
    gate_a, gate_b, ready = line_gather(gate_block, ready)
    gate_high = ready
    up_a, up_b, ready = line_gather(up_block, ready)
    up_high = ready
    down_a, down_b, ready = line_gather(down_block, ready)
    down_high = ready

    def natural_row(row):
        both = jnp.concatenate([in_a[row : row + 1], in_b[row : row + 1]], axis=1)
        step = width // n_dp
        out = None
        for k in range(n_dp):
            order = [reversed_bits(k ^ p, n_dp) for p in range(n_dp)]
            moved = jnp.concatenate([both[:, q * step : (q + 1) * step] for q in order], axis=1)
            out = moved if out is None else jnp.where(z == k, moved, out)
        return out.astype(F32)

    gain_one = natural_row(3 * channels)
    gain_two = natural_row(3 * channels + 1)
    out_a, out_b, tap_cols = run(
        functools.partial(out_kernel, n_dp),
        [((channels, cut), BF16), ((channels, cut), BF16), ((channels, LANES), BF16)],
        [z],
        [out_lines, out_came],
    )
    taps = tap_cols[:, : conv_weight.shape[1]].astype(F32).T

    deal = in_came[:, :, 3 * channels + 2 :].reshape(n, own_rows * spare)[:, : batches * n]
    deal = deal.reshape(n, batches, n).transpose(1, 0, 2).astype(jnp.int32)
    m_index = jnp.arange(batches, dtype=jnp.int32)[:, None, None, None]
    j_index = jnp.arange(n, dtype=jnp.int32)[None, :, None, None]
    t_index = jnp.arange(piece_rows, dtype=jnp.int32)[None, None, None, :]

    def place_of(e, m):
        out = jnp.zeros_like(e + m)
        for part in range(batches):
            for k, name in enumerate(names[part]):
                out = jnp.where((e == name) & (m == part), k, out)
        return out

    def within(m, holder, row):
        rel = holder ^ me
        return ((rel & 1) * half + place_of(rel >> 1, m)) * rows_dev + row

    def arrival_row(m, holder, row):
        rel = holder ^ me
        return (((rel & 1) * batches + m) * half + place_of(rel >> 1, m)) * rows_dev + row

    slot_row = j_index * piece_rows + t_index
    source = within(m_index, deal[:, :, :, None], slot_row).reshape(batches, group)
    own_deal = lax.dynamic_index_in_dim(deal, me, 1, keepdims=True)[:, :, :, None]
    own_source = arrival_row(m_index, own_deal, me * piece_rows + t_index).reshape(own_total, 1)
    inverse = jnp.sum(jnp.where(deal == me, jnp.arange(n, dtype=jnp.int32)[None, None, :], 0), axis=2)
    slot_source = arrival_row(
        m_index[:, :, 0], j_index[:, :, 0], inverse[:, :, None] * piece_rows + t_index[:, 0]
    ).reshape(own_total, 1)

    lengths = seq_lengths[:, 0, :]
    places = jnp.arange(group, dtype=jnp.int32)
    seq_start = jnp.zeros((batches, group), jnp.int32)
    start = jnp.zeros((batches,), jnp.int32)
    for k in range(lengths.shape[1]):
        seq_start = jnp.where(start[:, None] <= places[None, :], start[:, None], seq_start)
        start = start + lengths[:, k]
    offset = (places[None, :] - seq_start)[:, :, None]

    arr = (total, channels)
    nat = (batches, group, channels)
    own = (own_total, width)
    side = (total, cut)
    normed_a, normed_b, product, c_high, c_low, b_arr, x_arr, own_tok = run(
        functools.partial(project_kernel, channels, len(tok_pieces)),
        [(side, BF16), (side, BF16), (arr, BF16), (arr, BF16), (arr, BF16), (arr, F32), (arr, F32), (own, BF16)],
        [],
        [*tok_pieces, in_a, in_b, own_source],
        [pltpu.VMEM((total, width), BF16)],
    )
    p_nat, c_nat, conv_out, gated_arr = run(
        functools.partial(conv_kernel, batches, n),
        [(nat, BF16), (nat, F32), (nat, F32), (arr, BF16)],
        [me],
        [product, c_high, c_low, source[:, :, None], offset, taps],
        [pltpu.VMEM((group, channels), F32)],
    )
    cot_turned = turned(cotangent, z, n_dp)
    cot_pieces, cot_steps = plane_gather([cot_turned[m] for m in range(batches)], ((ff_came, *tok_steps[-1]), ()))

    def summed_rows(*pairs, wait=()):
        far = half_rows(pairs, 1, BF16, chunk)
        near = half_rows(pairs, 0, F32, chunk)
        return plane_reduce(near, far, batches, wait)

    mine = ((rows_dev, width), BF16)
    hidden, unit_two, *ff_own = run(
        functools.partial(hidden_kernel, batches, n_dp),
        [(own, F32), (own, F32)] + [mine] * batches,
        [z],
        [own_tok, gain_two, *summed_rows((gated_arr, out_a, out_b), wait=(*gate_high, *cot_steps[-1]))],
    )
    ff_pieces, ff_steps = plane_gather(ff_own, ((), (gate_b, *up_high)))
    cot_a, cot_b = run(
        functools.partial(side_kernel, len(cot_pieces)), [(side, BF16), (side, BF16)], [], cot_pieces
    )

    ff = (total, share)
    ff_pieces[0] = after(ff_pieces[0], *down_high)
    lean_a, lean_b, ff_inner, by_gate, by_up = run(
        functools.partial(gate_kernel, len(ff_pieces)),
        [(side, BF16), (side, BF16), (ff, BF16), (ff, BF16), (ff, BF16)],
        [],
        [*ff_pieces, gate_a, gate_b, up_a, up_b],
    )

    def outer_sum(former, left, right, wait=None):
        send = dot(former, right, ((0,), (0,)), BF16)
        keep = dot(former, left, ((0,), (0,)))
        return line_reduce(keep, send, wait)

    def returned(terms, *wait):
        value = (terms[0] + terms[1].astype(F32)).astype(BF16)
        rows = dot(identity, value, ((1,), (1,)), BF16)
        return dealt(after(rows.reshape(n, own_rows, -1), *wait))

    *down_sum, down_low = outer_sum(ff_inner, cot_a, cot_b)
    d_gate, d_up = run(
        functools.partial(inner_kernel, chunk),
        [(ff, BF16), (ff, BF16)],
        [],
        [cot_a, cot_b, down_a, down_b, by_gate, by_up],
    )
    d_ff = summed_rows((d_gate, gate_a, gate_b), (d_up, up_a, up_b), wait=down_low)
    *gate_sum, gate_low = outer_sum(d_gate, lean_a, lean_b, down_low)
    *up_sum, up_low = outer_sum(d_up, lean_a, lean_b, gate_low)
    cot_own = cotangent.reshape(own)
    branch_own = run(
        functools.partial(branch_kernel, batches, n_dp),
        [mine] * batches,
        [z],
        [cot_own, hidden, unit_two, gain_two, *d_ff],
    )
    branch_pieces, branch_steps = plane_gather(branch_own, (gate_low, ()))
    block_sum = summed_rows((ff_inner, down_a, down_b), wait=branch_steps[-1])
    [block_out] = run(functools.partial(block_kernel, batches, n_dp), [(own, BF16)], [z], [hidden, *block_sum])
    block_out = block_out.reshape(tokens_in.shape)
    down_back = returned(down_sum, *branch_steps[-1])

    branch_pieces[0] = after(branch_pieces[0], *up_low)
    branch, *d_proj, conv_term, d_hidden_own = run(
        functools.partial(conv_back_kernel, batches, n, len(branch_pieces)),
        [((total, width), BF16), (arr, BF16), (arr, BF16), (arr, BF16), ((3, channels), F32), (own, BF16)],
        [me],
        [
            *branch_pieces,
            out_a,
            out_b,
            conv_out,
            c_nat,
            p_nat,
            b_arr,
            x_arr,
            source[:, None, :],
            offset,
            slot_source,
            taps,
        ],
        [pltpu.VMEM((total, channels), F32)],
    )
    rows_of = [slice(k * channels, (k + 1) * channels) for k in range(3)]
    gate_back = returned(gate_sum, down_back)
    d_normed = summed_rows(
        *[(d_proj[k], in_a[rows_of[k]], in_b[rows_of[k]]) for k in range(3)], wait=(down_back, gate_back)
    )
    [tokens_grad] = run(
        functools.partial(final_kernel, batches, n_dp),
        [(own, BF16)],
        [z],
        [tokens_in.reshape(own), gain_one, d_hidden_own, *d_normed],
    )
    tokens_grad = tokens_grad.reshape(tokens_in.shape)

    in_send = jnp.concatenate([dot(d_proj[k], normed_b, ((0,), (0,)), BF16) for k in range(3)], axis=0)
    in_keep = jnp.concatenate([dot(d_proj[k], normed_a, ((0,), (0,))) for k in range(3)], axis=0)
    *in_sum, in_low = line_reduce(in_keep, in_send, up_low)
    up_back = returned(up_sum)
    conv_cols = jnp.pad(conv_term.T, ((0, 0), (0, LANES - conv_term.shape[0])))
    keep, send = run(
        functools.partial(relative_kernel, n_dp),
        [((channels // 2, width + LANES), F32), ((channels // 2, width + LANES), BF16)],
        [z],
        [dot(gated_arr, branch, ((0,), (0,))), conv_cols],
    )
    send = after(send, *in_low)
    for bit in bits_of(n_dp):
        came = swap(send, bit, "dp").astype(F32)
        keep = keep + came
        if 2 * bit < n_dp:
            keep, send = jnp.split(keep, 2, axis=0)
            send = send.astype(BF16)
    out_grad = keep[:, :width]
    conv_grad = keep[:, width : width + conv_weight.shape[1]]
    in_back = returned(in_sum)

    def joined(kernel, came, weight):
        shape = weight.shape
        return run(kernel, [(shape, F32), ((own_rows, 1), F32)], [], [came, weight])

    join = functools.partial(join_kernel, n, whole, rest)
    down_grad, _ = joined(join, down_back, down_weight)
    gate_grad, gate_dots = joined(join, gate_back, gate_weight)
    up_grad, up_dots = joined(join, up_back, up_weight)
    in_grad, in_dots = joined(functools.partial(join_in_kernel, n, 3 * n_dp), in_back, in_weight)
    norm_gain_grad = in_dots[:, 0] / norm_gain.astype(F32)
    ff_gain_grad = (gate_dots + up_dots)[:, 0] / ff_gain.astype(F32)
    return (
        block_out,
        tokens_grad,
        in_grad,
        conv_grad,
        out_grad,
        norm_gain_grad,
        ff_gain_grad,
        gate_grad,
        up_grad,
        down_grad,
    )


def solution(mesh):
    rows = P(("dp", "shard"), None)
    tokens = P(None, ("dp", "shard"), None)
    vector = P(("dp", "shard"))
    placed = (
        tokens,
        rows,
        rows,
        rows,
        vector,
        vector,
        rows,
        rows,
        rows,
        tokens,
        P(None, "dp", "shard", None),
        P(None, "dp", None),
    )
    return jax.shard_map(
        body,
        mesh=mesh,
        in_specs=placed,
        out_specs=(tokens, tokens, rows, rows, rows, vector, vector, rows, rows, rows),
        check_vma=False,
    )
```

time: 2340 us -> 574 us (0.25)
  waiting for transfers between devices: 1960 us -> 208 us
  matrix products: 182 us -> 50.7 us
  Pallas kernels: 0 us -> 131 us
  blocking collectives: 85.5 us -> 0 us
  starting transfers between devices: 15.3 us -> 84 us
    reduce_scatter x4 -> x0, waiting for transfers between devices: 1130 us -> none  [the longest x1 387 us: body(): lax.psum_scatter(gate_term, ('dp', 'shard'), scatter_dimension=0, tiled=T...]
    all_gather x5 -> x0, waiting for transfers between devices: 434 us -> none  [the longest x1 131 us: body(): lax.all_gather(gate_weight, ('dp', 'shard'), axis=0, tiled=True)]
    unnamed x13 -> x0, waiting for transfers between devices: 389 us -> none
    ppermute x2 -> x72, waiting for transfers between devices: 0.01 us -> 204 us  [swap(): return lax.ppermute(value, axis, [(i, i ^ bit) for i in range(n)])]
    dot_general x15 -> x21, matrix products: 182 us -> 50.7 us  [dot(): lax.dot_general(former, latter, ((dims[0], dims[1]), ((), ())), preferred...]
    pallas_call x0 -> x33, Pallas kernels: none -> 131 us  [the longest x25 90.7 us: run(): pl.pallas_call(kernel, out_shape=[jax.ShapeDtypeStruct(shape, dtype) for...]
    ppermute x2 -> x72, starting transfers between devices: 4.75 us -> 59.8 us  [swap(): return lax.ppermute(value, axis, [(i, i ^ bit) for i in range(n)])]
    all_gather x1 -> x0, blocking collectives: 45.2 us -> none  [body(): lax.all_gather(conv_weight, ('dp', 'shard'), axis=0, tiled=True)]
  transfers between devices with their start and end apart: 15 -> 78, of which waited for: 10 -> 25; matrix products, arithmetic and copies ran while one was open for 8% -> 18% of each run, Pallas kernels for 0% -> 19%
where the time goes in v2:
time: 574 us; the launch traced here: 567 us
  waiting for transfers between devices  208 us (36%)
  Pallas kernels  131 us (23%)
  starting transfers between devices  84 us (15%)
  local copies, waits for them, and re-layouts  70.5 us (12%)
  matrix products  50.7 us (9%)
  other arithmetic  20.6 us (4%)
    ppermute x72, waiting for transfers between devices, swap(): return lax.ppermute(value, axis, [(i, i ^ bit) for i in range(n)])  204 us
    pallas_call x25, Pallas kernels, run(): pl.pallas_call(kernel, out_shape=[jax.ShapeDtypeStruct(shape, dtype) for...  90.7 us
    ppermute x72, starting transfers between devices, swap(): return lax.ppermute(value, axis, [(i, i ^ bit) for i in range(n)])  59.8 us
    dot_general x21, matrix products, dot(): lax.dot_general(former, latter, ((dims[0], dims[1]), ((), ())), preferred...  50.7 us
    unnamed x283, local copies, waits for them, and re-layouts  41.9 us
    pallas_call x8, Pallas kernels, half_rows(): pl.pallas_call(functools.partial(rows_kernel, len(pairs), chunk), out_sha...  40.2 us
    all_to_all x6, starting transfers between devices, dealt(): lax.all_to_all(blocks, 'shard', split_axis=0, concat_axis=0, tiled=True)  24.3 us
  transfers between devices with their start and end apart: 78, of which 25 were waited for; matrix products, arithmetic and copies ran while one was open for 18% of the time, Pallas kernels for 19%

profile of v2, /device:TPU:0, one launch (start us, length us, event | category | flops | bytes accessed | tf_op | source)
XLA Modules:
  0.0 567.0 jit_solution(2244492211760658544)
XLA Ops:
  40.2 4.8 all-to-all-start.1
  45.1 12.3 %collective-permute-done.8 = bf16[592,384]{1,0:T(8,128)(2,1)S(1)} collective-permute-done((bf16[592,384]{1,0:T(8,128)(2,1)S(1)}, bf16[592,384]{1,0:T(8,128)(2,1)S(1)}, u32[]{:S(2)}, u32[]{:S(2)}) %collective-permute-start.8) | collective-permute-done | bytes 454688 | tf_op jit(solution)/shard_map/ppermute | solution.py:28
  65.9 15.0 %collective-permute-done.9.refs_9_ = bf16[592,768]{1,0:T(8,128)(2,1)} collective-permute-done((bf16[592,768]{1,0:T(8,128)(2,1)}, bf16[592,768]{1,0:T(8,128)(2,1)}, u32[]{:S(2)}, u32[]{:S(2)}) %collective-permute-start.9) | collective-permute-done | bytes 909344 | tf_op jit(solution)/shard_map/ppermute | solution.py:28
  81.0 10.4 %shard_map.195 = (bf16[1536,768]{1,0:T(8,128)(2,1)}, bf16[1536,768]{1,0:T(8,128)(2,1)}, bf16[1536,192]{1,0:T(8,128)(2,1)S(1)}, bf16[1536,192]{1,0:T(8,128)(2,1)}...) custom-call(bf16[192,1536]{1,0:T(8,128)(2,1)S(1)} %pad_maximum_fusion.2., ...), custom_call_target="tpu_custom_call" | custom-call | flops 1000 | bytes 1000 | tf_op jit(solution)/shard_map/pallas_call | solution.py:189
  93.8 4.2 shard_map.197
  105.8 6.2 %collective-permute-done.16 = bf16[96,1536]{1,0:T(8,128)(2,1)S(1)} collective-permute-done((bf16[96,1536]{1,0:T(8,128)(2,1)S(1)}, bf16[96,1536]{1,0:T(8,128)(2,1)S(1)}, u32[]{:S(2)}, u32[]{:S(2)}) %collective-permute-start.16) | collective-permute-done | bytes 294944 | tf_op jit(solution)/shard_map/ppermute | solution.py:28
  116.8 20.5 %collective-permute-done.13 = bf16[864,384]{1,0:T(8,128)(2,1)S(1)} collective-permute-done((bf16[864,384]{1,0:T(8,128)(2,1)S(1)}, bf16[864,384]{1,0:T(8,128)(2,1)S(1)}, u32[]{:S(2)}, u32[]{:S(2)}) %collective-permute-start.13) | collective-permute-done | bytes 663584 | tf_op jit(solution)/shard_map/ppermute | solution.py:28
  146.9 19.5 %collective-permute-done.24 = bf16[864,384]{1,0:T(8,128)(2,1)S(1)} collective-permute-done((bf16[864,384]{1,0:T(8,128)(2,1)S(1)}, bf16[864,384]{1,0:T(8,128)(2,1)S(1)}, u32[]{:S(2)}, u32[]{:S(2)}) %collective-permute-start.24) | collective-permute-done | bytes 663584 | tf_op jit(solution)/shard_map/ppermute | solution.py:28
  169.6 6.0 %collective-permute-done.20.refs_2_ = bf16[96,1536]{1,0:T(8,128)(2,1)S(1)} collective-permute-done((bf16[96,1536]{1,0:T(8,128)(2,1)S(1)}, bf16[96,1536]{1,0:T(8,128)(2,1)S(1)}, u32[]{:S(2)}, u32[]{:S(2)}) %collective-permute-start.20) | collective-permute-done | bytes 294944 | tf_op jit(solution)/shard_map/ppermute | solution.py:28
  181.1 17.7 %collective-permute-done.25 = bf16[864,384]{1,0:T(8,128)(2,1)} collective-permute-done((bf16[864,384]{1,0:T(8,128)(2,1)}, bf16[864,384]{1,0:T(8,128)(2,1)}, u32[]{:S(2)}, u32[]{:S(2)}) %collective-permute-start.25) | collective-permute-done | bytes 663584 | tf_op jit(solution)/shard_map/ppermute | solution.py:28
  202.1 6.3 %collective-permute-done.27 = bf16[96,1536]{1,0:T(8,128)(2,1)S(1)} collective-permute-done((bf16[96,1536]{1,0:T(8,128)(2,1)S(1)}, bf16[96,1536]{1,0:T(8,128)(2,1)S(1)}, u32[]{:S(2)}, u32[]{:S(2)}) %collective-permute-start.27) | collective-permute-done | bytes 294944 | tf_op jit(solution)/shard_map/ppermute | solution.py:28
  214.6 11.8 %collective-permute-done.33.refs_11_.refs_5_ = bf16[864,768]{1,0:T(8,128)(2,1)S(1)} collective-permute-done((bf16[864,768]{1,0:T(8,128)(2,1)S(1)}, bf16[864,768]{1,0:T(8,128)(2,1)S(1)}, u32[]{:S(2)}, u32[]{:S(2)}) %collective-permute-start.33) | collective-permute-done | bytes 1327136 | tf_op jit(solution)/shard_map/ppermute | solution.py:28
  239.5 17.6 %shard_map.204 = (bf16[1536,768]{1,0:T(8,128)(2,1)}, bf16[1536,768]{1,0:T(8,128)(2,1)}, bf16[1536,864]{1,0:T(8,128)(2,1)}, bf16[1536,864]{1,0:T(8,128)(2,1)}, bf16[1536,864]{1,0:T(8,128)(2,1)}) custom-call(bf16[192,1536]{1,0:T(8,128)(2,1)S(1)} %pad_maximum_fusion.4.refs_0_, bf16[192,1536]{1,0:T(8,128)(2,1)} %collective-permute-done.26.refs_1_, ...), custom_call_target="tpu_custom_call" | custom-call | flops 1000 | bytes 1000 | tf_op jit(solution)/shard_map/pallas_call | solution.py:189
  257.1 11.5 %shard_map.209 = (bf16[1536,864]{1,0:T(8,128)(2,1)}, bf16[1536,864]{1,0:T(8,128)(2,1)}) custom-call(bf16[1536,768]{1,0:T(8,128)(2,1)S(1)} %copy-done.17, bf16[1536,768]{1,0:T(8,128)(2,1)} %get-tuple-element.149.cot_b, bf16[864,768]{1,0:T(8,128)(2,1)S(1)} %constant_dynamic-update-slice_fusion.8.refs_1_.down_a, ...), custom_call_target="tpu_custom_call" | custom-call | flops 1000 | bytes 1000 | tf_op jit(solution)/shard_map/pallas_call | solution.py:189
  268.7 8.3 %shard_map.211 = bf16[768,1536]{1,0:T(8,128)(2,1)} custom-call(bf16[1536,864]{1,0:T(8,128)(2,1)} %get-tuple-element.152.refs_0_, bf16[864,768]{1,0:T(8,128)(2,1)S(1)} %copy-done.6, bf16[864,768]{1,0:T(8,128)(2,1)S(1)} %copy-done.12, bf16[1536,864]{1,0:T(8,128)(2,1)} %get-tuple-element.153.refs_3_, bf16[864,768]{1,0:T(8,128)(2,1)S(1)} %copy-done.9, ...), custom_call_target="tpu_custom_call" | custom-call | flops 1000 | bytes 1000 | tf_op jit(solution)/shard_map/pallas_call | solution.py:407
  285.4 6.3 %convolution_convert_fusion.1 = bf16[864,768]{1,0:T(8,128)(2,1)} fusion(bf16[1536,864]{1,0:T(8,128)(2,1)} %get-tuple-element.152.refs_0_, bf16[1536,768]{1,0:T(8,128)(2,1)} %get-tuple-element.165), kind=kOutput, calls=%fused_computation.5 | convolution fusion | flops 2039095296 | bytes 6340608 | tf_op jit(solution)/shard_map/dot_general | solution.py:17
  291.7 20.5 %collective-permute-done.41 = bf16[864,768]{1,0:T(8,128)(2,1)} collective-permute-done((bf16[864,768]{1,0:T(8,128)(2,1)}, bf16[864,768]{1,0:T(8,128)(2,1)}, u32[]{:S(2)}, u32[]{:S(2)}) %collective-permute-start.41) | collective-permute-done | bytes 1327136 | tf_op jit(solution)/shard_map/ppermute | solution.py:28
  316.1 5.9 %shard_map.206 = bf16[768,1536]{1,0:T(8,128)(2,1)} custom-call(bf16[1536,864]{1,0:T(8,128)(2,1)} %get-tuple-element.143.refs_0_, bf16[864,768]{1,0:T(8,128)(2,1)S(1)} %copy-done.4, bf16[864,768]{1,0:T(8,128)(2,1)} %collective-permute-done.34.refs_2_.down_b), custom_call_target="tpu_custom_call" | custom-call | flops 1000 | bytes 1000 | tf_op jit(solution)/shard_map/pallas_call | solution.py:407
  322.1 9.1 %shard_map.210.near = f32[768,1536]{1,0:T(8,128)} custom-call(bf16[1536,864]{1,0:T(8,128)(2,1)} %get-tuple-element.152.refs_0_, bf16[864,768]{1,0:T(8,128)(2,1)S(1)} %copy-done.7, bf16[864,768]{1,0:T(8,128)(2,1)S(1)} %copy-done.13, bf16[1536,864]{1,0:T(8,128)(2,1)} %get-tuple-element.153.refs_3_, bf16[864,768]{1,0:T(8,128)(2,1)S(1)} %copy-done.10, ...), custom_call_target="tpu_custom_call" | custom-call | flops 1000 | bytes 1000 | tf_op jit(solution)/shard_map/pallas_call | solution.py:407
  346.8 7.0 %collective-permute-done.43.refs_3_ = bf16[192,1536]{1,0:T(8,128)(2,1)S(1)} collective-permute-done((bf16[192,1536]{1,0:T(8,128)(2,1)S(1)}, bf16[192,1536]{1,0:T(8,128)(2,1)S(1)}, u32[]{:S(2)}, u32[]{:S(2)}) %collective-permute-start.43) | collective-permute-done | bytes 589856 | tf_op jit(solution)/shard_map/ppermute | solution.py:28
  357.3 4.8 convert_add_fusion.1
  368.9 4.9 collective-permute-done.47
  376.0 28.7 %collective-permute-done.55 = bf16[864,768]{1,0:T(8,128)(2,1)} collective-permute-done((bf16[864,768]{1,0:T(8,128)(2,1)}, bf16[864,768]{1,0:T(8,128)(2,1)}, u32[]{:S(2)}, u32[]{:S(2)}) %collective-permute-start.55) | collective-permute-done | bytes 1327136 | tf_op jit(solution)/shard_map/ppermute | solution.py:28
  410.9 6.2 %shard_map.205.near = f32[768,1536]{1,0:T(8,128)} custom-call(bf16[1536,864]{1,0:T(8,128)(2,1)S(1)} %copy-done.1, bf16[864,768]{1,0:T(8,128)(2,1)S(1)} %copy-done.4, bf16[864,768]{1,0:T(8,128)(2,1)} %collective-permute-done.34.refs_2_.down_b), custom_call_target="tpu_custom_call" | custom-call | flops 1000 | bytes 1000 | tf_op jit(solution)/shard_map/pallas_call | solution.py:407
  422.0 4.1 shard_map.207
  435.6 4.7 collective-permute-done.71
  454.1 11.1 %shard_map.217 = (bf16[1536,1536]{1,0:T(8,128)(2,1)}, bf16[1536,192]{1,0:T(8,128)(2,1)}, bf16[1536,192]{1,0:T(8,128)(2,1)}, bf16[1536,192]{1,0:T(8,128)(2,1)}, f...) custom-call(s32[1]{0:T(128)} %bitcast.12.me, bf16[192,1536]{1,0:T(8,128)(2,1)} %constant_dynamic-update-slice_fusion.10.refs_0_, ...), custom_call_target="tpu_custom_call" | custom-call | flops 1000 | bytes 1000 | tf_op jit(solution)/shard_map/pallas_call | solution.py:189
  472.8 4.2 shard_map.218.near
  496.3 4.2 all-to-all-start.3
  518.8 4.4 shard_map.220
  528.4 14.3 %collective-permute-done.68 = bf16[576,384]{1,0:T(8,128)(2,1)S(1)} collective-permute-done((bf16[576,384]{1,0:T(8,128)(2,1)S(1)}, bf16[576,384]{1,0:T(8,128)(2,1)S(1)}, u32[]{:S(2)}, u32[]{:S(2)}) %collective-permute-start.68) | collective-permute-done | bytes 442400 | tf_op jit(solution)/shard_map/ppermute | solution.py:28
  544.1 4.2 all-to-all-start.4
  (559 shorter events, 247.5 us)
Async XLA Ops:
  27.2 32.0 %collective-permute-start.11 = (bf16[96,1664]{1,0:T(8,128)(2,1)S(1)}, bf16[96,1664]{1,0:T(8,128)(2,1)S(1)}, u32[]{:S(2)}, u32[]{:S(2)}) collective-permute-start(bf16[96,1664]{1,0:T(8,128)(2,1)S(1)} %pad_maximum_fusion.7.first), channel_id=1, source_target_pairs={{0,8},{8,0},{16,24},{24,16},{1,9},{9,1},{17,25},{25,17},{2,10},{10... | collective-permute-start | bytes 958472 | tf_op jit(solution)/shard_map/ppermute | solution.py:28
  30.0 35.9 %collective-permute-start.4 = (bf16[192,1536]{1,0:T(8,128)(2,1)S(1)}, bf16[192,1536]{1,0:T(8,128)(2,1)}, u32[]{:S(2)}, u32[]{:S(2)}) collective-permute-start(bf16[192,1536]{1,0:T(8,128)(2,1)S(1)} %pad_maximum_fusion.2.refs_0_), channel_id=1, source_target_pairs={{0,1},{1,0},{2,3},{3,2},{4,5},{5,4},{6,7},{7,6},{8,9},{9,8},{10,11... | collective-permute-start | bytes 1769480 | tf_op jit(solution)/shard_map/ppermute | solution.py:28
  30.1 29.9 %collective-permute-start.1 = (bf16[192,1536]{1,0:T(8,128)(2,1)S(1)}, bf16[192,1536]{1,0:T(8,128)(2,1)}, u32[]{:S(2)}, u32[]{:S(2)}) collective-permute-start(bf16[192,1536]{1,0:T(8,128)(2,1)S(1)} %pad_maximum_fusion.2.refs_0_), channel_id=1, source_target_pairs={{0,4},{1,5},{2,6},{3,7},{4,0},{5,1},{6,2},{7,3},{8,12},{9,13},{10,... | collective-permute-start | bytes 1769480 | tf_op jit(solution)/shard_map/ppermute | solution.py:28
  40.2 61.1 %all-to-all-start.1 = ((bf16[8,144,864]{2,1,0:T(8,128)(2,1)}), bf16[8,144,864]{2,1,0:T(8,128)(2,1)}, u32[]{:S(2)}, u32[]{:S(2)}) async-start(bf16[8,144,864]{2,1,0:T(8,128)(2,1)} %shard_map.201), calls=%async_computation.1 | async-start | bytes 4128768 | tf_op jit(solution)/shard_map/all_to_all | solution.py:542
  101.2 37.2 %collective-permute-start.12 = (bf16[768,1536]{1,0:T(8,128)(2,1)}, bf16[768,1536]{1,0:T(8,128)(2,1)}, u32[]{:S(2)}, u32[]{:S(2)}) collective-permute-start(bf16[768,1536]{1,0:T(8,128)(2,1)} %shard_map.199), channel_id=1, source_target_pairs={{0,1},{1,0},{2,3},{3,2},{4,5},{5,4},{6,7},{7,6},{8,9},{9,8},{10,11... | collective-permute-start | bytes 7077896 | tf_op jit(solution)/shard_map/ppermute | solution.py:28
  105.7 31.7 %collective-permute-start.13 = (bf16[864,384]{1,0:T(8,128)(2,1)S(1)}, bf16[864,384]{1,0:T(8,128)(2,1)S(1)}, u32[]{:S(2)}, u32[]{:S(2)}) collective-permute-start(bf16[864,384]{1,0:T(8,128)(2,1)S(1)} %convolution_convert_fusion.8), channel_id=1, source_target_pairs={{0,16},{8,24},{16,0},{24,8},{1,17},{9,25},{17,1},{25,9},{2,18},{10... | collective-permute-start | bytes 1990664 | tf_op jit(solution)/shard_map/ppermute | solution.py:28
  112.0 29.9 %collective-permute-start.17 = (bf16[192,1536]{1,0:T(8,128)(2,1)S(1)}, bf16[192,1536]{1,0:T(8,128)(2,1)S(1)}, u32[]{:S(2)}, u32[]{:S(2)}) collective-permute-start(bf16[192,1536]{1,0:T(8,128)(2,1)S(1)} %constant_dynamic-update-slice_fusion.2.refs_2_), channel_id=1, source_target_pairs={{0,2},{1,3},{2,0},{3,1},{4,6},{5,7},{6,4},{7,5},{8,10},{9,11},{10,... | collective-permute-start | bytes 1769480 | tf_op jit(solution)/shard_map/ppermute | solution.py:28
  112.6 29.3 %collective-permute-start.15 = (bf16[192,1536]{1,0:T(8,128)(2,1)S(1)}, bf16[192,1536]{1,0:T(8,128)(2,1)S(1)}, u32[]{:S(2)}, u32[]{:S(2)}) collective-permute-start(bf16[192,1536]{1,0:T(8,128)(2,1)S(1)} %constant_dynamic-update-slice_fusion.refs_0_), channel_id=1, source_target_pairs={{0,4},{1,5},{2,6},{3,7},{4,0},{5,1},{6,2},{7,3},{8,12},{9,13},{10,... | collective-permute-start | bytes 1769480 | tf_op jit(solution)/shard_map/ppermute | solution.py:28
  137.4 29.1 %collective-permute-start.24 = (bf16[864,384]{1,0:T(8,128)(2,1)S(1)}, bf16[864,384]{1,0:T(8,128)(2,1)S(1)}, u32[]{:S(2)}, u32[]{:S(2)}) collective-permute-start(bf16[864,384]{1,0:T(8,128)(2,1)S(1)} %convolution_convert_fusion.7), channel_id=1, source_target_pairs={{0,16},{8,24},{16,0},{24,8},{1,17},{9,25},{17,1},{25,9},{2,18},{10... | collective-permute-start | bytes 1990664 | tf_op jit(solution)/shard_map/ppermute | solution.py:28
  137.5 61.3 %collective-permute-start.23 = (bf16[864,768]{1,0:T(8,128)(2,1)S(1)}, bf16[864,768]{1,0:T(8,128)(2,1)S(1)}, u32[]{:S(2)}, u32[]{:S(2)}) collective-permute-start(bf16[864,768]{1,0:T(8,128)(2,1)S(1)} %constant_dynamic-update-slice_fusion.4.refs_8_.refs_1_), channel_id=1, source_target_pairs={{0,8},{8,0},{16,24},{24,16},{1,9},{9,1},{17,25},{25,17},{2,10},{10... | collective-permute-start | bytes 3981320 | tf_op jit(solution)/shard_map/ppermute | solution.py:28
  166.5 32.4 %collective-permute-start.25 = (bf16[864,384]{1,0:T(8,128)(2,1)}, bf16[864,384]{1,0:T(8,128)(2,1)}, u32[]{:S(2)}, u32[]{:S(2)}) collective-permute-start(bf16[864,384]{1,0:T(8,128)(2,1)} %convolution_convert_fusion.6), channel_id=1, source_target_pairs={{0,16},{8,24},{16,0},{24,8},{1,17},{9,25},{17,1},{25,9},{2,18},{10... | collective-permute-start | bytes 1990664 | tf_op jit(solution)/shard_map/ppermute | solution.py:28
  169.5 39.7 %collective-permute-start.38 = (bf16[192,1536]{1,0:T(8,128)(2,1)S(1)}, bf16[192,1536]{1,0:T(8,128)(2,1)S(1)}, u32[]{:S(2)}, u32[]{:S(2)}) collective-permute-start(bf16[192,1536]{1,0:T(8,128)(2,1)S(1)} %constant_dynamic-update-slice_fusion.2.refs_2_), channel_id=1, source_target_pairs={{0,1},{1,0},{2,3},{3,2},{4,5},{5,4},{6,7},{7,6},{8,9},{9,8},{10,11... | collective-permute-start | bytes 1769480 | tf_op jit(solution)/shard_map/ppermute | solution.py:28
  178.5 47.9 %collective-permute-start.33 = (bf16[864,768]{1,0:T(8,128)(2,1)S(1)}, bf16[864,768]{1,0:T(8,128)(2,1)S(1)}, u32[]{:S(2)}, u32[]{:S(2)}) collective-permute-start(bf16[864,768]{1,0:T(8,128)(2,1)S(1)} %constant_dynamic-update-slice_fusion.6.refs_10_.refs_4_), channel_id=1, source_target_pairs={{0,8},{8,0},{16,24},{24,16},{1,9},{9,1},{17,25},{25,17},{2,10},{10... | collective-permute-start | bytes 3981320 | tf_op jit(solution)/shard_map/ppermute | solution.py:28
  208.4 48.7 %collective-permute-start.34 = (bf16[864,768]{1,0:T(8,128)(2,1)S(1)}, bf16[864,768]{1,0:T(8,128)(2,1)}, u32[]{:S(2)}, u32[]{:S(2)}) collective-permute-start(bf16[864,768]{1,0:T(8,128)(2,1)S(1)} %constant_dynamic-update-slice_fusion.8.refs_1_.down_a), channel_id=1, source_target_pairs={{0,8},{8,0},{16,24},{24,16},{1,9},{9,1},{17,25},{25,17},{2,10},{10... | collective-permute-start | bytes 3981320 | tf_op jit(solution)/shard_map/ppermute | solution.py:28
  277.0 57.5 %collective-permute-start.40 = (bf16[768,1536]{1,0:T(8,128)(2,1)}, bf16[768,1536]{1,0:T(8,128)(2,1)}, u32[]{:S(2)}, u32[]{:S(2)}) collective-permute-start(bf16[768,1536]{1,0:T(8,128)(2,1)} %shard_map.211), channel_id=1, source_target_pairs={{0,1},{1,0},{2,3},{3,2},{4,5},{5,4},{6,7},{7,6},{8,9},{9,8},{10,11... | collective-permute-start | bytes 7077896 | tf_op jit(solution)/shard_map/ppermute | solution.py:28
  280.8 31.4 %collective-permute-start.41 = (bf16[864,768]{1,0:T(8,128)(2,1)}, bf16[864,768]{1,0:T(8,128)(2,1)}, u32[]{:S(2)}, u32[]{:S(2)}) collective-permute-start(bf16[864,768]{1,0:T(8,128)(2,1)} %convolution_convert_fusion.2), channel_id=1, source_target_pairs={{0,8},{8,0},{16,24},{24,16},{1,9},{9,1},{17,25},{25,17},{2,10},{10... | collective-permute-start | bytes 3981320 | tf_op jit(solution)/shard_map/ppermute | solution.py:28
  312.2 32.9 %collective-permute-start.46 = (bf16[864,768]{1,0:T(8,128)(2,1)}, bf16[864,768]{1,0:T(8,128)(2,1)}, u32[]{:S(2)}, u32[]{:S(2)}) collective-permute-start(bf16[864,768]{1,0:T(8,128)(2,1)} %convolution_convert_fusion.1), channel_id=1, source_target_pairs={{0,8},{8,0},{16,24},{24,16},{1,9},{9,1},{17,25},{25,17},{2,10},{10... | collective-permute-start | bytes 3981320 | tf_op jit(solution)/shard_map/ppermute | solution.py:28
  322.0 95.1 %collective-permute-start.35 = (bf16[768,1536]{1,0:T(8,128)(2,1)}, bf16[768,1536]{1,0:T(8,128)(2,1)}, u32[]{:S(2)}, u32[]{:S(2)}) collective-permute-start(bf16[768,1536]{1,0:T(8,128)(2,1)} %shard_map.206), channel_id=1, source_target_pairs={{0,1},{1,0},{2,3},{3,2},{4,5},{5,4},{6,7},{7,6},{8,9},{9,8},{10,11... | collective-permute-start | bytes 7077896 | tf_op jit(solution)/shard_map/ppermute | solution.py:28
  345.0 65.1 %collective-permute-start.61 = (bf16[864,384]{1,0:T(8,128)(2,1)S(1)}, bf16[864,384]{1,0:T(8,128)(2,1)}, u32[]{:S(2)}, u32[]{:S(2)}) collective-permute-start(bf16[864,384]{1,0:T(8,128)(2,1)S(1)} %slice.314), channel_id=1, source_target_pairs={{0,16},{8,24},{16,0},{24,8},{1,17},{9,25},{17,1},{25,9},{2,18},{10... | collective-permute-start | bytes 1990664 | tf_op jit(solution)/shard_map/ppermute | solution.py:28
  345.1 59.6 %collective-permute-start.55 = (bf16[864,768]{1,0:T(8,128)(2,1)}, bf16[864,768]{1,0:T(8,128)(2,1)}, u32[]{:S(2)}, u32[]{:S(2)}) collective-permute-start(bf16[864,768]{1,0:T(8,128)(2,1)} %convolution_convert_fusion), channel_id=1, source_target_pairs={{0,8},{8,0},{16,24},{24,16},{1,9},{9,1},{17,25},{25,17},{2,10},{10... | collective-permute-start | bytes 3981320 | tf_op jit(solution)/shard_map/ppermute | solution.py:28
  373.8 43.3 %collective-permute-start.62 = (bf16[864,384]{1,0:T(8,128)(2,1)S(1)}, bf16[864,384]{1,0:T(8,128)(2,1)S(1)}, u32[]{:S(2)}, u32[]{:S(2)}) collective-permute-start(bf16[864,384]{1,0:T(8,128)(2,1)S(1)} %slice.313), channel_id=1, source_target_pairs={{0,16},{8,24},{16,0},{24,8},{1,17},{9,25},{17,1},{25,9},{2,18},{10... | collective-permute-start | bytes 1990664 | tf_op jit(solution)/shard_map/ppermute | solution.py:28
  374.6 43.0 %collective-permute-start.48 = (bf16[192,1536]{1,0:T(8,128)(2,1)}, bf16[192,1536]{1,0:T(8,128)(2,1)}, u32[]{:S(2)}, u32[]{:S(2)}) collective-permute-start(bf16[192,1536]{1,0:T(8,128)(2,1)} %constant_dynamic-update-slice_fusion.10.refs_0_), channel_id=1, source_target_pairs={{0,4},{1,5},{2,6},{3,7},{4,0},{5,1},{6,2},{7,3},{8,12},{9,13},{10,... | collective-permute-start | bytes 1769480 | tf_op jit(solution)/shard_map/ppermute | solution.py:28
  410.1 30.2 %collective-permute-start.71 = (bf16[864,384]{1,0:T(8,128)(2,1)}, bf16[864,384]{1,0:T(8,128)(2,1)}, u32[]{:S(2)}, u32[]{:S(2)}) collective-permute-start(bf16[864,384]{1,0:T(8,128)(2,1)} %slice.312), channel_id=1, source_target_pairs={{0,16},{8,24},{16,0},{24,8},{1,17},{9,25},{17,1},{25,9},{2,18},{10... | collective-permute-start | bytes 1990664 | tf_op jit(solution)/shard_map/ppermute | solution.py:28
  417.1 34.3 %collective-permute-start.56 = (bf16[192,1536]{1,0:T(8,128)(2,1)}, bf16[192,1536]{1,0:T(8,128)(2,1)}, u32[]{:S(2)}, u32[]{:S(2)}) collective-permute-start(bf16[192,1536]{1,0:T(8,128)(2,1)} %constant_dynamic-update-slice_fusion.10.refs_0_), channel_id=1, source_target_pairs={{0,1},{1,0},{2,3},{3,2},{4,5},{5,4},{6,7},{7,6},{8,9},{9,8},{10,11... | collective-permute-start | bytes 1769480 | tf_op jit(solution)/shard_map/ppermute | solution.py:28
  417.1 36.2 %collective-permute-start.58 = (bf16[192,1536]{1,0:T(8,128)(2,1)}, bf16[192,1536]{1,0:T(8,128)(2,1)}, u32[]{:S(2)}, u32[]{:S(2)}) collective-permute-start(bf16[192,1536]{1,0:T(8,128)(2,1)} %constant_dynamic-update-slice_fusion.12.refs_2_), channel_id=1, source_target_pairs={{0,1},{1,0},{2,3},{3,2},{4,5},{5,4},{6,7},{7,6},{8,9},{9,8},{10,11... | collective-permute-start | bytes 1769480 | tf_op jit(solution)/shard_map/ppermute | solution.py:28
  417.6 35.7 %collective-permute-start.57 = (bf16[192,1536]{1,0:T(8,128)(2,1)}, bf16[192,1536]{1,0:T(8,128)(2,1)}, u32[]{:S(2)}, u32[]{:S(2)}) collective-permute-start(bf16[192,1536]{1,0:T(8,128)(2,1)} %collective-permute-done.48.refs_1_), channel_id=1, source_target_pairs={{0,1},{1,0},{2,3},{3,2},{4,5},{5,4},{6,7},{7,6},{8,9},{9,8},{10,11... | collective-permute-start | bytes 1769480 | tf_op jit(solution)/shard_map/ppermute | solution.py:28
  419.2 34.1 %collective-permute-start.59 = (bf16[192,1536]{1,0:T(8,128)(2,1)}, bf16[192,1536]{1,0:T(8,128)(2,1)}, u32[]{:S(2)}, u32[]{:S(2)}) collective-permute-start(bf16[192,1536]{1,0:T(8,128)(2,1)} %collective-permute-done.50.refs_3_), channel_id=1, source_target_pairs={{0,1},{1,0},{2,3},{3,2},{4,5},{5,4},{6,7},{7,6},{8,9},{9,8},{10,11... | collective-permute-start | bytes 1769480 | tf_op jit(solution)/shard_map/ppermute | solution.py:28
  440.3 39.4 %collective-permute-start.51 = (bf16[192,1536]{1,0:T(8,128)(2,1)}, bf16[192,1536]{1,0:T(8,128)(2,1)}, u32[]{:S(2)}, u32[]{:S(2)}) collective-permute-start(bf16[192,1536]{1,0:T(8,128)(2,1)} %get-tuple-element.170), channel_id=1, source_target_pairs={{0,4},{1,5},{2,6},{3,7},{4,0},{5,1},{6,2},{7,3},{8,12},{9,13},{10,... | collective-permute-start | bytes 1769480 | tf_op jit(solution)/shard_map/ppermute | solution.py:28
  445.2 51.1 %all-to-all-start.5 = ((bf16[8,48,864]{2,1,0:T(8,128)(2,1)}), bf16[8,48,864]{2,1,0:T(8,128)(2,1)S(1)}, u32[]{:S(2)}, u32[]{:S(2)}) async-start(bf16[8,48,864]{2,1,0:T(8,128)(2,1)} %bitcast.140), calls=%async_computation.5 | async-start | bytes 1376256 | tf_op jit(solution)/shard_map/all_to_all | solution.py:542
  451.4 28.3 %collective-permute-start.52 = (bf16[192,1536]{1,0:T(8,128)(2,1)}, bf16[192,1536]{1,0:T(8,128)(2,1)S(1)}, u32[]{:S(2)}, u32[]{:S(2)}) collective-permute-start(bf16[192,1536]{1,0:T(8,128)(2,1)} %copy-done.94), channel_id=1, source_target_pairs={{0,2},{1,3},{2,0},{3,1},{4,6},{5,7},{6,4},{7,5},{8,10},{9,11},{10,... | collective-permute-start | bytes 1769480 | tf_op jit(solution)/shard_map/ppermute | solution.py:28
  485.2 33.6 %collective-permute-start.60 = (bf16[768,1536]{1,0:T(8,128)(2,1)}, bf16[768,1536]{1,0:T(8,128)(2,1)}, u32[]{:S(2)}, u32[]{:S(2)}) collective-permute-start(bf16[768,1536]{1,0:T(8,128)(2,1)} %shard_map.219), channel_id=1, source_target_pairs={{0,1},{1,0},{2,3},{3,2},{4,5},{5,4},{6,7},{7,6},{8,9},{9,8},{10,11... | collective-permute-start | bytes 7077896 | tf_op jit(solution)/shard_map/ppermute | solution.py:28
  526.1 29.5 %collective-permute-start.70 = (bf16[48,1664]{1,0:T(8,128)(2,1)}, bf16[48,1664]{1,0:T(8,128)(2,1)}, u32[]{:S(2)}, u32[]{:S(2)}) collective-permute-start(bf16[48,1664]{1,0:T(8,128)(2,1)} %split.13), channel_id=1, source_target_pairs={{0,16},{8,24},{16,0},{24,8},{1,17},{9,25},{17,1},{25,9},{2,18},{10... | collective-permute-start | bytes 479240 | tf_op jit(solution)/shard_map/ppermute | solution.py:28
  (185 other events, 2129.5 us)

commit v3 on v2

--- a/solution.py
+++ b/solution.py
@@ -79,24 +79,25 @@
                 out[k * rows : (k + 1) * rows, :] = value.astype(out.dtype)
 
 
-def first_fold_kernel(rows, plans, near, came, *refs):
+def first_fold_kernel(rows, plans, near, *refs):
     count = len(plans)
-    sends, keeps = refs[:count], refs[count:]
+    came, sends, keeps = refs[: len(refs) - 2 * count], refs[len(refs) - 2 * count : -count], refs[-count:]
+    per = came[0].shape[0] // rows
     for m, (going, staying) in enumerate(plans):
         for out, places in ((sends[m], going), (keeps[m], staying)):
             for k, place in enumerate(places):
                 at = slice(place * rows, (place + 1) * rows)
-                value = near[at, :] + came[at, :].astype(F32)
+                there = slice(place % per * rows, (place % per + 1) * rows)
+                value = near[at, :] + came[place // per][there, :].astype(F32)
                 out[k * rows : (k + 1) * rows, :] = value.astype(out.dtype)
 
 
-def plane_reduce(near, far, parts, wait=()):
+def plane_reduce(near, came, parts, wait=()):
     n = lax.axis_size("shard")
     half = n // 2
     outer = bits_of(n)[1:]
     width = near.shape[1]
     rows = near.shape[0] // (parts * half)
-    came = swap(far, 1)
     names = gather_names(n, parts)
     kept, arrived = near, came
     for k in reversed(range(len(outer))):
@@ -110,40 +111,38 @@
         shape = (len(plans[0][0]) * rows, width)
         outs = [(shape, BF16)] * parts + [(shape, F32)] * parts
         if kept is near:
-            made = run(functools.partial(first_fold_kernel, rows, plans), outs, [], [near, came])
+            made = run(functools.partial(first_fold_kernel, rows, plans), outs, [], [near, *came])
             sends = [after(send, *wait) for send in made[:parts]]
         else:
             made = run(functools.partial(fold_kernel, rows, plans), outs, [], [*kept, *arrived])
             sends = made[:parts]
+        first = kept is near
         kept = made[parts:]
         arrived = [swap(sends[m], route(outer, m)[k]) for m in range(parts)]
-    return [*kept, *arrived]
-
-
-def line_gather(block, wait=None):
+        if first:
+            first_came = arrived
+    return [*kept, *arrived], first_came
+
+
+def line_gather(block, waits=((), ())):
     n = lax.axis_size("dp")
-    block = after(block, *(wait or ()))
-    ready = None
+    block = after(block, *waits[0])
     for bit in reversed(bits_of(n)):
         came = swap(block, bit, "dp")
-        ready = (came,) if ready is None else ready
         if bit == 1:
-            return block, came, ready
-        block = jnp.concatenate([block, came], axis=1)
-
-
-def line_reduce(keep, send, wait=None):
+            return block, came
+        block = after(jnp.concatenate([block, came], axis=1), *waits[1])
+
+
+def line_reduce(keep, send, wait=()):
     n = lax.axis_size("dp")
-    ready = None
-    send = after(send, *(wait or ()))
     for bit in bits_of(n):
         came = swap(send, bit, "dp")
-        ready = (came,) if ready is None else ready
         if 2 * bit == n:
-            return keep, came, ready
+            return keep, came
         total = keep + came.astype(F32)
-        cut = total.shape[1] // 2
-        keep, send = total[:, :cut], total[:, cut:].astype(BF16)
+        cut = total.shape[0] // 2
+        keep, send = total[:cut], after(total[cut:].astype(BF16), *wait)
 
 
 def reversed_bits(index, n):
@@ -216,11 +215,17 @@
             out[s, at, whole:] = weights[k][:, first : first + rest]
 
 
-def join_kernel(n, whole, rest, came, weight, grad, dots):
-    grad[:, n * whole :] = jnp.concatenate([came[s, :, whole:] for s in range(n)], axis=1).astype(F32)
-    for s in range(n):
-        grad[:, s * whole : (s + 1) * whole] = came[s, :, :whole].astype(F32)
-    dots[...] = jnp.sum(grad[...] * weight[...].astype(F32), axis=1, keepdims=True)
+def join_kernel(n, whole, rest, count, came, *refs):
+    weights, outs = refs[:count], refs[count:]
+    share = whole + rest
+    for k in range(count):
+        grad, dots = outs[2 * k : 2 * k + 2]
+        first = k * share
+        tails = [came[s, :, first + whole : first + share] for s in range(n)]
+        grad[:, n * whole :] = jnp.concatenate(tails, axis=1).astype(F32)
+        for s in range(n):
+            grad[:, s * whole : (s + 1) * whole] = came[s, :, first : first + whole].astype(F32)
+        dots[...] = jnp.sum(grad[...] * weights[k][...].astype(F32), axis=1, keepdims=True)
 
 
 def join_in_kernel(n, groups, came, weight, grad, dots):
@@ -238,15 +243,14 @@
     return [pieces[reversed_bits(p, n)] for p in range(n)]
 
 
-def out_kernel(n, z, first, second, left, right, tap_cols):
+def out_kernel(n, z, first, second, full, tap_cols):
     rows = first.shape[0] // (n // 2)
-    cut = left.shape[1]
+    width = full.shape[1]
     pieces = [(first, second)[p // (n // 2)][p % (n // 2) * rows : (p % (n // 2) + 1) * rows, :] for p in range(n)]
     for p, piece in enumerate(by_line(pieces, z[0], n)):
         at = slice(p * rows, (p + 1) * rows)
-        left[at, :] = piece[:, :cut]
-        right[at, :] = piece[:, cut : 2 * cut]
-        tap_cols[at, :] = piece[:, 2 * cut :]
+        full[at, :] = piece[:, :width]
+        tap_cols[at, :] = piece[:, width:]
 
 
 def relative_kernel(n, z, term, conv_term, keep, send):
@@ -263,13 +267,37 @@
             out[at, lanes] = pieces[p].astype(out.dtype)
 
 
-def side_kernel(count, *refs):
-    pieces, (left, right) = refs[:count], refs[count:]
+def stack_kernel(count, *refs):
+    pieces, out = refs[:count], refs[count]
     rows = pieces[0].shape[0]
-    cut = left.shape[1]
     for k in range(count):
-        left[k * rows : (k + 1) * rows, :] = pieces[k][:, :cut]
-        right[k * rows : (k + 1) * rows, :] = pieces[k][:, cut:]
+        out[k * rows : (k + 1) * rows, :] = pieces[k][...]
+
+
+def product_kernel(former, latter, out):
+    out[...] = mm(former[...], latter[...]).astype(out.dtype)
+
+
+def product(former, latter, blocks):
+    rows = former.shape[0] // blocks
+    return pl.pallas_call(
+        product_kernel,
+        out_shape=jax.ShapeDtypeStruct((former.shape[0], latter.shape[1]), BF16),
+        grid=(blocks,),
+        in_specs=[
+            pl.BlockSpec((rows, former.shape[1]), lambda i: (i, 0)),
+            pl.BlockSpec(latter.shape, lambda i: (0, 0)),
+        ],
+        out_specs=pl.BlockSpec((rows, latter.shape[1]), lambda i: (i, 0)),
+        compiler_params=pltpu.CompilerParams(vmem_limit_bytes=48 * 2**20),
+        cost_estimate=pl.CostEstimate(flops=1000, bytes_accessed=1000, transcendentals=0),
+    )(former, latter)
+
+
+def columns_kernel(chunk, rows, out):
+    for k in range(rows.shape[1] // chunk):
+        at = slice(k * chunk, (k + 1) * chunk)
+        out[at, :] = rows[:, at].astype(F32).T.astype(BF16)
 
 
 def project_kernel(channels, count, *refs):
@@ -349,7 +377,7 @@
     hidden[...] = value
     unit = value * lax.rsqrt(jnp.mean(value * value, axis=1, keepdims=True) + EPS)
     unit_out[...] = unit
-    lean = exchange(unit * gain[...], z[0], n_dp, False).astype(BF16)
+    lean = (unit * gain[...]).astype(BF16)
     rows = parts[0].shape[0]
     for m in range(batches):
         parts[m][...] = lean[m * rows : (m + 1) * rows]
@@ -357,18 +385,16 @@
 
 def gate_kernel(count, *refs):
     pieces = refs[:count]
-    gate_a, gate_b, up_a, up_b, lean_a, lean_b, inner, by_gate, by_up = refs[count:]
+    two, lean, inner, by_gate, by_up = refs[count:]
     rows = pieces[0].shape[0]
-    split = gate_a.shape[1]
+    share = two.shape[0] // 2
     for k in range(0, count, 2):
         at = slice(k * rows, (k + 2) * rows)
         for j in range(2):
-            here = slice((k + j) * rows, (k + j + 1) * rows)
-            lean_a[here, :] = pieces[k + j][:, :split]
-            lean_b[here, :] = pieces[k + j][:, split:]
-        left, right = lean_a[at, :], lean_b[at, :]
-        gate = mt(left, gate_a[...]) + mt(right, gate_b[...])
-        up = mt(left, up_a[...]) + mt(right, up_b[...])
+            lean[(k + j) * rows : (k + j + 1) * rows, :] = pieces[k + j][...]
+        part = lean[at, :]
+        gate = mt(part, two[:share, :])
+        up = mt(part, two[share:, :])
         sig = jax.nn.sigmoid(gate)
         silu = gate * sig
         inner[at, :] = (silu * up).astype(BF16)
@@ -376,51 +402,74 @@
         by_up[at, :] = silu.astype(BF16)
 
 
-def inner_kernel(chunk, cot_a, cot_b, down_a, down_b, by_gate, by_up, d_gate, d_up):
-    for k in range(cot_a.shape[0] // chunk):
+def inner_kernel(chunk, cot, down, by_gate, by_up, *refs):
+    d_two = refs[-1]
+    share = by_gate.shape[1]
+    for k in range(cot.shape[0] // chunk):
         at = slice(k * chunk, (k + 1) * chunk)
-        d_inner = mt(cot_a[at, :], down_a[...]) + mt(cot_b[at, :], down_b[...])
-        d_gate[at, :] = (d_inner * by_gate[at, :].astype(F32)).astype(BF16)
-        d_up[at, :] = (d_inner * by_up[at, :].astype(F32)).astype(BF16)
-
-
-def rows_kernel(pairs, chunk, *refs):
-    out = refs[-1]
-    for k in range(out.shape[0] // chunk):
-        at = slice(k * chunk, (k + 1) * chunk)
-        for j in range(2):
-            split = refs[1 + j].shape[1]
-            value = mm(refs[0][at, :], refs[1 + j][...])
-            for pair in range(1, pairs):
-                value += mm(refs[3 * pair][at, :], refs[3 * pair + 1 + j][...])
-            out[at, j * split : (j + 1) * split] = value.astype(out.dtype)
-
-
-def half_rows(pairs, part, dtype, chunk):
-    total = pairs[0][0].shape[0]
-    width = 2 * pairs[0][1].shape[1]
-    specs, arrays = [], []
-    for lhs, left, right in pairs:
-        specs.append(pl.BlockSpec((total // 2, lhs.shape[1]), lambda i: (part, 0)))
-        specs += [pl.BlockSpec(left.shape, lambda i: (0, 0)), pl.BlockSpec(right.shape, lambda i: (0, 0))]
-        arrays += [lhs, left, right]
+        d_inner = mt(cot[at, :], down[...])
+        d_two[at, :share] = (d_inner * by_gate[at, :].astype(F32)).astype(BF16)
+        d_two[at, share:] = (d_inner * by_up[at, :].astype(F32)).astype(BF16)
+
+
+def inner_half(part, chunk, cot, down, by_gate, by_up, other=None):
+    total, share = by_gate.shape
+
+    def rows_of(width):
+        return pl.BlockSpec((total // 2, width), lambda i: (part, 0))
+
+    extra = [] if other is None else [other]
     return pl.pallas_call(
-        functools.partial(rows_kernel, len(pairs), chunk),
-        out_shape=jax.ShapeDtypeStruct((total // 2, width), dtype),
+        functools.partial(inner_kernel, chunk),
+        out_shape=jax.ShapeDtypeStruct((total, 2 * share), BF16),
         grid=(1,),
-        in_specs=specs,
-        out_specs=pl.BlockSpec((total // 2, width), lambda i: (0, 0)),
+        in_specs=[rows_of(cot.shape[1]), pl.BlockSpec(down.shape, lambda i: (0, 0)), rows_of(share), rows_of(share)]
+        + [pl.BlockSpec(memory_space=pl.ANY)] * len(extra),
+        out_specs=rows_of(2 * share),
+        input_output_aliases={4: 0} if extra else {},
         compiler_params=pltpu.CompilerParams(vmem_limit_bytes=48 * 2**20),
         cost_estimate=pl.CostEstimate(flops=1000, bytes_accessed=1000, transcendentals=0),
-    )(*arrays)
-
-
-def branch_kernel(batches, n_dp, z, cot, hidden, unit, gain, *refs):
+    )(cot, down, by_gate, by_up, *extra)
+
+
+def rows_kernel(*refs, sides):
+    lhs, rhs, outs = refs[0], refs[1 : 1 + sides], refs[1 + sides :]
+    rows = outs[0].shape[0]
+    per = max(1, 384 // rows)
+    step = min(rows, 384)
+    for k in range(0, len(outs), per):
+        count = min(per, len(outs) - k)
+        for first in range(0, rows, step):
+            at = slice(k * rows + first, k * rows + first + step * count)
+            for j in range(sides):
+                split = rhs[j].shape[1]
+                value = mm(lhs[at, :], rhs[j][...])
+                for piece in range(count):
+                    here = value[piece * step : (piece + 1) * step]
+                    outs[k + piece][first : first + step, j * split : (j + 1) * split] = here.astype(outs[0].dtype)
+
+
+def half_rows(lhs, rhs, part, dtype, pieces):
+    rows = lhs.shape[0] // 2
+    width = sum(side.shape[1] for side in rhs)
+    shape = (rows // pieces, width)
+    return pl.pallas_call(
+        functools.partial(rows_kernel, sides=len(rhs)),
+        out_shape=[jax.ShapeDtypeStruct(shape, dtype)] * pieces,
+        grid=(1,),
+        in_specs=[pl.BlockSpec((rows, lhs.shape[1]), lambda i: (part, 0))]
+        + [pl.BlockSpec(side.shape, lambda i: (0, 0)) for side in rhs],
+        out_specs=[pl.BlockSpec(shape, lambda i: (0, 0))] * pieces,
+        compiler_params=pltpu.CompilerParams(vmem_limit_bytes=48 * 2**20),
+        cost_estimate=pl.CostEstimate(flops=1000, bytes_accessed=1000, transcendentals=0),
+    )(lhs, *rhs)
+
+
+def branch_kernel(batches, cot, hidden, unit, gain, *refs):
     terms, parts = refs[: 2 * batches], refs[2 * batches :]
-    back = exchange(summed(batches, terms), z[0], n_dp, True)
     value = hidden[...]
     inv = lax.rsqrt(jnp.mean(value * value, axis=1, keepdims=True) + EPS)
-    scaled = back * gain[...]
+    scaled = summed(batches, terms) * gain[...]
     one = unit[...]
     mean = jnp.mean(scaled * one, axis=1, keepdims=True)
     lean = (cot[...].astype(F32) + inv * (scaled - one * mean)).astype(BF16)
@@ -431,13 +480,13 @@
 
 def conv_back_kernel(batches, n, count, me, *refs):
     pieces = refs[:count]
-    out_a, out_b, conv, c_nat, p_nat, b_arr, x_arr, source, offset, slot, taps = refs[count : count + 11]
-    branch, d_b, d_c, d_x, conv_grad, own, natural = refs[count + 11 :]
+    out_ref, conv, c_nat, p_nat, b_arr, x_arr, source, offset, slot, taps = refs[count : count + 10]
+    branch, d_proj, conv_grad, own, natural = refs[count + 10 :]
+    channels = taps.shape[1]
     total = branch.shape[0]
     group = total // batches
     half = group // 2
     rows = group // n
-    cut = out_a.shape[1]
     names = gather_names(n, batches)
     for k in range(count):
         size = pieces[k].shape[0]
@@ -446,7 +495,7 @@
         for m in range(batches):
             k = c * batches + m
             at = slice(k * half, (k + 1) * half)
-            gated = mt(branch[at, :cut], out_a[...]) + mt(branch[at, cut:], out_b[...])
+            gated = mt(branch[at, :], out_ref[...])
             for j, e in enumerate(names[m]):
                 other = me[0] ^ (2 * e + c)
                 at = m * group + other * rows
@@ -475,9 +524,9 @@
         for c in range(2):
             there = pl.ds((c * batches + m) * half, half)
             piece = d_prod[c * half : (c + 1) * half]
-            d_b[there, :] = (piece * x_arr[there, :]).astype(BF16)
-            d_c[there, :] = c_back[c * half : (c + 1) * half].astype(BF16)
-            d_x[there, :] = (piece * b_arr[there, :]).astype(BF16)
+            d_proj[there, :channels] = (piece * x_arr[there, :]).astype(BF16)
+            d_proj[there, channels : 2 * channels] = c_back[c * half : (c + 1) * half].astype(BF16)
+            d_proj[there, 2 * channels :] = (piece * b_arr[there, :]).astype(BF16)
     for k in range(3):
         conv_grad[k : k + 1, :] = totals[k]
     lanes = lax.broadcasted_iota(jnp.int32, (slot.shape[0], total), 1)
@@ -496,9 +545,9 @@
     out[...] = (d_hidden[...].astype(F32) + inv * (scaled - unit * mean)).astype(BF16)
 
 
-def block_kernel(batches, n_dp, z, hidden, *refs):
+def block_kernel(batches, hidden, *refs):
     terms, out = refs[:-1], refs[-1]
-    out[...] = (hidden[...] + exchange(summed(batches, terms), z[0], n_dp, True)).astype(BF16)
+    out[...] = (hidden[...] + summed(batches, terms)).astype(BF16)
 
 
 def body(
@@ -552,18 +601,19 @@
     extra = jnp.concatenate([norm_gain[:, None], ff_gain[:, None], table], axis=1)
     in_parts = jnp.concatenate([in_parts, jnp.broadcast_to(extra[None], (n,) + extra.shape)], axis=2)
     in_came = dealt(in_parts)
-    tok_turned = turned(tokens_in, z, n_dp)
+    tok_turned = turned(after(tokens_in, in_parts), z, n_dp)
     tok_pieces, tok_steps = plane_gather([tok_turned[m] for m in range(batches)])
     out_aug = jnp.concatenate(
         [out_weight, conv_weight, jnp.zeros((own_rows, LANES - conv_weight.shape[1]), BF16)], axis=1
     )
     out_lines = out_aug
+    out_steps = []
     for bit in reversed(bits_of(n_dp)):
         out_came = swap(out_lines, bit, "dp")
+        out_steps.append(out_came)
         if bit > 1:
             out_lines = jnp.concatenate([out_lines, out_came], axis=0)
 
-    in_a, in_b, ready = line_gather(flipped(in_came))
     weights = [gate_weight, up_weight, down_weight]
     [ff_parts] = run(
         functools.partial(spread_kernel, n, whole, rest, 3),
@@ -571,16 +621,59 @@
         [],
         weights,
     )
-    ff_came = dealt(after(ff_parts, in_came))
-    gate_block, up_block, down_block = [
-        flipped(ff_came[:, k * own_rows : (k + 1) * own_rows]) for k in range(3)
-    ]
-    gate_a, gate_b, ready = line_gather(gate_block, ready)
-    gate_high = ready
-    up_a, up_b, ready = line_gather(up_block, ready)
-    up_high = ready
-    down_a, down_b, ready = line_gather(down_block, ready)
-    down_high = ready
+    ff_came = dealt(after(ff_parts, in_came, *tok_steps[0], out_steps[0]))
+    out_full, tap_cols = run(
+        functools.partial(out_kernel, n_dp),
+        [((channels, width), BF16), ((channels, LANES), BF16)],
+        [z],
+        [out_lines, out_came],
+    )
+    taps = tap_cols[:, : conv_weight.shape[1]].astype(F32).T
+
+    deal = in_came[:, :, 3 * channels + 2 :].reshape(n, own_rows * spare)[:, : batches * n]
+    deal = deal.reshape(n, batches, n).transpose(1, 0, 2).astype(jnp.int32)
+    m_index = jnp.arange(batches, dtype=jnp.int32)[:, None, None, None]
+    j_index = jnp.arange(n, dtype=jnp.int32)[None, :, None, None]
+    t_index = jnp.arange(piece_rows, dtype=jnp.int32)[None, None, None, :]
+
+    def place_of(e, m):
+        out = jnp.zeros_like(e + m)
+        for part in range(batches):
+            for k, name in enumerate(names[part]):
+                out = jnp.where((e == name) & (m == part), k, out)
+        return out
+
+    def within(m, holder, row):
+        rel = holder ^ me
+        return ((rel & 1) * half + place_of(rel >> 1, m)) * rows_dev + row
+
+    def arrival_row(m, holder, row):
+        rel = holder ^ me
+        return (((rel & 1) * batches + m) * half + place_of(rel >> 1, m)) * rows_dev + row
+
+    slot_row = j_index * piece_rows + t_index
+    source = within(m_index, deal[:, :, :, None], slot_row).reshape(batches, group)
+    own_deal = lax.dynamic_index_in_dim(deal, me, 1, keepdims=True)[:, :, :, None]
+    own_source = arrival_row(m_index, own_deal, me * piece_rows + t_index).reshape(own_total, 1)
+    inverse = jnp.sum(jnp.where(deal == me, jnp.arange(n, dtype=jnp.int32)[None, None, :], 0), axis=2)
+    slot_source = arrival_row(
+        m_index[:, :, 0], j_index[:, :, 0], inverse[:, :, None] * piece_rows + t_index[:, 0]
+    ).reshape(own_total, 1)
+
+    lengths = seq_lengths[:, 0, :]
+    places = jnp.arange(group, dtype=jnp.int32)
+    seq_start = jnp.zeros((batches, group), jnp.int32)
+    start = jnp.zeros((batches,), jnp.int32)
+    for k in range(lengths.shape[1]):
+        seq_start = jnp.where(start[:, None] <= places[None, :], start[:, None], seq_start)
+        start = start + lengths[:, k]
+    offset = (places[None, :] - seq_start)[:, :, None]
+
+    waits = (*tok_pieces, out_full, taps, source, own_source, slot_source, offset)
+    in_a, in_b = line_gather(flipped(in_came), ((), waits))
+    gate_block, up_block = [flipped(ff_came[:, k * own_rows : (k + 1) * own_rows]) for k in range(2)]
+    two_block = after(jnp.concatenate([gate_block, up_block], axis=0), in_b)
+    two = lax.all_gather(two_block, "dp", axis=1, tiled=True)
 
     def natural_row(row):
         both = jnp.concatenate([in_a[row : row + 1], in_b[row : row + 1]], axis=1)
@@ -594,58 +687,11 @@
 
     gain_one = natural_row(3 * channels)
     gain_two = natural_row(3 * channels + 1)
-    out_a, out_b, tap_cols = run(
-        functools.partial(out_kernel, n_dp),
-        [((channels, cut), BF16), ((channels, cut), BF16), ((channels, LANES), BF16)],
-        [z],
-        [out_lines, out_came],
-    )
-    taps = tap_cols[:, : conv_weight.shape[1]].astype(F32).T
-
-    deal = in_came[:, :, 3 * channels + 2 :].reshape(n, own_rows * spare)[:, : batches * n]
-    deal = deal.reshape(n, batches, n).transpose(1, 0, 2).astype(jnp.int32)
-    m_index = jnp.arange(batches, dtype=jnp.int32)[:, None, None, None]
-    j_index = jnp.arange(n, dtype=jnp.int32)[None, :, None, None]
-    t_index = jnp.arange(piece_rows, dtype=jnp.int32)[None, None, None, :]
-
-    def place_of(e, m):
-        out = jnp.zeros_like(e + m)
-        for part in range(batches):
-            for k, name in enumerate(names[part]):
-                out = jnp.where((e == name) & (m == part), k, out)
-        return out
-
-    def within(m, holder, row):
-        rel = holder ^ me
-        return ((rel & 1) * half + place_of(rel >> 1, m)) * rows_dev + row
-
-    def arrival_row(m, holder, row):
-        rel = holder ^ me
-        return (((rel & 1) * batches + m) * half + place_of(rel >> 1, m)) * rows_dev + row
-
-    slot_row = j_index * piece_rows + t_index
-    source = within(m_index, deal[:, :, :, None], slot_row).reshape(batches, group)
-    own_deal = lax.dynamic_index_in_dim(deal, me, 1, keepdims=True)[:, :, :, None]
-    own_source = arrival_row(m_index, own_deal, me * piece_rows + t_index).reshape(own_total, 1)
-    inverse = jnp.sum(jnp.where(deal == me, jnp.arange(n, dtype=jnp.int32)[None, None, :], 0), axis=2)
-    slot_source = arrival_row(
-        m_index[:, :, 0], j_index[:, :, 0], inverse[:, :, None] * piece_rows + t_index[:, 0]
-    ).reshape(own_total, 1)
-
-    lengths = seq_lengths[:, 0, :]
-    places = jnp.arange(group, dtype=jnp.int32)
-    seq_start = jnp.zeros((batches, group), jnp.int32)
-    start = jnp.zeros((batches,), jnp.int32)
-    for k in range(lengths.shape[1]):
-        seq_start = jnp.where(start[:, None] <= places[None, :], start[:, None], seq_start)
-        start = start + lengths[:, k]
-    offset = (places[None, :] - seq_start)[:, :, None]
-
     arr = (total, channels)
     nat = (batches, group, channels)
     own = (own_total, width)
     side = (total, cut)
-    normed_a, normed_b, product, c_high, c_low, b_arr, x_arr, own_tok = run(
+    normed_a, normed_b, made, c_high, c_low, b_arr, x_arr, own_tok = run(
         functools.partial(project_kernel, channels, len(tok_pieces)),
         [(side, BF16), (side, BF16), (arr, BF16), (arr, BF16), (arr, BF16), (arr, F32), (arr, F32), (own, BF16)],
         [],
@@ -656,80 +702,72 @@
         functools.partial(conv_kernel, batches, n),
         [(nat, BF16), (nat, F32), (nat, F32), (arr, BF16)],
         [me],
-        [product, c_high, c_low, source[:, :, None], offset, taps],
+        [made, c_high, c_low, source[:, :, None], offset, taps],
         [pltpu.VMEM((group, channels), F32)],
     )
-    cot_turned = turned(cotangent, z, n_dp)
-    cot_pieces, cot_steps = plane_gather([cot_turned[m] for m in range(batches)], ((ff_came, *tok_steps[-1]), ()))
-
-    def summed_rows(*pairs, wait=()):
-        far = half_rows(pairs, 1, BF16, chunk)
-        near = half_rows(pairs, 0, F32, chunk)
-        return plane_reduce(near, far, batches, wait)
+    down_block = flipped(after(ff_came, gated_arr)[:, 2 * own_rows :])
+    down = lax.all_gather(down_block, "dp", axis=1, tiled=True)
+    cot_pieces, cot_steps = plane_gather([cotangent[m] for m in range(batches)], ((ff_came, *tok_steps[-1]), ()))
+
+    def summed_rows(lhs, rhs, wait=()):
+        far = half_rows(lhs, rhs, 1, BF16, 2 * batches)
+        [near] = half_rows(lhs, rhs, 0, F32, 1)
+        return plane_reduce(near, [swap(piece, 1) for piece in far], batches, wait)[0]
 
     mine = ((rows_dev, width), BF16)
     hidden, unit_two, *ff_own = run(
         functools.partial(hidden_kernel, batches, n_dp),
         [(own, F32), (own, F32)] + [mine] * batches,
         [z],
-        [own_tok, gain_two, *summed_rows((gated_arr, out_a, out_b), wait=(*gate_high, *cot_steps[-1]))],
-    )
-    ff_pieces, ff_steps = plane_gather(ff_own, ((), (gate_b, *up_high)))
-    cot_a, cot_b = run(
-        functools.partial(side_kernel, len(cot_pieces)), [(side, BF16), (side, BF16)], [], cot_pieces
-    )
+        [own_tok, gain_two, *summed_rows(gated_arr, [out_full], cot_steps[-1])],
+    )
+    ff_pieces, ff_steps = plane_gather(ff_own)
+    whole_rows = ((total, width), BF16)
+    [cot_all] = run(functools.partial(stack_kernel, len(cot_pieces)), [whole_rows], [], cot_pieces)
 
     ff = (total, share)
-    ff_pieces[0] = after(ff_pieces[0], *down_high)
-    lean_a, lean_b, ff_inner, by_gate, by_up = run(
+    lean, ff_inner, by_gate, by_up = run(
         functools.partial(gate_kernel, len(ff_pieces)),
-        [(side, BF16), (side, BF16), (ff, BF16), (ff, BF16), (ff, BF16)],
+        [whole_rows, (ff, BF16), (ff, BF16), (ff, BF16)],
         [],
-        [*ff_pieces, gate_a, gate_b, up_a, up_b],
-    )
-
-    def outer_sum(former, left, right, wait=None):
-        send = dot(former, right, ((0,), (0,)), BF16)
-        keep = dot(former, left, ((0,), (0,)))
-        return line_reduce(keep, send, wait)
-
-    def returned(terms, *wait):
-        value = (terms[0] + terms[1].astype(F32)).astype(BF16)
-        rows = dot(identity, value, ((1,), (1,)), BF16)
-        return dealt(after(rows.reshape(n, own_rows, -1), *wait))
-
-    *down_sum, down_low = outer_sum(ff_inner, cot_a, cot_b)
-    d_gate, d_up = run(
-        functools.partial(inner_kernel, chunk),
-        [(ff, BF16), (ff, BF16)],
-        [],
-        [cot_a, cot_b, down_a, down_b, by_gate, by_up],
-    )
-    d_ff = summed_rows((d_gate, gate_a, gate_b), (d_up, up_a, up_b), wait=down_low)
-    *gate_sum, gate_low = outer_sum(d_gate, lean_a, lean_b, down_low)
-    *up_sum, up_low = outer_sum(d_up, lean_a, lean_b, gate_low)
+        [*ff_pieces, two],
+    )
+
+    def line_sum(former, latter, wait=()):
+        value = after(product(former, latter, 4), *wait)
+        return lax.psum_scatter(value, "dp", scatter_dimension=0, tiled=True)
+
+    turn = functools.partial(columns_kernel, width // 6)
+    [cot_columns] = run(turn, [((width, total), BF16)], [], [cot_all])
+    [lean_columns] = run(turn, [((width, total), BF16)], [], [lean])
+    down_sum = line_sum(cot_columns, ff_inner)
+    d_far = inner_half(1, chunk, cot_all, down, by_gate, by_up)
+    far = half_rows(d_far, [two], 1, BF16, 2 * batches)
+    came = [swap(piece, 1) for piece in far]
+    d_two = inner_half(0, chunk, after(cot_all, *far), down, by_gate, by_up, d_far)
+    [near] = half_rows(after(d_two, *came), [two], 0, F32, 1)
+    d_ff, first_came = plane_reduce(near, came, batches)
+    two_sum = line_sum(lean_columns, d_two, first_came)
     cot_own = cotangent.reshape(own)
     branch_own = run(
-        functools.partial(branch_kernel, batches, n_dp),
+        functools.partial(branch_kernel, batches),
         [mine] * batches,
-        [z],
+        [],
         [cot_own, hidden, unit_two, gain_two, *d_ff],
     )
-    branch_pieces, branch_steps = plane_gather(branch_own, (gate_low, ()))
-    block_sum = summed_rows((ff_inner, down_a, down_b), wait=branch_steps[-1])
-    [block_out] = run(functools.partial(block_kernel, batches, n_dp), [(own, BF16)], [z], [hidden, *block_sum])
-    block_out = block_out.reshape(tokens_in.shape)
-    down_back = returned(down_sum, *branch_steps[-1])
-
-    branch_pieces[0] = after(branch_pieces[0], *up_low)
-    branch, *d_proj, conv_term, d_hidden_own = run(
+    branch_pieces, branch_steps = plane_gather(branch_own)
+
+    block_came = [swap(piece, 1) for piece in half_rows(ff_inner, [down], 1, BF16, 2 * batches)]
+    [block_near] = half_rows(ff_inner, [down], 0, F32, 1)
+    branch_pieces[0] = after(branch_pieces[0], block_near, *block_came)
+
+    branch, d_proj, conv_term, d_hidden_own = run(
         functools.partial(conv_back_kernel, batches, n, len(branch_pieces)),
-        [((total, width), BF16), (arr, BF16), (arr, BF16), (arr, BF16), ((3, channels), F32), (own, BF16)],
+        [whole_rows, ((total, 3 * channels), BF16), ((3, channels), F32), (own, BF16)],
         [me],
         [
             *branch_pieces,
-            out_a,
-            out_b,
+            out_full,
             conv_out,
             c_nat,
             p_nat,
@@ -742,11 +780,12 @@
         ],
         [pltpu.VMEM((total, channels), F32)],
     )
-    rows_of = [slice(k * channels, (k + 1) * channels) for k in range(3)]
-    gate_back = returned(gate_sum, down_back)
-    d_normed = summed_rows(
-        *[(d_proj[k], in_a[rows_of[k]], in_b[rows_of[k]]) for k in range(3)], wait=(down_back, gate_back)
-    )
+    in_sides = [in_a[: 3 * channels], in_b[: 3 * channels]]
+    down_back = dealt(down_sum.reshape(n, own_rows, -1))
+    d_normed = summed_rows(d_proj, in_sides, (down_back,))
+    block_sum, _ = plane_reduce(block_near, block_came, batches, d_normed[batches:])
+    [block_out] = run(functools.partial(block_kernel, batches), [(own, BF16)], [], [hidden, *block_sum])
+    block_out = block_out.reshape(tokens_in.shape)
     [tokens_grad] = run(
         functools.partial(final_kernel, batches, n_dp),
         [(own, BF16)],
@@ -755,10 +794,6 @@
     )
     tokens_grad = tokens_grad.reshape(tokens_in.shape)
 
-    in_send = jnp.concatenate([dot(d_proj[k], normed_b, ((0,), (0,)), BF16) for k in range(3)], axis=0)
-    in_keep = jnp.concatenate([dot(d_proj[k], normed_a, ((0,), (0,))) for k in range(3)], axis=0)
-    *in_sum, in_low = line_reduce(in_keep, in_send, up_low)
-    up_back = returned(up_sum)
     conv_cols = jnp.pad(conv_term.T, ((0, 0), (0, LANES - conv_term.shape[0])))
     keep, send = run(
         functools.partial(relative_kernel, n_dp),
@@ -766,25 +801,29 @@
         [z],
         [dot(gated_arr, branch, ((0,), (0,))), conv_cols],
     )
-    send = after(send, *in_low)
+    out_came = []
     for bit in bits_of(n_dp):
-        came = swap(send, bit, "dp").astype(F32)
-        keep = keep + came
+        came = swap(send, bit, "dp")
+        out_came.append(came)
+        keep = keep + came.astype(F32)
         if 2 * bit < n_dp:
             keep, send = jnp.split(keep, 2, axis=0)
-            send = send.astype(BF16)
+            send = after(send.astype(BF16), *d_normed[batches:])
+    in_sum = line_reduce(dot(normed_a, d_proj, ((0,), (0,))), dot(normed_b, d_proj, ((0,), (0,)), BF16), (*d_normed[batches:], out_came[0]))
     out_grad = keep[:, :width]
     conv_grad = keep[:, width : width + conv_weight.shape[1]]
-    in_back = returned(in_sum)
-
-    def joined(kernel, came, weight):
-        shape = weight.shape
-        return run(kernel, [(shape, F32), ((own_rows, 1), F32)], [], [came, weight])
+    two_back = dealt(two_sum.reshape(n, own_rows, -1))
+    in_total = (in_sum[0] + in_sum[1].astype(F32)).astype(BF16).reshape(n, own_rows, -1)
+    in_back = dealt(after(in_total, two_back))
+
+    def joined(kernel, came, *weights):
+        outs = [((own_rows, 1), F32)] * (2 * len(weights))
+        outs[::2] = [(weight.shape, F32) for weight in weights]
+        return run(kernel, outs, [], [came, *weights])
 
     join = functools.partial(join_kernel, n, whole, rest)
-    down_grad, _ = joined(join, down_back, down_weight)
-    gate_grad, gate_dots = joined(join, gate_back, gate_weight)
-    up_grad, up_dots = joined(join, up_back, up_weight)
+    down_grad, _ = joined(functools.partial(join, 1), down_back, down_weight)
+    gate_grad, gate_dots, up_grad, up_dots = joined(functools.partial(join, 2), two_back, gate_weight, up_weight)
     in_grad, in_dots = joined(functools.partial(join_in_kernel, n, 3 * n_dp), in_back, in_weight)
     norm_gain_grad = in_dots[:, 0] / norm_gain.astype(F32)
     ff_gain_grad = (gate_dots + up_dots)[:, 0] / ff_gain.astype(F32)

time: 574 us -> 504 us (0.88)
  waiting for transfers between devices: 208 us -> 136 us
  matrix products: 50.7 us -> 16.3 us
  Pallas kernels: 131 us -> 152 us
  between operations: 2.69 us -> 15.2 us
  local copies, waits for them, and re-layouts: 70.5 us -> 80.2 us
  other arithmetic: 20.6 us -> 13.6 us
    ppermute x72, waiting for transfers between devices: 204 us -> 112 us  [swap(): return lax.ppermute(value, axis, [(i, i ^ bit) for i in range(n)])]
    dot_general x21 -> x7, matrix products: 50.7 us -> 16.3 us  [dot(): lax.dot_general(former, latter, ((dims[0], dims[1]), ((), ())), preferred...]
    pallas_call x8 -> x12, Pallas kernels: 40.2 us -> 68.8 us  [the longest x8 34.7 us: half_rows(): pl.pallas_call(functools.partial(rows_kernel, sides=len(rhs)), out_shape=...]
    unnamed x283 -> x210, local copies, waits for them, and re-layouts: 41.9 us -> 56.4 us
    all_gather x0 -> x2, waiting for transfers between devices: none -> 14.3 us  [the longest x1 14.3 us: body(): down = lax.all_gather(down_block, 'dp', axis=1, tiled=True)]
    pallas_call x25, Pallas kernels: 90.7 us -> 83 us  [run(): pl.pallas_call(kernel, out_shape=[jax.ShapeDtypeStruct(shape, dtype) for...]
    reduce_scatter x0 -> x2, waiting for transfers between devices: none -> 7.46 us  [line_sum(): return lax.psum_scatter(value, 'dp', scatter_dimension=0, tiled=True)]
    all_to_all x6 -> x5, starting transfers between devices: 24.3 us -> 22 us  [dealt(): lax.all_to_all(blocks, 'shard', split_axis=0, concat_axis=0, tiled=True)]
  transfers between devices with their start and end apart: 78 -> 81, of which waited for: 25 -> 26; matrix products, arithmetic and copies ran while one was open for 18% -> 11% of each run, Pallas kernels for 19% -> 30%
where the time goes in v3:
time: 504 us; the launch traced here: 496 us
  Pallas kernels  152 us (30%)
  waiting for transfers between devices  136 us (27%)
  starting transfers between devices  82.8 us (16%)
  local copies, waits for them, and re-layouts  80.2 us (16%)
  matrix products  16.3 us (3%)
  between operations  15.2 us (3%)
  other arithmetic  13.6 us (3%)
    ppermute x72, waiting for transfers between devices, swap(): return lax.ppermute(value, axis, [(i, i ^ bit) for i in range(n)])  112 us
    pallas_call x25, Pallas kernels, run(): pl.pallas_call(kernel, out_shape=[jax.ShapeDtypeStruct(shape, dtype) for...  83 us
    ppermute x72, starting transfers between devices, swap(): return lax.ppermute(value, axis, [(i, i ^ bit) for i in range(n)])  60.3 us
    unnamed x210, local copies, waits for them, and re-layouts  56.4 us
    pallas_call x8, Pallas kernels, half_rows(): pl.pallas_call(functools.partial(rows_kernel, sides=len(rhs)), out_shape=...  34.7 us
    all_to_all x5, starting transfers between devices, dealt(): lax.all_to_all(blocks, 'shard', split_axis=0, concat_axis=0, tiled=True)  22 us
    pallas_call x2, Pallas kernels, product(): pl.pallas_call(product_kernel, out_shape=jax.ShapeDtypeStruct((former.sha...  21 us
    dot_general x7, matrix products, dot(): lax.dot_general(former, latter, ((dims[0], dims[1]), ((), ())), preferred...  16.3 us
  transfers between devices with their start and end apart: 81, of which 26 were waited for; matrix products, arithmetic and copies ran while one was open for 11% of the time, Pallas kernels for 30%

profile of v3, /device:TPU:0, one launch (start us, length us, event | category | flops | bytes accessed | tf_op | source)
XLA Modules:
  0.0 495.6 jit_solution(15824802349664359255)
XLA Ops:
  12.6 5.3 %all-to-all-start = ((bf16[8,48,592]{2,1,0:T(8,128)(2,1)}), bf16[8,48,592]{2,1,0:T(8,128)(2,1)}, u32[]{:S(2)}, u32[]{:S(2)}) async-start(bf16[8,48,592]{2,1,0:T(8,128)(2,1)} %pad_maximum_fusion.4), calls=%async_computation | async-start | bytes 983040 | tf_op jit(solution)/shard_map/all_to_all | solution.py:591
  27.9 5.2 %collective-permute-done.9 = bf16[48,1664]{1,0:T(8,128)(2,1)S(1)} collective-permute-done((bf16[48,1664]{1,0:T(8,128)(2,1)S(1)}, bf16[48,1664]{1,0:T(8,128)(2,1)S(1)}, u32[]{:S(2)}, u32[]{:S(2)}) %collective-permute-start.9) | collective-permute-done | bytes 159776 | tf_op jit(solution)/shard_map/ppermute | solution.py:28
  37.4 4.3 all-to-all-start.1
  53.6 16.5 %collective-permute-done.8 = bf16[592,384]{1,0:T(8,128)(2,1)} collective-permute-done((bf16[592,384]{1,0:T(8,128)(2,1)}, bf16[592,384]{1,0:T(8,128)(2,1)}, u32[]{:S(2)}, u32[]{:S(2)}) %collective-permute-start.8) | collective-permute-done | bytes 454688 | tf_op jit(solution)/shard_map/ppermute | solution.py:28
  78.5 16.1 %collective-permute-done.11.refs_9_ = bf16[592,768]{1,0:T(8,128)(2,1)} collective-permute-done((bf16[592,768]{1,0:T(8,128)(2,1)}, bf16[592,768]{1,0:T(8,128)(2,1)}, u32[]{:S(2)}, u32[]{:S(2)}) %collective-permute-start.11) | collective-permute-done | bytes 909344 | tf_op jit(solution)/shard_map/ppermute | solution.py:28
  105.3 10.6 %shard_map.196 = (bf16[1536,768]{1,0:T(8,128)(2,1)}, bf16[1536,768]{1,0:T(8,128)(2,1)}, bf16[1536,192]{1,0:T(8,128)(2,1)S(1)}, bf16[1536,192]{1,0:T(8,128)(2,1)}...) custom-call(bf16[192,1536]{1,0:T(8,128)(2,1)S(1)} %pad_maximum_fusion.2., ...), custom_call_target="tpu_custom_call" | custom-call | flops 1000 | bytes 1000 | tf_op jit(solution)/shard_map/pallas_call | solution.py:188
  118.4 4.2 shard_map.197
  138.7 6.8 %collective-permute-done.19.refs_3_ = bf16[192,1536]{1,0:T(8,128)(2,1)S(1)} collective-permute-done((bf16[192,1536]{1,0:T(8,128)(2,1)S(1)}, bf16[192,1536]{1,0:T(8,128)(2,1)S(1)}, u32[]{:S(2)}, u32[]{:S(2)}) %collective-permute-start.19) | collective-permute-done | bytes 589856 | tf_op jit(solution)/shard_map/ppermute | solution.py:28
  149.8 11.4 %collective-permute-done.21.refs_3_ = bf16[192,1536]{1,0:T(8,128)(2,1)S(1)} collective-permute-done((bf16[192,1536]{1,0:T(8,128)(2,1)S(1)}, bf16[192,1536]{1,0:T(8,128)(2,1)S(1)}, u32[]{:S(2)}, u32[]{:S(2)}) %collective-permute-start.21) | collective-permute-done | bytes 589856 | tf_op jit(solution)/shard_map/ppermute | solution.py:28
  173.7 4.7 collective-permute-done.26
  183.5 7.9 %collective-permute-done.27.refs_3_ = bf16[192,1536]{1,0:T(8,128)(2,1)S(1)} collective-permute-done((bf16[192,1536]{1,0:T(8,128)(2,1)S(1)}, bf16[192,1536]{1,0:T(8,128)(2,1)S(1)}, u32[]{:S(2)}, u32[]{:S(2)}) %collective-permute-start.27) | collective-permute-done | bytes 589856 | tf_op jit(solution)/shard_map/ppermute | solution.py:28
  210.0 16.0 %shard_map.204 = (bf16[1536,1536]{1,0:T(8,128)(2,1)}, bf16[1536,864]{1,0:T(8,128)(2,1)}, bf16[1536,864]{1,0:T(8,128)(2,1)}, bf16[1536,864]{1,0:T(8,128)(2,1)}) custom-call(bf16[192,1536]{1,0:T(8,128)(2,1)S(1)} %constant_dynamic-update-slice_fusion.4.refs_0_, bf16[192,1536]{1,0:T(8,128)(2,1)S(1)} %copy-done.60, ...), custom_call_target="tpu_custom_call" | custom-call | flops 1000 | bytes 1000 | tf_op jit(solution)/shard_map/pallas_call | solution.py:188
  227.8 7.9 %shard_map.221 = bf16[1536,864]{1,0:T(8,128)(2,1)} custom-call(bf16[1536,1536]{1,0:T(8,128)(2,1)} %copy-done.4, bf16[1536,864]{1,0:T(8,128)(2,1)S(1)} %copy-done.2), custom_call_target="tpu_custom_call" | custom-call | flops 1000 | bytes 1000 | tf_op jit(solution)/shard_map/pallas_call | solution.py:283
  235.7 14.3 %all-gather.5.cloned.1.call-done.refs_1_.down = bf16[864,1536]{1,0:T(8,128)(2,1)} async-done(((bf16[864,384]{1,0:T(8,128)(2,1)}), bf16[864,1536]{1,0:T(8,128)(2,1)}) %all-gather.5.cloned.1.call-update) | async-done | bytes 2654224 | tf_op jit(solution)/shard_map/all_gather | solution.py:709
  251.8 6.5 %shard_map.209.refs_0_ = bf16[1536,1728]{1,0:T(8,128)(2,1)} custom-call(bf16[1536,1536]{1,0:T(8,128)(2,1)} %shard_map.208.cot.rows, bf16[864,1536]{1,0:T(8,128)(2,1)S(1)} %copy-done, bf16[1536,864]{1,0:T(8,128)(2,1)S(1)} %copy-done.7, bf16[1536,864]{1,0:T(8,128)(2,1)} %get-tuple-element.156.by_up), custom_call_target="tpu_custom_call" | custom-call | flops 1000 | bytes 1000 | tf_op jit(solution)/shard_map/pallas_call | solution.py:422
  258.3 7.8 %shard_map.210 = (bf16[192,1536]{1,0:T(8,128)(2,1)S(1)}, bf16[192,1536]{1,0:T(8,128)(2,1)S(1)}, bf16[192,1536]{1,0:T(8,128)(2,1)S(1)}, bf16[192,1536]{1,0:T(8,128)(2,1)S(1)}) custom-call(bf16[1536,1728]{1,0:T(8,128)(2,1)} %shard_map.209.refs_0_, bf16[1728,1536]{1,0:T(8,128)(2,1)} %all-gather.3.cloned.1.call-done.refs_8_.refs_1_), custom_call_target="tpu_custom_call" | custom-call | flops 1000 | bytes 1000 | tf_op jit(solution)/shard_map/pallas_call | solution.py:456
  267.1 6.5 %shard_map.211.refs_0_.latter = bf16[1536,1728]{1,0:T(8,128)(2,1)} custom-call(bf16[1536,1536]{1,0:T(8,128)(2,1)} %shard_map.208.cot.rows, bf16[864,1536]{1,0:T(8,128)(2,1)S(1)} %copy-done, bf16[1536,864]{1,0:T(8,128)(2,1)S(1)} %copy-done.7, bf16[1536,864]{1,0:T(8,128)(2,1)} %get-tuple-element.156.by_up, ...), custom_call_target="tpu_custom_call", output_to_operand_aliasing={{}: (4, {})} | custom-call | flops 1000 | bytes 1000 | tf_op jit(solution)/shard_map/pallas_call | solution.py:422
  273.7 7.8 %shard_map.212.near = f32[768,1536]{1,0:T(8,128)S(1)} custom-call(bf16[1536,1728]{1,0:T(8,128)(2,1)} %shard_map.211.refs_0_.latter, bf16[1728,1536]{1,0:T(8,128)(2,1)} %all-gather.3.cloned.1.call-done.refs_8_.refs_1_), custom_call_target="tpu_custom_call" | custom-call | flops 1000 | bytes 1000 | tf_op jit(solution)/shard_map/pallas_call | solution.py:456
  293.9 13.1 %shard_map.228 = bf16[1536,1728]{1,0:T(8,128)(2,1)} custom-call(bf16[1536,1536]{1,0:T(8,128)(2,1)S(1)} %shard_map.227.former, bf16[1536,1728]{1,0:T(8,128)(2,1)} %shard_map.211.refs_0_.latter), custom_call_target="tpu_custom_call" | custom-call | flops 1000 | bytes 1000 | tf_op jit(solution)/shard_map/pallas_call | solution.py:283
  315.1 4.8 shard_map.206
  325.8 4.6 collective-permute-done.50
  337.0 8.1 %collective-permute-done.51.refs_3_ = bf16[192,1536]{1,0:T(8,128)(2,1)} collective-permute-done((bf16[192,1536]{1,0:T(8,128)(2,1)}, bf16[192,1536]{1,0:T(8,128)(2,1)}, u32[]{:S(2)}, u32[]{:S(2)}) %collective-permute-start.51) | collective-permute-done | bytes 589856 | tf_op jit(solution)/shard_map/ppermute | solution.py:28
  349.8 4.8 shard_map.205.near
  354.7 11.0 %shard_map.216 = (bf16[1536,1536]{1,0:T(8,128)(2,1)}, bf16[1536,576]{1,0:T(8,128)(2,1)}, f32[3,192]{1,0:T(4,128)S(1)}, bf16[192,1536]{1,0:T(8,128)(2,1)S(1)}) custom-call(s32[1]{0:T(128)} %bitcast.15.me, bf16[192,1536]{1,0:T(8,128)(2,1)} %constant_dynamic-update-slice_fusion.8.refs_0_, bf16[192,1536]{1,0:T(8,128)(2,1)} %collective-permute-done.49.refs_1_, ...), custom_call_target="tpu_custom_call" | custom-call | flops 1000 | bytes 1000 | tf_op jit(solution)/shard_map/pallas_call | solution.py:188
  372.3 4.2 all-to-all-start.2
  376.6 4.3 convolution_convert_fusion
  382.3 4.2 shard_map.217.near
  386.6 4.3 shard_map.219
  414.6 7.5 %reduce-scatter.5.cloned.1.call-done = bf16[384,1728]{1,0:T(8,128)(2,1)} async-done(((bf16[1536,1728]{1,0:T(8,128)(2,1)}), bf16[384,1728]{1,0:T(8,128)(2,1)}) %reduce-scatter.5.cloned.1.call-update) | async-done | bytes 1327120 | tf_op jit(solution)/shard_map/reduce_scatter | solution.py:738
  429.8 5.5 %collective-permute-start.70 = (bf16[384,576]{0,1:T(8,128)(2,1)S(1)}, bf16[384,576]{0,1:T(8,128)(2,1)S(1)}, u32[]{:S(2)}, u32[]{:S(2)}) collective-permute-start(bf16[384,576]{0,1:T(8,128)(2,1)S(1)} %slice.190), channel_id=1, source_target_pairs={{0,16},{8,24},{16,0},{24,8},{1,17},{9,25},{17,1},{25,9},{2,18},{10... | collective-permute-start | bytes 1327112 | tf_op jit(solution)/shard_map/ppermute | solution.py:28
  445.2 12.8 %collective-permute-done.70 = bf16[384,576]{0,1:T(8,128)(2,1)S(1)} collective-permute-done((bf16[384,576]{0,1:T(8,128)(2,1)S(1)}, bf16[384,576]{0,1:T(8,128)(2,1)S(1)}, u32[]{:S(2)}, u32[]{:S(2)}) %collective-permute-start.70) | collective-permute-done | bytes 442400 | tf_op jit(solution)/shard_map/ppermute | solution.py:28
  469.0 4.1 all-to-all-start.4
  (475 shorter events, 227.3 us)
Async XLA Ops:
  12.6 24.9 %all-to-all-start = ((bf16[8,48,592]{2,1,0:T(8,128)(2,1)}), bf16[8,48,592]{2,1,0:T(8,128)(2,1)}, u32[]{:S(2)}, u32[]{:S(2)}) async-start(bf16[8,48,592]{2,1,0:T(8,128)(2,1)} %pad_maximum_fusion.4), calls=%async_computation | async-start | bytes 983040 | tf_op jit(solution)/shard_map/all_to_all | solution.py:591
  35.7 36.7 %collective-permute-start.6 = (bf16[192,1536]{1,0:T(8,128)(2,1)S(1)}, bf16[192,1536]{1,0:T(8,128)(2,1)}, u32[]{:S(2)}, u32[]{:S(2)}) collective-permute-start(bf16[192,1536]{1,0:T(8,128)(2,1)S(1)} %pad_maximum_fusion.3.refs_2_), channel_id=1, source_target_pairs={{0,1},{1,0},{2,3},{3,2},{4,5},{5,4},{6,7},{7,6},{8,9},{9,8},{10,11... | collective-permute-start | bytes 1769480 | tf_op jit(solution)/shard_map/ppermute | solution.py:28
  37.2 35.2 %collective-permute-start.4 = (bf16[192,1536]{1,0:T(8,128)(2,1)S(1)}, bf16[192,1536]{1,0:T(8,128)(2,1)}, u32[]{:S(2)}, u32[]{:S(2)}) collective-permute-start(bf16[192,1536]{1,0:T(8,128)(2,1)S(1)} %pad_maximum_fusion.2.refs_0_), channel_id=1, source_target_pairs={{0,1},{1,0},{2,3},{3,2},{4,5},{5,4},{6,7},{7,6},{8,9},{9,8},{10,11... | collective-permute-start | bytes 1769480 | tf_op jit(solution)/shard_map/ppermute | solution.py:28
  37.4 37.4 %all-to-all-start.1 = ((bf16[8,144,864]{2,1,0:T(8,128)(2,1)}), bf16[8,144,864]{2,1,0:T(8,128)(2,1)}, u32[]{:S(2)}, u32[]{:S(2)}) async-start(bf16[8,144,864]{2,1,0:T(8,128)(2,1)} %shard_map.201), calls=%async_computation.1 | async-start | bytes 4128768 | tf_op jit(solution)/shard_map/all_to_all | solution.py:591
  41.8 161.8 %all-gather.3.cloned.1.call-start = ((), (), s32[]{:S(2)}) async-start(), calls=%async_computation.7 | async-start | bytes 6635520 | tf_op jit(solution)/shard_map/all_gather | solution.py:676
  45.8 24.4 %collective-permute-start.8 = (bf16[592,384]{1,0:T(8,128)(2,1)}, bf16[592,384]{1,0:T(8,128)(2,1)}, u32[]{:S(2)}, u32[]{:S(2)}) collective-permute-start(bf16[592,384]{1,0:T(8,128)(2,1)} %convolution_convert_fusion.4), channel_id=1, source_target_pairs={{0,16},{8,24},{16,0},{24,8},{1,17},{9,25},{17,1},{25,9},{2,18},{10... | collective-permute-start | bytes 1363976 | tf_op jit(solution)/shard_map/ppermute | solution.py:28
  51.5 20.9 %collective-permute-start.7 = (bf16[192,1536]{1,0:T(8,128)(2,1)}, bf16[192,1536]{1,0:T(8,128)(2,1)}, u32[]{:S(2)}, u32[]{:S(2)}) collective-permute-start(bf16[192,1536]{1,0:T(8,128)(2,1)} %collective-permute-done.3.refs_3_), channel_id=1, source_target_pairs={{0,1},{1,0},{2,3},{3,2},{4,5},{5,4},{6,7},{7,6},{8,9},{9,8},{10,11... | collective-permute-start | bytes 1769480 | tf_op jit(solution)/shard_map/ppermute | solution.py:28
  53.1 19.3 %collective-permute-start.5 = (bf16[192,1536]{1,0:T(8,128)(2,1)}, bf16[192,1536]{1,0:T(8,128)(2,1)}, u32[]{:S(2)}, u32[]{:S(2)}) collective-permute-start(bf16[192,1536]{1,0:T(8,128)(2,1)} %collective-permute-done.1.refs_1_), channel_id=1, source_target_pairs={{0,1},{1,0},{2,3},{3,2},{4,5},{5,4},{6,7},{7,6},{8,9},{9,8},{10,11... | collective-permute-start | bytes 1769480 | tf_op jit(solution)/shard_map/ppermute | solution.py:28
  72.4 22.3 %collective-permute-start.11 = (bf16[592,768]{1,0:T(8,128)(2,1)}, bf16[592,768]{1,0:T(8,128)(2,1)}, u32[]{:S(2)}, u32[]{:S(2)}) collective-permute-start(bf16[592,768]{1,0:T(8,128)(2,1)} %pad_maximum_fusion.1.refs_8_), channel_id=1, source_target_pairs={{0,8},{8,0},{16,24},{24,16},{1,9},{9,1},{17,25},{25,17},{2,10},{10... | collective-permute-start | bytes 2727944 | tf_op jit(solution)/shard_map/ppermute | solution.py:28
  94.7 155.3 %all-gather.5.cloned.1.call-start = ((), (), s32[]{:S(2)}) async-start(), calls=%async_computation.8 | async-start | bytes 3317760 | tf_op jit(solution)/shard_map/all_gather | solution.py:709
  98.7 29.8 %collective-permute-start.18 = (bf16[96,1536]{1,0:T(8,128)(2,1)}, bf16[96,1536]{1,0:T(8,128)(2,1)}, u32[]{:S(2)}, u32[]{:S(2)}) collective-permute-start(bf16[96,1536]{1,0:T(8,128)(2,1)} %get-tuple-element.133), channel_id=1, source_target_pairs={{0,4},{1,5},{2,6},{3,7},{4,0},{5,1},{6,2},{7,3},{8,12},{9,13},{10,... | collective-permute-start | bytes 884744 | tf_op jit(solution)/shard_map/ppermute | solution.py:28
  103.9 26.2 %collective-permute-start.16 = (bf16[96,1536]{1,0:T(8,128)(2,1)}, bf16[96,1536]{1,0:T(8,128)(2,1)}, u32[]{:S(2)}, u32[]{:S(2)}) collective-permute-start(bf16[96,1536]{1,0:T(8,128)(2,1)} %get-tuple-element.132), channel_id=1, source_target_pairs={{0,2},{1,3},{2,0},{3,1},{4,6},{5,7},{6,4},{7,5},{8,10},{9,11},{10,... | collective-permute-start | bytes 884744 | tf_op jit(solution)/shard_map/ppermute | solution.py:28
  128.3 244.1 %reduce-scatter.3.cloned.1.call-start = ((), (), s32[]{:S(2)}) async-start(), calls=%async_computation.9 | async-start | bytes 3440640 | tf_op jit(solution)/shard_map/reduce_scatter | solution.py:738
  165.0 18.0 %collective-permute-start.38 = (bf16[192,1536]{1,0:T(8,128)(2,1)S(1)}, bf16[192,1536]{1,0:T(8,128)(2,1)S(1)}, u32[]{:S(2)}, u32[]{:S(2)}) collective-permute-start(bf16[192,1536]{1,0:T(8,128)(2,1)S(1)} %constant_dynamic-update-slice_fusion.2.refs_2_), channel_id=1, source_target_pairs={{0,1},{1,0},{2,3},{3,2},{4,5},{5,4},{6,7},{7,6},{8,9},{9,8},{10,11... | collective-permute-start | bytes 1769480 | tf_op jit(solution)/shard_map/ppermute | solution.py:28
  165.1 17.9 %collective-permute-start.36 = (bf16[192,1536]{1,0:T(8,128)(2,1)S(1)}, bf16[192,1536]{1,0:T(8,128)(2,1)S(1)}, u32[]{:S(2)}, u32[]{:S(2)}) collective-permute-start(bf16[192,1536]{1,0:T(8,128)(2,1)S(1)} %constant_dynamic-update-slice_fusion.refs_0_), channel_id=1, source_target_pairs={{0,1},{1,0},{2,3},{3,2},{4,5},{5,4},{6,7},{7,6},{8,9},{9,8},{10,11... | collective-permute-start | bytes 1769480 | tf_op jit(solution)/shard_map/ppermute | solution.py:28
  165.6 17.9 %collective-permute-start.39 = (bf16[192,1536]{1,0:T(8,128)(2,1)S(1)}, bf16[192,1536]{1,0:T(8,128)(2,1)S(1)}, u32[]{:S(2)}, u32[]{:S(2)}) collective-permute-start(bf16[192,1536]{1,0:T(8,128)(2,1)S(1)} %collective-permute-done.19.refs_3_), channel_id=1, source_target_pairs={{0,1},{1,0},{2,3},{3,2},{4,5},{5,4},{6,7},{7,6},{8,9},{9,8},{10,11... | collective-permute-start | bytes 1769480 | tf_op jit(solution)/shard_map/ppermute | solution.py:28
  183.0 17.4 %collective-permute-start.30 = (bf16[192,1536]{1,0:T(8,128)(2,1)S(1)}, bf16[192,1536]{1,0:T(8,128)(2,1)S(1)}, u32[]{:S(2)}, u32[]{:S(2)}) collective-permute-start(bf16[192,1536]{1,0:T(8,128)(2,1)S(1)} %constant_dynamic-update-slice_fusion.6.refs_2_), channel_id=1, source_target_pairs={{0,1},{1,0},{2,3},{3,2},{4,5},{5,4},{6,7},{7,6},{8,9},{9,8},{10,11... | collective-permute-start | bytes 1769480 | tf_op jit(solution)/shard_map/ppermute | solution.py:28
  183.5 17.7 %collective-permute-start.28 = (bf16[192,1536]{1,0:T(8,128)(2,1)S(1)}, bf16[192,1536]{1,0:T(8,128)(2,1)S(1)}, u32[]{:S(2)}, u32[]{:S(2)}) collective-permute-start(bf16[192,1536]{1,0:T(8,128)(2,1)S(1)} %constant_dynamic-update-slice_fusion.4.refs_0_), channel_id=1, source_target_pairs={{0,1},{1,0},{2,3},{3,2},{4,5},{5,4},{6,7},{7,6},{8,9},{9,8},{10,11... | collective-permute-start | bytes 1769480 | tf_op jit(solution)/shard_map/ppermute | solution.py:28
  235.7 186.3 %reduce-scatter.5.cloned.1.call-start = ((), (), s32[]{:S(2)}) async-start(), calls=%async_computation.10 | async-start | bytes 6881280 | tf_op jit(solution)/shard_map/reduce_scatter | solution.py:738
  287.3 19.7 %collective-permute-start.44 = (bf16[192,1536]{1,0:T(8,128)(2,1)S(1)}, bf16[192,1536]{1,0:T(8,128)(2,1)S(1)}, u32[]{:S(2)}, u32[]{:S(2)}) collective-permute-start(bf16[192,1536]{1,0:T(8,128)(2,1)S(1)} %get-tuple-element.165), channel_id=1, source_target_pairs={{0,4},{1,5},{2,6},{3,7},{4,0},{5,1},{6,2},{7,3},{8,12},{9,13},{10,... | collective-permute-start | bytes 1769480 | tf_op jit(solution)/shard_map/ppermute | solution.py:28
  288.8 18.3 %collective-permute-start.45 = (bf16[192,1536]{1,0:T(8,128)(2,1)S(1)}, bf16[192,1536]{1,0:T(8,128)(2,1)S(1)}, u32[]{:S(2)}, u32[]{:S(2)}) collective-permute-start(bf16[192,1536]{1,0:T(8,128)(2,1)S(1)} %get-tuple-element.166), channel_id=1, source_target_pairs={{0,2},{1,3},{2,0},{3,1},{4,6},{5,7},{6,4},{7,5},{8,10},{9,11},{10,... | collective-permute-start | bytes 1769480 | tf_op jit(solution)/shard_map/ppermute | solution.py:28
  334.8 19.8 %collective-permute-start.35 = (bf16[192,1536]{1,0:T(8,128)(2,1)}, bf16[192,1536]{1,0:T(8,128)(2,1)}, u32[]{:S(2)}, u32[]{:S(2)}) collective-permute-start(bf16[192,1536]{1,0:T(8,128)(2,1)} %get-tuple-element.150), channel_id=1, source_target_pairs={{0,1},{1,0},{2,3},{3,2},{4,5},{5,4},{6,7},{7,6},{8,9},{9,8},{10,11... | collective-permute-start | bytes 1769480 | tf_op jit(solution)/shard_map/ppermute | solution.py:28
  335.7 19.0 %collective-permute-start.54 = (bf16[192,1536]{1,0:T(8,128)(2,1)}, bf16[192,1536]{1,0:T(8,128)(2,1)}, u32[]{:S(2)}, u32[]{:S(2)}) collective-permute-start(bf16[192,1536]{1,0:T(8,128)(2,1)} %constant_dynamic-update-slice_fusion.10.refs_2_), channel_id=1, source_target_pairs={{0,1},{1,0},{2,3},{3,2},{4,5},{5,4},{6,7},{7,6},{8,9},{9,8},{10,11... | collective-permute-start | bytes 1769480 | tf_op jit(solution)/shard_map/ppermute | solution.py:28
  337.0 17.6 %collective-permute-start.52 = (bf16[192,1536]{1,0:T(8,128)(2,1)}, bf16[192,1536]{1,0:T(8,128)(2,1)}, u32[]{:S(2)}, u32[]{:S(2)}) collective-permute-start(bf16[192,1536]{1,0:T(8,128)(2,1)} %constant_dynamic-update-slice_fusion.8.refs_0_), channel_id=1, source_target_pairs={{0,1},{1,0},{2,3},{3,2},{4,5},{5,4},{6,7},{7,6},{8,9},{9,8},{10,11... | collective-permute-start | bytes 1769480 | tf_op jit(solution)/shard_map/ppermute | solution.py:28
  372.3 20.7 %all-to-all-start.2 = ((bf16[8,48,864]{2,1,0:T(8,128)(2,1)}), bf16[8,48,864]{2,1,0:T(8,128)(2,1)}, u32[]{:S(2)}, u32[]{:S(2)}) async-start(bf16[8,48,864]{2,1,0:T(8,128)(2,1)} %bitcast.120), calls=%async_computation.3 | async-start | bytes 1376256 | tf_op jit(solution)/shard_map/all_to_all | solution.py:591
  380.9 45.2 %collective-permute-start.68 = (bf16[768,576]{0,1:T(8,128)(2,1)}, bf16[768,576]{0,1:T(8,128)(2,1)}, u32[]{:S(2)}, u32[]{:S(2)}) collective-permute-start(bf16[768,576]{0,1:T(8,128)(2,1)} %convolution_convert_fusion), channel_id=1, source_target_pairs={{0,8},{8,0},{16,24},{24,16},{1,9},{9,1},{17,25},{25,17},{2,10},{10... | collective-permute-start | bytes 2654216 | tf_op jit(solution)/shard_map/ppermute | solution.py:28
  405.9 23.8 %collective-permute-start.69 = (bf16[96,1664]{1,0:T(8,128)(2,1)}, bf16[96,1664]{1,0:T(8,128)(2,1)}, u32[]{:S(2)}, u32[]{:S(2)}) collective-permute-start(bf16[96,1664]{1,0:T(8,128)(2,1)} %get-tuple-element.206), channel_id=1, source_target_pairs={{0,8},{8,0},{16,24},{24,16},{1,9},{9,1},{17,25},{25,17},{2,10},{10... | collective-permute-start | bytes 958472 | tf_op jit(solution)/shard_map/ppermute | solution.py:28
  422.0 46.9 %all-to-all-start.3 = ((bf16[8,48,1728]{2,1,0:T(8,128)(2,1)}), bf16[8,48,1728]{2,1,0:T(8,128)(2,1)S(1)}, u32[]{:S(2)}, u32[]{:S(2)}) async-start(bf16[8,48,1728]{2,1,0:T(8,128)(2,1)} %bitcast.119), calls=%async_computation.5 | async-start | bytes 2752512 | tf_op jit(solution)/shard_map/all_to_all | solution.py:591
  429.8 28.2 %collective-permute-start.70 = (bf16[384,576]{0,1:T(8,128)(2,1)S(1)}, bf16[384,576]{0,1:T(8,128)(2,1)S(1)}, u32[]{:S(2)}, u32[]{:S(2)}) collective-permute-start(bf16[384,576]{0,1:T(8,128)(2,1)S(1)} %slice.190), channel_id=1, source_target_pairs={{0,16},{8,24},{16,0},{24,8},{1,17},{9,25},{17,1},{25,9},{2,18},{10... | collective-permute-start | bytes 1327112 | tf_op jit(solution)/shard_map/ppermute | solution.py:28
  435.3 25.5 %collective-permute-start.65 = (bf16[192,1536]{1,0:T(8,128)(2,1)}, bf16[192,1536]{1,0:T(8,128)(2,1)S(1)}, u32[]{:S(2)}, u32[]{:S(2)}) collective-permute-start(bf16[192,1536]{1,0:T(8,128)(2,1)} %get-tuple-element.194), channel_id=1, source_target_pairs={{0,2},{1,3},{2,0},{3,1},{4,6},{5,7},{6,4},{7,5},{8,10},{9,11},{10,... | collective-permute-start | bytes 1769480 | tf_op jit(solution)/shard_map/ppermute | solution.py:28
  437.2 23.6 %collective-permute-start.64 = (bf16[192,1536]{1,0:T(8,128)(2,1)}, bf16[192,1536]{1,0:T(8,128)(2,1)}, u32[]{:S(2)}, u32[]{:S(2)}) collective-permute-start(bf16[192,1536]{1,0:T(8,128)(2,1)} %get-tuple-element.192), channel_id=1, source_target_pairs={{0,4},{1,5},{2,6},{3,7},{4,0},{5,1},{6,2},{7,3},{8,12},{9,13},{10,... | collective-permute-start | bytes 1769480 | tf_op jit(solution)/shard_map/ppermute | solution.py:28
  442.5 30.6 %collective-permute-start.71 = (bf16[48,1664]{1,0:T(8,128)(2,1)S(1)}, bf16[48,1664]{1,0:T(8,128)(2,1)S(1)}, u32[]{:S(2)}, u32[]{:S(2)}) collective-permute-start(bf16[48,1664]{1,0:T(8,128)(2,1)S(1)} %split.13), channel_id=1, source_target_pairs={{0,16},{8,24},{16,0},{24,8},{1,17},{9,25},{17,1},{25,9},{2,18},{10... | collective-permute-start | bytes 479240 | tf_op jit(solution)/shard_map/ppermute | solution.py:28
  (151 other events, 1137.7 us)
Sparse Core Ops, SparseCore 0:
  94.8 99.3 all-gather.2
  196.4 53.5 all-gather.4
  252.3 52.8 reduce-scatter.2
  307.3 114.6 reduce-scatter.4

commit v4 on v3

--- a/solution.py
+++ b/solution.py
@@ -92,7 +92,7 @@
                 out[k * rows : (k + 1) * rows, :] = value.astype(out.dtype)
 
 
-def plane_reduce(near, came, parts, wait=()):
+def plane_reduce(near, came, parts, wait=(), late=()):
     n = lax.axis_size("shard")
     half = n // 2
     outer = bits_of(n)[1:]
@@ -115,7 +115,7 @@
             sends = [after(send, *wait) for send in made[:parts]]
         else:
             made = run(functools.partial(fold_kernel, rows, plans), outs, [], [*kept, *arrived])
-            sends = made[:parts]
+            sends = [after(send, *late) for send in made[:parts]]
         first = kept is near
         kept = made[parts:]
         arrived = [swap(sends[m], route(outer, m)[k]) for m in range(parts)]
@@ -127,10 +127,12 @@
 def line_gather(block, waits=((), ())):
     n = lax.axis_size("dp")
     block = after(block, *waits[0])
+    first = None
     for bit in reversed(bits_of(n)):
         came = swap(block, bit, "dp")
+        first = came if first is None else first
         if bit == 1:
-            return block, came
+            return block, came, first
         block = after(jnp.concatenate([block, came], axis=1), *waits[1])
 
 
@@ -191,7 +193,7 @@
         in_specs=[SCALAR] * len(scalars) + [WHOLE] * len(arrays),
         out_specs=[WHOLE] * len(outs),
         scratch_shapes=list(scratch),
-        compiler_params=pltpu.CompilerParams(vmem_limit_bytes=48 * 2**20),
+        compiler_params=pltpu.CompilerParams(vmem_limit_bytes=2 * lax.axis_size("shard") * 2**20),
         cost_estimate=pl.CostEstimate(flops=1000, bytes_accessed=1000, transcendentals=0),
     )(*[jnp.asarray(v, jnp.int32).reshape(1) for v in scalars], *arrays)
 
@@ -601,8 +603,6 @@
     extra = jnp.concatenate([norm_gain[:, None], ff_gain[:, None], table], axis=1)
     in_parts = jnp.concatenate([in_parts, jnp.broadcast_to(extra[None], (n,) + extra.shape)], axis=2)
     in_came = dealt(in_parts)
-    tok_turned = turned(after(tokens_in, in_parts), z, n_dp)
-    tok_pieces, tok_steps = plane_gather([tok_turned[m] for m in range(batches)])
     out_aug = jnp.concatenate(
         [out_weight, conv_weight, jnp.zeros((own_rows, LANES - conv_weight.shape[1]), BF16)], axis=1
     )
@@ -614,14 +614,9 @@
         if bit > 1:
             out_lines = jnp.concatenate([out_lines, out_came], axis=0)
 
-    weights = [gate_weight, up_weight, down_weight]
-    [ff_parts] = run(
-        functools.partial(spread_kernel, n, whole, rest, 3),
-        [((n, 3 * own_rows, share), BF16)],
-        [],
-        weights,
-    )
-    ff_came = dealt(after(ff_parts, in_came, *tok_steps[0], out_steps[0]))
+    tok_turned = turned(after(tokens_in, in_parts), z, n_dp)
+    tok_pieces, tok_steps = plane_gather([tok_turned[m] for m in range(batches)], ((), (out_steps[0],)))
+
     out_full, tap_cols = run(
         functools.partial(out_kernel, n_dp),
         [((channels, width), BF16), ((channels, LANES), BF16)],
@@ -670,9 +665,17 @@
     offset = (places[None, :] - seq_start)[:, :, None]
 
     waits = (*tok_pieces, out_full, taps, source, own_source, slot_source, offset)
-    in_a, in_b = line_gather(flipped(in_came), ((), waits))
+    in_a, in_b, in_first = line_gather(flipped(in_came), ((), waits))
+
+    def spread(*weights):
+        rows = sum(weight.shape[0] for weight in weights)
+        kernel = functools.partial(spread_kernel, n, whole, rest, len(weights))
+        return run(kernel, [((n, rows, share), BF16)], [], weights)[0]
+
+    ff_came = dealt(after(spread(gate_weight, up_weight), in_first, *tok_steps[-1]))
     gate_block, up_block = [flipped(ff_came[:, k * own_rows : (k + 1) * own_rows]) for k in range(2)]
     two_block = after(jnp.concatenate([gate_block, up_block], axis=0), in_b)
+    down_came = dealt(after(spread(down_weight), ff_came))
     two = lax.all_gather(two_block, "dp", axis=1, tiled=True)
 
     def natural_row(row):
@@ -705,7 +708,7 @@
         [made, c_high, c_low, source[:, :, None], offset, taps],
         [pltpu.VMEM((group, channels), F32)],
     )
-    down_block = flipped(after(ff_came, gated_arr)[:, 2 * own_rows :])
+    down_block = flipped(after(down_came, gated_arr))
     down = lax.all_gather(down_block, "dp", axis=1, tiled=True)
     cot_pieces, cot_steps = plane_gather([cotangent[m] for m in range(batches)], ((ff_came, *tok_steps[-1]), ()))
 
@@ -719,7 +722,7 @@
         functools.partial(hidden_kernel, batches, n_dp),
         [(own, F32), (own, F32)] + [mine] * batches,
         [z],
-        [own_tok, gain_two, *summed_rows(gated_arr, [out_full], cot_steps[-1])],
+        [own_tok, gain_two, *summed_rows(gated_arr, [out_full], (*cot_steps[-1], down_came))],
     )
     ff_pieces, ff_steps = plane_gather(ff_own)
     whole_rows = ((total, width), BF16)
@@ -755,11 +758,11 @@
         [],
         [cot_own, hidden, unit_two, gain_two, *d_ff],
     )
-    branch_pieces, branch_steps = plane_gather(branch_own)
-
     block_came = [swap(piece, 1) for piece in half_rows(ff_inner, [down], 1, BF16, 2 * batches)]
     [block_near] = half_rows(ff_inner, [down], 0, F32, 1)
-    branch_pieces[0] = after(branch_pieces[0], block_near, *block_came)
+    branch_pieces, branch_steps = plane_gather(branch_own, ((), (block_near,)))
+    block_sum, block_first = plane_reduce(block_near, block_came, batches, branch_steps[-1])
+
 
     branch, d_proj, conv_term, d_hidden_own = run(
         functools.partial(conv_back_kernel, batches, n, len(branch_pieces)),
@@ -781,9 +784,12 @@
         [pltpu.VMEM((total, channels), F32)],
     )
     in_sides = [in_a[: 3 * channels], in_b[: 3 * channels]]
-    down_back = dealt(down_sum.reshape(n, own_rows, -1))
-    d_normed = summed_rows(d_proj, in_sides, (down_back,))
-    block_sum, _ = plane_reduce(block_near, block_came, batches, d_normed[batches:])
+    down_back = dealt(after(down_sum, *branch_steps[-1]).reshape(n, own_rows, -1))
+    far = half_rows(after(d_proj, *block_first), in_sides, 1, BF16, 2 * batches)
+    [near] = half_rows(d_proj, in_sides, 0, F32, 1)
+    d_normed, _ = plane_reduce(
+        near, [swap(piece, 1) for piece in far], batches, (down_back, *block_sum[batches:])
+    )
     [block_out] = run(functools.partial(block_kernel, batches), [(own, BF16)], [], [hidden, *block_sum])
     block_out = block_out.reshape(tokens_in.shape)
     [tokens_grad] = run(

time: 504 us -> 487 us (0.966)
  Pallas kernels: 152 us -> 126 us
  local copies, waits for them, and re-layouts: 80.2 us -> 85.9 us
    pallas_call x25 -> x26, Pallas kernels: 83 us -> 58.2 us  [run(): pl.pallas_call(kernel, out_shape=[jax.ShapeDtypeStruct(shape, dtype) for...]
    all_to_all x5 -> x6, waiting for transfers between devices: 2.3 us -> 19 us  [dealt(): lax.all_to_all(blocks, 'shard', split_axis=0, concat_axis=0, tiled=True)]
    all_gather x1, waiting for transfers between devices: 14.3 us -> 1.96 us  [body(): down = lax.all_gather(down_block, 'dp', axis=1, tiled=True)]
    unnamed x210 -> x266, local copies, waits for them, and re-layouts: 56.4 us -> 65 us
    all_to_all x5 -> x6, starting transfers between devices: 22 us -> 26.6 us  [dealt(): lax.all_to_all(blocks, 'shard', split_axis=0, concat_axis=0, tiled=True)]
  transfers between devices with their start and end apart: 81 -> 82, of which waited for: 26 -> 26; matrix products, arithmetic and copies ran while one was open for 11% -> 11% of each run, Pallas kernels for 30% -> 26%
where the time goes in v4:
time: 487 us; the launch traced here: 478 us
  waiting for transfers between devices  135 us (28%)
  Pallas kernels  126 us (26%)
  local copies, waits for them, and re-layouts  85.9 us (18%)
  starting transfers between devices  82.6 us (17%)
  other arithmetic  17.1 us (4%)
  matrix products  16.2 us (3%)
  between operations  15.5 us (3%)
    ppermute x72, waiting for transfers between devices, swap(): return lax.ppermute(value, axis, [(i, i ^ bit) for i in range(n)])  110 us
    unnamed x266, local copies, waits for them, and re-layouts  65 us
    pallas_call x26, Pallas kernels, run(): pl.pallas_call(kernel, out_shape=[jax.ShapeDtypeStruct(shape, dtype) for...  58.2 us
    ppermute x72, starting transfers between devices, swap(): return lax.ppermute(value, axis, [(i, i ^ bit) for i in range(n)])  55.5 us
    pallas_call x8, Pallas kernels, half_rows(): pl.pallas_call(functools.partial(rows_kernel, sides=len(rhs)), out_shape=...  34.2 us
    all_to_all x6, starting transfers between devices, dealt(): lax.all_to_all(blocks, 'shard', split_axis=0, concat_axis=0, tiled=True)  26.6 us
    pallas_call x2, Pallas kernels, product(): pl.pallas_call(product_kernel, out_shape=jax.ShapeDtypeStruct((former.sha...  20.9 us
    all_to_all x6, waiting for transfers between devices, dealt(): lax.all_to_all(blocks, 'shard', split_axis=0, concat_axis=0, tiled=True)  19 us
  transfers between devices with their start and end apart: 82, of which 26 were waited for; matrix products, arithmetic and copies ran while one was open for 11% of the time, Pallas kernels for 26%

profile of v4, /device:TPU:0, one launch (start us, length us, event | category | flops | bytes accessed | tf_op | source)
XLA Modules:
  0.0 478.3 jit_solution(16257896770089228483)
XLA Ops:
  12.6 5.3 %all-to-all-start = ((bf16[8,48,592]{2,1,0:T(8,128)(2,1)}), bf16[8,48,592]{2,1,0:T(8,128)(2,1)S(1)}, u32[]{:S(2)}, u32[]{:S(2)}) async-start(bf16[8,48,592]{2,1,0:T(8,128)(2,1)} %pad_maximum_fusion.6), calls=%async_computation | async-start | bytes 983040 | tf_op jit(solution)/shard_map/all_to_all | solution.py:593
  28.1 4.7 collective-permute-done.3
  45.0 15.9 %collective-permute-done.9 = bf16[592,384]{1,0:T(8,128)(2,1)} collective-permute-done((bf16[592,384]{1,0:T(8,128)(2,1)S(1)}, bf16[592,384]{1,0:T(8,128)(2,1)}, u32[]{:S(2)}, u32[]{:S(2)}) %collective-permute-start.9) | collective-permute-done | bytes 454688 | tf_op jit(solution)/shard_map/ppermute | solution.py:28
  60.9 4.3 all-to-all-start.1
  69.4 14.7 %all-to-all-done.1 = bf16[8,96,864]{2,1,0:T(8,128)(2,1)} async-done(((bf16[8,96,864]{2,1,0:T(8,128)(2,1)}), bf16[8,96,864]{2,1,0:T(8,128)(2,1)}, u32[]{:S(2)}, u32[]{:S(2)}) %all-to-all-start.1) | async-done | bytes 1327136 | tf_op jit(solution)/shard_map/all_to_all | solution.py:593
  95.7 4.2 all-to-all-start.2
  108.6 7.9 %shard_map.196 = (bf16[1536,768]{1,0:T(8,128)(2,1)S(1)}, bf16[1536,768]{1,0:T(8,128)(2,1)S(1)}, bf16[1536,192]{1,0:T(8,128)(2,1)S(1)}, bf16[1536,192]{1,0:T(8,12...) custom-call(bf16[192,1536]{1,0:T(8,128)(2,1)} %pad_maximum_fusion.2., ...), custom_call_target="tpu_custom_call" | custom-call | flops 1000 | bytes 1000 | tf_op jit(solution)/shard_map/pallas_call | solution.py:190
  142.1 10.1 %collective-permute-done.19.refs_3_ = bf16[192,1536]{1,0:T(8,128)(2,1)S(1)} collective-permute-done((bf16[192,1536]{1,0:T(8,128)(2,1)}, bf16[192,1536]{1,0:T(8,128)(2,1)S(1)}, u32[]{:S(2)}, u32[]{:S(2)}) %collective-permute-start.19) | collective-permute-done | bytes 589856 | tf_op jit(solution)/shard_map/ppermute | solution.py:28
  158.0 11.7 %collective-permute-done.21.refs_3_ = bf16[192,1536]{1,0:T(8,128)(2,1)S(1)} collective-permute-done((bf16[192,1536]{1,0:T(8,128)(2,1)S(1)}, bf16[192,1536]{1,0:T(8,128)(2,1)S(1)}, u32[]{:S(2)}, u32[]{:S(2)}) %collective-permute-start.21) | collective-permute-done | bytes 589856 | tf_op jit(solution)/shard_map/ppermute | solution.py:28
  173.5 5.1 %collective-permute-done.22.refs_2_ = bf16[96,1536]{1,0:T(8,128)(2,1)S(1)} collective-permute-done((bf16[96,1536]{1,0:T(8,128)(2,1)S(1)}, bf16[96,1536]{1,0:T(8,128)(2,1)S(1)}, u32[]{:S(2)}, u32[]{:S(2)}) %collective-permute-start.22) | collective-permute-done | bytes 294944 | tf_op jit(solution)/shard_map/ppermute | solution.py:28
  181.7 4.7 collective-permute-done.26
  191.2 8.3 %collective-permute-done.27.refs_3_ = bf16[192,1536]{1,0:T(8,128)(2,1)S(1)} collective-permute-done((bf16[192,1536]{1,0:T(8,128)(2,1)S(1)}, bf16[192,1536]{1,0:T(8,128)(2,1)S(1)}, u32[]{:S(2)}, u32[]{:S(2)}) %collective-permute-start.27) | collective-permute-done | bytes 589856 | tf_op jit(solution)/shard_map/ppermute | solution.py:28
  219.4 11.2 %shard_map.205 = (bf16[1536,1536]{1,0:T(8,128)(2,1)S(1)}, bf16[1536,864]{1,0:T(8,128)(2,1)S(1)}, bf16[1536,864]{1,0:T(8,128)(2,1)S(1)}, bf16[1536,864]{1,0:T(8,128)(2,1)S(1)}) custom-call(bf16[192,1536]{1,0:T(8,128)(2,1)S(1)} %copy-done.53, bf16[192,1536]{1,0:T(8,128)(2,1)S(1)} %copy-done.75, bf16[192,1536]{1,0:T(8,128)(2,1)S(1)} %copy-done.55, ...), custom_call_target="tpu_custom_call" | custom-call | flops 1000 | bytes 1000 | tf_op jit(solution)/shard_map/pallas_call | solution.py:190
  235.7 7.7 %shard_map.224 = bf16[1536,864]{1,0:T(8,128)(2,1)S(1)} custom-call(bf16[1536,1536]{1,0:T(8,128)(2,1)} %copy-done.7, bf16[1536,864]{1,0:T(8,128)(2,1)S(1)} %get-tuple-element.154.refs_0_.latter), custom_call_target="tpu_custom_call" | custom-call | flops 1000 | bytes 1000 | tf_op jit(solution)/shard_map/pallas_call | solution.py:285
  248.8 6.5 %shard_map.210.refs_0_ = bf16[1536,1728]{1,0:T(8,128)(2,1)} custom-call(bf16[1536,1536]{1,0:T(8,128)(2,1)} %copy-done, bf16[864,1536]{1,0:T(8,128)(2,1)S(1)} %copy-done.2, bf16[1536,864]{1,0:T(8,128)(2,1)S(1)} %copy-done.11, bf16[1536,864]{1,0:T(8,128)(2,1)} %copy-done.12), custom_call_target="tpu_custom_call" | custom-call | flops 1000 | bytes 1000 | tf_op jit(solution)/shard_map/pallas_call | solution.py:424
  255.2 7.8 %shard_map.211 = (bf16[192,1536]{1,0:T(8,128)(2,1)S(1)}, bf16[192,1536]{1,0:T(8,128)(2,1)S(1)}, bf16[192,1536]{1,0:T(8,128)(2,1)S(1)}, bf16[192,1536]{1,0:T(8,128)(2,1)S(1)}) custom-call(bf16[1536,1728]{1,0:T(8,128)(2,1)} %shard_map.210.refs_0_, bf16[1728,1536]{1,0:T(8,128)(2,1)} %all-gather.3.cloned.1.call-done.refs_8_.refs_1_), custom_call_target="tpu_custom_call" | custom-call | flops 1000 | bytes 1000 | tf_op jit(solution)/shard_map/pallas_call | solution.py:458
  264.1 6.7 %shard_map.212.refs_0_.latter = bf16[1536,1728]{1,0:T(8,128)(2,1)} custom-call(bf16[1536,1536]{1,0:T(8,128)(2,1)} %copy-done, bf16[864,1536]{1,0:T(8,128)(2,1)S(1)} %copy-done.2, bf16[1536,864]{1,0:T(8,128)(2,1)S(1)} %copy-done.11, bf16[1536,864]{1,0:T(8,128)(2,1)} %copy-done.12, bf16[1536,1728]{1,0:T(8,128)(2,1)} %shard_map.210.refs_0_), custom_call_target="tpu_custom_call", output_to_operand_aliasing={{}: (4, {})} | custom-call | flops 1000 | bytes 1000 | tf_op jit(solution)/shard_map/pallas_call | solution.py:424
  270.8 7.8 %shard_map.213.near = f32[768,1536]{1,0:T(8,128)S(1)} custom-call(bf16[1536,1728]{1,0:T(8,128)(2,1)} %shard_map.212.refs_0_.latter, bf16[1728,1536]{1,0:T(8,128)(2,1)} %all-gather.3.cloned.1.call-done.refs_8_.refs_1_), custom_call_target="tpu_custom_call" | custom-call | flops 1000 | bytes 1000 | tf_op jit(solution)/shard_map/pallas_call | solution.py:458
  284.2 13.2 %shard_map.229 = bf16[1536,1728]{1,0:T(8,128)(2,1)} custom-call(bf16[1536,1536]{1,0:T(8,128)(2,1)S(1)} %shard_map.228.former, bf16[1536,1728]{1,0:T(8,128)(2,1)} %shard_map.212.refs_0_.latter), custom_call_target="tpu_custom_call" | custom-call | flops 1000 | bytes 1000 | tf_op jit(solution)/shard_map/pallas_call | solution.py:285
  300.4 7.1 %collective-permute-done.46.refs_2_ = bf16[96,1536]{1,0:T(8,128)(2,1)S(1)} collective-permute-done((bf16[96,1536]{1,0:T(8,128)(2,1)S(1)}, bf16[96,1536]{1,0:T(8,128)(2,1)S(1)}, u32[]{:S(2)}, u32[]{:S(2)}) %collective-permute-start.46) | collective-permute-done | bytes 294944 | tf_op jit(solution)/shard_map/ppermute | solution.py:28
  309.6 4.5 shard_map.207
  316.1 4.8 %shard_map.206.near = f32[768,1536]{1,0:T(8,128)} custom-call(bf16[1536,864]{1,0:T(8,128)(2,1)S(1)} %copy-done.5, bf16[864,1536]{1,0:T(8,128)(2,1)S(1)} %copy-done.3), custom_call_target="tpu_custom_call" | custom-call | flops 1000 | bytes 1000 | tf_op jit(solution)/shard_map/pallas_call | solution.py:458
  332.9 5.5 %collective-permute-done.51.refs_3_ = bf16[192,1536]{1,0:T(8,128)(2,1)} collective-permute-done((bf16[192,1536]{1,0:T(8,128)(2,1)S(1)}, bf16[192,1536]{1,0:T(8,128)(2,1)}, u32[]{:S(2)}, u32[]{:S(2)}) %collective-permute-start.51) | collective-permute-done | bytes 589856 | tf_op jit(solution)/shard_map/ppermute | solution.py:28
  349.8 7.8 %shard_map.219 = (bf16[1536,1536]{1,0:T(8,128)(2,1)S(1)}, bf16[1536,576]{1,0:T(8,128)(2,1)S(1)}, f32[3,192]{1,0:T(4,128)S(1)}, bf16[192,1536]{1,0:T(8,128)(2,1)S(1)}) custom-call(s32[1]{0:T(128)} %bitcast.15.me, bf16[192,1536]{1,0:T(8,128)(2,1)} %pad_maximum_fusion.4.refs_0_, bf16[192,1536]{1,0:T(8,128)(2,1)} %collective-permute-done.49.refs_1_, ...), custom_call_target="tpu_custom_call" | custom-call | flops 1000 | bytes 1000 | tf_op jit(solution)/shard_map/pallas_call | solution.py:190
  376.3 4.9 %convolution_convert_fusion = bf16[768,576]{0,1:T(8,128)(2,1)} fusion(bf16[1536,768]{1,0:T(8,128)(2,1)} %copy-done.97, bf16[1536,576]{1,0:T(8,128)(2,1)} %copy-done.15), kind=kOutput, calls=%fused_computation.2 | convolution fusion | flops 1359396864 | bytes 5013504 | tf_op jit(solution)/shard_map/dot_general | solution.py:17
  381.8 4.1 shard_map.220.near
  404.3 4.1 collective-permute-done.65.refs_3_
  417.0 5.2 %all-to-all-start.4 = ((bf16[8,48,1728]{2,1,0:T(8,128)(2,1)}), bf16[8,48,1728]{2,1,0:T(8,128)(2,1)S(1)}, u32[]{:S(2)}, u32[]{:S(2)}) async-start(bf16[8,48,1728]{2,1,0:T(8,128)(2,1)} %bitcast.121), calls=%async_computation.6 | async-start | bytes 2752512 | tf_op jit(solution)/shard_map/all_to_all | solution.py:593
  426.5 4.0 collective-permute-start.70
  436.4 17.6 %collective-permute-done.70 = bf16[384,576]{0,1:T(8,128)(2,1)S(1)} collective-permute-done((bf16[384,576]{0,1:T(8,128)(2,1)S(1)}, bf16[384,576]{0,1:T(8,128)(2,1)S(1)}, u32[]{:S(2)}, u32[]{:S(2)}) %collective-permute-start.70) | collective-permute-done | bytes 442400 | tf_op jit(solution)/shard_map/ppermute | solution.py:28
  455.1 4.0 all-to-all-start.5
  464.3 4.2 all-to-all-done.5.came
  (534 shorter events, 227.3 us)
Async XLA Ops:
  12.6 25.0 %all-to-all-start = ((bf16[8,48,592]{2,1,0:T(8,128)(2,1)}), bf16[8,48,592]{2,1,0:T(8,128)(2,1)S(1)}, u32[]{:S(2)}, u32[]{:S(2)}) async-start(bf16[8,48,592]{2,1,0:T(8,128)(2,1)} %pad_maximum_fusion.6), calls=%async_computation | async-start | bytes 983040 | tf_op jit(solution)/shard_map/all_to_all | solution.py:593
  33.8 27.1 %collective-permute-start.4 = (bf16[192,1536]{1,0:T(8,128)(2,1)S(1)}, bf16[192,1536]{1,0:T(8,128)(2,1)}, u32[]{:S(2)}, u32[]{:S(2)}) collective-permute-start(bf16[192,1536]{1,0:T(8,128)(2,1)S(1)} %pad_maximum_fusion.3.refs_2_), channel_id=1, source_target_pairs={{0,2},{1,3},{2,0},{3,1},{4,6},{5,7},{6,4},{7,5},{8,10},{9,11},{10,... | collective-permute-start | bytes 1769480 | tf_op jit(solution)/shard_map/ppermute | solution.py:28
  37.2 23.7 %collective-permute-start.2 = (bf16[192,1536]{1,0:T(8,128)(2,1)}, bf16[192,1536]{1,0:T(8,128)(2,1)}, u32[]{:S(2)}, u32[]{:S(2)}) collective-permute-start(bf16[192,1536]{1,0:T(8,128)(2,1)} %pad_maximum_fusion.2.refs_0_), channel_id=1, source_target_pairs={{0,4},{1,5},{2,6},{3,7},{4,0},{5,1},{6,2},{7,3},{8,12},{9,13},{10,... | collective-permute-start | bytes 1769480 | tf_op jit(solution)/shard_map/ppermute | solution.py:28
  38.3 22.6 %collective-permute-start.9 = (bf16[592,384]{1,0:T(8,128)(2,1)S(1)}, bf16[592,384]{1,0:T(8,128)(2,1)}, u32[]{:S(2)}, u32[]{:S(2)}) collective-permute-start(bf16[592,384]{1,0:T(8,128)(2,1)S(1)} %convolution_convert_fusion.4), channel_id=1, source_target_pairs={{0,16},{8,24},{16,0},{24,8},{1,17},{9,25},{17,1},{25,9},{2,18},{10... | collective-permute-start | bytes 1363976 | tf_op jit(solution)/shard_map/ppermute | solution.py:28
  41.8 25.1 %collective-permute-start.10 = (bf16[96,1664]{1,0:T(8,128)(2,1)S(1)}, bf16[96,1664]{1,0:T(8,128)(2,1)S(1)}, u32[]{:S(2)}, u32[]{:S(2)}) collective-permute-start(bf16[96,1664]{1,0:T(8,128)(2,1)S(1)} %pad_maximum_fusion.7.first), channel_id=1, source_target_pairs={{0,8},{8,0},{16,24},{24,16},{1,9},{9,1},{17,25},{25,17},{2,10},{10... | collective-permute-start | bytes 958472 | tf_op jit(solution)/shard_map/ppermute | solution.py:28
  43.5 25.1 %collective-permute-start.7 = (bf16[192,1536]{1,0:T(8,128)(2,1)S(1)}, bf16[192,1536]{1,0:T(8,128)(2,1)}, u32[]{:S(2)}, u32[]{:S(2)}) collective-permute-start(bf16[192,1536]{1,0:T(8,128)(2,1)S(1)} %pad_maximum_fusion.3.refs_2_), channel_id=1, source_target_pairs={{0,1},{1,0},{2,3},{3,2},{4,5},{5,4},{6,7},{7,6},{8,9},{9,8},{10,11... | collective-permute-start | bytes 1769480 | tf_op jit(solution)/shard_map/ppermute | solution.py:28
  60.9 23.2 %all-to-all-start.1 = ((bf16[8,96,864]{2,1,0:T(8,128)(2,1)}), bf16[8,96,864]{2,1,0:T(8,128)(2,1)}, u32[]{:S(2)}, u32[]{:S(2)}) async-start(bf16[8,96,864]{2,1,0:T(8,128)(2,1)} %shard_map.201), calls=%async_computation.1 | async-start | bytes 2752512 | tf_op jit(solution)/shard_map/all_to_all | solution.py:593
  65.2 143.1 %all-gather.3.cloned.1.call-start = ((), (), s32[]{:S(2)}) async-start(), calls=%async_computation.8 | async-start | bytes 6635520 | tf_op jit(solution)/shard_map/all_gather | solution.py:679
  68.8 22.6 %collective-permute-start.11 = (bf16[592,768]{1,0:T(8,128)(2,1)S(1)}, bf16[592,768]{1,0:T(8,128)(2,1)}, u32[]{:S(2)}, u32[]{:S(2)}) collective-permute-start(bf16[592,768]{1,0:T(8,128)(2,1)S(1)} %pad_maximum_fusion.1.refs_8_), channel_id=1, source_target_pairs={{0,8},{8,0},{16,24},{24,16},{1,9},{9,1},{17,25},{25,17},{2,10},{10... | collective-permute-start | bytes 2727944 | tf_op jit(solution)/shard_map/ppermute | solution.py:28
  95.7 35.9 %all-to-all-start.2 = ((bf16[8,48,864]{2,1,0:T(8,128)(2,1)}), bf16[8,48,864]{2,1,0:T(8,128)(2,1)}, u32[]{:S(2)}, u32[]{:S(2)}) async-start(bf16[8,48,864]{2,1,0:T(8,128)(2,1)} %shard_map.202), calls=%async_computation.2 | async-start | bytes 1376256 | tf_op jit(solution)/shard_map/all_to_all | solution.py:593
  99.9 147.1 %all-gather.5.cloned.1.call-start = ((), (), s32[]{:S(2)}) async-start(), calls=%async_computation.9 | async-start | bytes 3317760 | tf_op jit(solution)/shard_map/all_gather | solution.py:712
  102.6 31.8 %collective-permute-start.18 = (bf16[96,1536]{1,0:T(8,128)(2,1)}, bf16[96,1536]{1,0:T(8,128)(2,1)}, u32[]{:S(2)}, u32[]{:S(2)}) collective-permute-start(bf16[96,1536]{1,0:T(8,128)(2,1)} %get-tuple-element.141), channel_id=1, source_target_pairs={{0,4},{1,5},{2,6},{3,7},{4,0},{5,1},{6,2},{7,3},{8,12},{9,13},{10,... | collective-permute-start | bytes 884744 | tf_op jit(solution)/shard_map/ppermute | solution.py:28
  107.1 30.2 %collective-permute-start.16 = (bf16[96,1536]{1,0:T(8,128)(2,1)S(1)}, bf16[96,1536]{1,0:T(8,128)(2,1)}, u32[]{:S(2)}, u32[]{:S(2)}) collective-permute-start(bf16[96,1536]{1,0:T(8,128)(2,1)S(1)} %get-tuple-element.140), channel_id=1, source_target_pairs={{0,2},{1,3},{2,0},{3,1},{4,6},{5,7},{6,4},{7,5},{8,10},{9,11},{10,... | collective-permute-start | bytes 884744 | tf_op jit(solution)/shard_map/ppermute | solution.py:28
  134.2 236.6 %reduce-scatter.3.cloned.1.call-start = ((), (), s32[]{:S(2)}) async-start(), calls=%async_computation.10 | async-start | bytes 3440640 | tf_op jit(solution)/shard_map/reduce_scatter | solution.py:741
  157.5 33.2 %collective-permute-start.38 = (bf16[192,1536]{1,0:T(8,128)(2,1)S(1)}, bf16[192,1536]{1,0:T(8,128)(2,1)S(1)}, u32[]{:S(2)}, u32[]{:S(2)}) collective-permute-start(bf16[192,1536]{1,0:T(8,128)(2,1)S(1)} %copy-done.51), channel_id=1, source_target_pairs={{0,1},{1,0},{2,3},{3,2},{4,5},{5,4},{6,7},{7,6},{8,9},{9,8},{10,11... | collective-permute-start | bytes 1769480 | tf_op jit(solution)/shard_map/ppermute | solution.py:28
  157.5 33.2 %collective-permute-start.36 = (bf16[192,1536]{1,0:T(8,128)(2,1)S(1)}, bf16[192,1536]{1,0:T(8,128)(2,1)S(1)}, u32[]{:S(2)}, u32[]{:S(2)}) collective-permute-start(bf16[192,1536]{1,0:T(8,128)(2,1)S(1)} %copy-done.50), channel_id=1, source_target_pairs={{0,1},{1,0},{2,3},{3,2},{4,5},{5,4},{6,7},{7,6},{8,9},{9,8},{10,11... | collective-permute-start | bytes 1769480 | tf_op jit(solution)/shard_map/ppermute | solution.py:28
  173.5 17.7 %collective-permute-start.39 = (bf16[192,1536]{1,0:T(8,128)(2,1)S(1)}, bf16[192,1536]{1,0:T(8,128)(2,1)S(1)}, u32[]{:S(2)}, u32[]{:S(2)}) collective-permute-start(bf16[192,1536]{1,0:T(8,128)(2,1)S(1)} %collective-permute-done.19.refs_3_), channel_id=1, source_target_pairs={{0,1},{1,0},{2,3},{3,2},{4,5},{5,4},{6,7},{7,6},{8,9},{9,8},{10,11... | collective-permute-start | bytes 1769480 | tf_op jit(solution)/shard_map/ppermute | solution.py:28
  245.0 172.0 %reduce-scatter.5.cloned.1.call-start = ((), (), s32[]{:S(2)}) async-start(), calls=%async_computation.11 | async-start | bytes 6881280 | tf_op jit(solution)/shard_map/reduce_scatter | solution.py:741
  280.0 17.3 %collective-permute-start.44 = (bf16[192,1536]{1,0:T(8,128)(2,1)}, bf16[192,1536]{1,0:T(8,128)(2,1)}, u32[]{:S(2)}, u32[]{:S(2)}) collective-permute-start(bf16[192,1536]{1,0:T(8,128)(2,1)} %get-tuple-element.174), channel_id=1, source_target_pairs={{0,4},{1,5},{2,6},{3,7},{4,0},{5,1},{6,2},{7,3},{8,12},{9,13},{10,... | collective-permute-start | bytes 1769480 | tf_op jit(solution)/shard_map/ppermute | solution.py:28
  341.1 19.5 %collective-permute-start.53 = (bf16[192,1536]{1,0:T(8,128)(2,1)}, bf16[192,1536]{1,0:T(8,128)(2,1)}, u32[]{:S(2)}, u32[]{:S(2)}) collective-permute-start(bf16[192,1536]{1,0:T(8,128)(2,1)} %get-tuple-element.186), channel_id=1, source_target_pairs={{0,2},{1,3},{2,0},{3,1},{4,6},{5,7},{6,4},{7,5},{8,10},{9,11},{10,... | collective-permute-start | bytes 1769480 | tf_op jit(solution)/shard_map/ppermute | solution.py:28
  342.5 18.2 %collective-permute-start.52 = (bf16[192,1536]{1,0:T(8,128)(2,1)}, bf16[192,1536]{1,0:T(8,128)(2,1)}, u32[]{:S(2)}, u32[]{:S(2)}) collective-permute-start(bf16[192,1536]{1,0:T(8,128)(2,1)} %get-tuple-element.184), channel_id=1, source_target_pairs={{0,4},{1,5},{2,6},{3,7},{4,0},{5,1},{6,2},{7,3},{8,12},{9,13},{10,... | collective-permute-start | bytes 1769480 | tf_op jit(solution)/shard_map/ppermute | solution.py:28
  363.9 17.4 %collective-permute-start.61 = (bf16[192,1536]{1,0:T(8,128)(2,1)}, bf16[192,1536]{1,0:T(8,128)(2,1)}, u32[]{:S(2)}, u32[]{:S(2)}) collective-permute-start(bf16[192,1536]{1,0:T(8,128)(2,1)} %get-tuple-element.200), channel_id=1, source_target_pairs={{0,1},{1,0},{2,3},{3,2},{4,5},{5,4},{6,7},{7,6},{8,9},{9,8},{10,11... | collective-permute-start | bytes 1769480 | tf_op jit(solution)/shard_map/ppermute | solution.py:28
  364.4 21.7 %collective-permute-start.62 = (bf16[192,1536]{1,0:T(8,128)(2,1)}, bf16[192,1536]{1,0:T(8,128)(2,1)}, u32[]{:S(2)}, u32[]{:S(2)}) collective-permute-start(bf16[192,1536]{1,0:T(8,128)(2,1)} %get-tuple-element.201), channel_id=1, source_target_pairs={{0,1},{1,0},{2,3},{3,2},{4,5},{5,4},{6,7},{7,6},{8,9},{9,8},{10,11... | collective-permute-start | bytes 1769480 | tf_op jit(solution)/shard_map/ppermute | solution.py:28
  364.4 21.7 %collective-permute-start.63 = (bf16[192,1536]{1,0:T(8,128)(2,1)}, bf16[192,1536]{1,0:T(8,128)(2,1)}, u32[]{:S(2)}, u32[]{:S(2)}) collective-permute-start(bf16[192,1536]{1,0:T(8,128)(2,1)} %get-tuple-element.202), channel_id=1, source_target_pairs={{0,1},{1,0},{2,3},{3,2},{4,5},{5,4},{6,7},{7,6},{8,9},{9,8},{10,11... | collective-permute-start | bytes 1769480 | tf_op jit(solution)/shard_map/ppermute | solution.py:28
  369.3 23.9 %collective-permute-start.54 = (bf16[96,1536]{1,0:T(8,128)(2,1)}, bf16[96,1536]{1,0:T(8,128)(2,1)S(1)}, u32[]{:S(2)}, u32[]{:S(2)}) collective-permute-start(bf16[96,1536]{1,0:T(8,128)(2,1)} %get-tuple-element.189), channel_id=1, source_target_pairs={{0,2},{1,3},{2,0},{3,1},{4,6},{5,7},{6,4},{7,5},{8,10},{9,11},{10,... | collective-permute-start | bytes 884744 | tf_op jit(solution)/shard_map/ppermute | solution.py:28
  370.8 22.5 %all-to-all-start.3 = ((bf16[8,48,864]{2,1,0:T(8,128)(2,1)}), bf16[8,48,864]{2,1,0:T(8,128)(2,1)S(1)}, u32[]{:S(2)}, u32[]{:S(2)}) async-start(bf16[8,48,864]{2,1,0:T(8,128)(2,1)} %bitcast.123), calls=%async_computation.4 | async-start | bytes 1376256 | tf_op jit(solution)/shard_map/all_to_all | solution.py:593
  374.4 18.9 %collective-permute-start.55 = (bf16[96,1536]{1,0:T(8,128)(2,1)}, bf16[96,1536]{1,0:T(8,128)(2,1)}, u32[]{:S(2)}, u32[]{:S(2)}) collective-permute-start(bf16[96,1536]{1,0:T(8,128)(2,1)} %copy-done.101), channel_id=1, source_target_pairs={{0,4},{1,5},{2,6},{3,7},{4,0},{5,1},{6,2},{7,3},{8,12},{9,13},{10,... | collective-permute-start | bytes 884744 | tf_op jit(solution)/shard_map/ppermute | solution.py:28
  381.2 41.0 %collective-permute-start.68 = (bf16[768,576]{0,1:T(8,128)(2,1)}, bf16[768,576]{0,1:T(8,128)(2,1)}, u32[]{:S(2)}, u32[]{:S(2)}) collective-permute-start(bf16[768,576]{0,1:T(8,128)(2,1)} %convolution_convert_fusion), channel_id=1, source_target_pairs={{0,8},{8,0},{16,24},{24,16},{1,9},{9,1},{17,25},{25,17},{2,10},{10... | collective-permute-start | bytes 2654216 | tf_op jit(solution)/shard_map/ppermute | solution.py:28
  400.7 25.9 %collective-permute-start.69 = (bf16[96,1664]{1,0:T(8,128)(2,1)}, bf16[96,1664]{1,0:T(8,128)(2,1)}, u32[]{:S(2)}, u32[]{:S(2)}) collective-permute-start(bf16[96,1664]{1,0:T(8,128)(2,1)} %get-tuple-element.218), channel_id=1, source_target_pairs={{0,8},{8,0},{16,24},{24,16},{1,9},{9,1},{17,25},{25,17},{2,10},{10... | collective-permute-start | bytes 958472 | tf_op jit(solution)/shard_map/ppermute | solution.py:28
  417.0 38.1 %all-to-all-start.4 = ((bf16[8,48,1728]{2,1,0:T(8,128)(2,1)}), bf16[8,48,1728]{2,1,0:T(8,128)(2,1)S(1)}, u32[]{:S(2)}, u32[]{:S(2)}) async-start(bf16[8,48,1728]{2,1,0:T(8,128)(2,1)} %bitcast.121), calls=%async_computation.6 | async-start | bytes 2752512 | tf_op jit(solution)/shard_map/all_to_all | solution.py:593
  426.5 27.5 %collective-permute-start.70 = (bf16[384,576]{0,1:T(8,128)(2,1)S(1)}, bf16[384,576]{0,1:T(8,128)(2,1)S(1)}, u32[]{:S(2)}, u32[]{:S(2)}) collective-permute-start(bf16[384,576]{0,1:T(8,128)(2,1)S(1)} %slice.186), channel_id=1, source_target_pairs={{0,16},{8,24},{16,0},{24,8},{1,17},{9,25},{17,1},{25,9},{2,18},{10... | collective-permute-start | bytes 1327112 | tf_op jit(solution)/shard_map/ppermute | solution.py:28
  433.8 25.3 %collective-permute-start.71 = (bf16[48,1664]{1,0:T(8,128)(2,1)}, bf16[48,1664]{1,0:T(8,128)(2,1)S(1)}, u32[]{:S(2)}, u32[]{:S(2)}) collective-permute-start(bf16[48,1664]{1,0:T(8,128)(2,1)} %split.13), channel_id=1, source_target_pairs={{0,16},{8,24},{16,0},{24,8},{1,17},{9,25},{17,1},{25,9},{2,18},{10... | collective-permute-start | bytes 479240 | tf_op jit(solution)/shard_map/ppermute | solution.py:28
  (181 other events, 1414.1 us)
Sparse Core Ops, SparseCore 0:
  91.5 100.2 all-gather.2
  193.5 53.5 all-gather.4
  249.3 52.8 reduce-scatter.2
  304.4 112.5 reduce-scatter.4

commit v5 on v4

--- a/solution.py
+++ b/solution.py
@@ -291,7 +291,7 @@
             pl.BlockSpec(latter.shape, lambda i: (0, 0)),
         ],
         out_specs=pl.BlockSpec((rows, latter.shape[1]), lambda i: (i, 0)),
-        compiler_params=pltpu.CompilerParams(vmem_limit_bytes=48 * 2**20),
+        compiler_params=pltpu.CompilerParams(vmem_limit_bytes=min(4 * lax.axis_size("shard"), 48) * 2**20),
         cost_estimate=pl.CostEstimate(flops=1000, bytes_accessed=1000, transcendentals=0),
     )(former, latter)
 
@@ -429,7 +429,7 @@
         + [pl.BlockSpec(memory_space=pl.ANY)] * len(extra),
         out_specs=rows_of(2 * share),
         input_output_aliases={4: 0} if extra else {},
-        compiler_params=pltpu.CompilerParams(vmem_limit_bytes=48 * 2**20),
+        compiler_params=pltpu.CompilerParams(vmem_limit_bytes=min(4 * lax.axis_size("shard"), 48) * 2**20),
         cost_estimate=pl.CostEstimate(flops=1000, bytes_accessed=1000, transcendentals=0),
     )(cot, down, by_gate, by_up, *extra)
 
@@ -462,7 +462,7 @@
         in_specs=[pl.BlockSpec((rows, lhs.shape[1]), lambda i: (part, 0))]
         + [pl.BlockSpec(side.shape, lambda i: (0, 0)) for side in rhs],
         out_specs=[pl.BlockSpec(shape, lambda i: (0, 0))] * pieces,
-        compiler_params=pltpu.CompilerParams(vmem_limit_bytes=48 * 2**20),
+        compiler_params=pltpu.CompilerParams(vmem_limit_bytes=min(4 * lax.axis_size("shard"), 48) * 2**20),
         cost_estimate=pl.CostEstimate(flops=1000, bytes_accessed=1000, transcendentals=0),
     )(lhs, *rhs)
 
@@ -744,7 +744,7 @@
     [cot_columns] = run(turn, [((width, total), BF16)], [], [cot_all])
     [lean_columns] = run(turn, [((width, total), BF16)], [], [lean])
     down_sum = line_sum(cot_columns, ff_inner)
-    d_far = inner_half(1, chunk, cot_all, down, by_gate, by_up)
+    d_far = inner_half(1, chunk, after(cot_all, lean_columns), down, by_gate, by_up)
     far = half_rows(d_far, [two], 1, BF16, 2 * batches)
     came = [swap(piece, 1) for piece in far]
     d_two = inner_half(0, chunk, after(cot_all, *far), down, by_gate, by_up, d_far)

time: 487 us -> 485 us (level)
  local copies, waits for them, and re-layouts: 85.9 us -> 112 us
  Pallas kernels: 126 us -> 100 us
    unnamed x266 -> x258, local copies, waits for them, and re-layouts: 65 us -> 93 us
    pallas_call x8, Pallas kernels: 34.2 us -> 21.2 us  [half_rows(): pl.pallas_call(functools.partial(rows_kernel, sides=len(rhs)), out_shape=...]
    ppermute x72, waiting for transfers between devices: 110 us -> 118 us  [swap(): return lax.ppermute(value, axis, [(i, i ^ bit) for i in range(n)])]
    pallas_call x2, Pallas kernels: 13.1 us -> 5.7 us  [inner_half(): pl.pallas_call(functools.partial(inner_kernel, chunk), out_shape=jax.Shap...]
    pallas_call x2, Pallas kernels: 20.9 us -> 14.9 us  [product(): pl.pallas_call(product_kernel, out_shape=jax.ShapeDtypeStruct((former.sha...]
  transfers between devices with their start and end apart: 82 -> 82, of which waited for: 26 -> 27; matrix products, arithmetic and copies ran while one was open for 11% -> 10% of each run, Pallas kernels for 26% -> 21%
where the time goes in v5:
time: 485 us; the launch traced here: 477 us
  waiting for transfers between devices  137 us (28%)
  local copies, waits for them, and re-layouts  112 us (23%)
  Pallas kernels  100 us (21%)
  starting transfers between devices  81 us (17%)
  matrix products  16.3 us (3%)
  between operations  15.4 us (3%)
  other arithmetic  14.7 us (3%)
    ppermute x72, waiting for transfers between devices, swap(): return lax.ppermute(value, axis, [(i, i ^ bit) for i in range(n)])  118 us
    unnamed x258, local copies, waits for them, and re-layouts  93 us
    pallas_call x26, Pallas kernels, run(): pl.pallas_call(kernel, out_shape=[jax.ShapeDtypeStruct(shape, dtype) for...  58.4 us
    ppermute x72, starting transfers between devices, swap(): return lax.ppermute(value, axis, [(i, i ^ bit) for i in range(n)])  55.2 us
    all_to_all x6, starting transfers between devices, dealt(): lax.all_to_all(blocks, 'shard', split_axis=0, concat_axis=0, tiled=True)  25.3 us
    pallas_call x8, Pallas kernels, half_rows(): pl.pallas_call(functools.partial(rows_kernel, sides=len(rhs)), out_shape=...  21.2 us
    all_to_all x6, waiting for transfers between devices, dealt(): lax.all_to_all(blocks, 'shard', split_axis=0, concat_axis=0, tiled=True)  19.1 us
    dot_general x7, matrix products, dot(): lax.dot_general(former, latter, ((dims[0], dims[1]), ((), ())), preferred...  16.3 us
  transfers between devices with their start and end apart: 82, of which 27 were waited for; matrix products, arithmetic and copies ran while one was open for 10% of the time, Pallas kernels for 21%

profile of v5, /device:TPU:0, one launch (start us, length us, event | category | flops | bytes accessed | tf_op | source)
XLA Modules:
  0.0 476.5 jit_solution(741694676980231864)
XLA Ops:
  12.6 5.3 %all-to-all-start = ((bf16[8,48,592]{2,1,0:T(8,128)(2,1)}), bf16[8,48,592]{2,1,0:T(8,128)(2,1)S(1)}, u32[]{:S(2)}, u32[]{:S(2)}) async-start(bf16[8,48,592]{2,1,0:T(8,128)(2,1)} %pad_maximum_fusion.6), calls=%async_computation | async-start | bytes 983040 | tf_op jit(solution)/shard_map/all_to_all | solution.py:593
  27.5 5.3 %collective-permute-done.3 = bf16[96,1536]{1,0:T(8,128)(2,1)} collective-permute-done((bf16[96,1536]{1,0:T(8,128)(2,1)S(1)}, bf16[96,1536]{1,0:T(8,128)(2,1)}, u32[]{:S(2)}, u32[]{:S(2)}) %collective-permute-start.3) | collective-permute-done | bytes 294944 | tf_op jit(solution)/shard_map/ppermute | solution.py:28
  43.8 16.9 %collective-permute-done.9 = bf16[592,384]{1,0:T(8,128)(2,1)} collective-permute-done((bf16[592,384]{1,0:T(8,128)(2,1)S(1)}, bf16[592,384]{1,0:T(8,128)(2,1)}, u32[]{:S(2)}, u32[]{:S(2)}) %collective-permute-start.9) | collective-permute-done | bytes 454688 | tf_op jit(solution)/shard_map/ppermute | solution.py:28
  60.7 4.3 all-to-all-start.1
  69.2 14.8 %all-to-all-done.1 = bf16[8,96,864]{2,1,0:T(8,128)(2,1)} async-done(((bf16[8,96,864]{2,1,0:T(8,128)(2,1)}), bf16[8,96,864]{2,1,0:T(8,128)(2,1)}, u32[]{:S(2)}, u32[]{:S(2)}) %all-to-all-start.1) | async-done | bytes 1327136 | tf_op jit(solution)/shard_map/all_to_all | solution.py:593
  87.7 3.4 collective-permute-done.11.refs_9_
  95.6 4.2 all-to-all-start.2
  109.4 7.9 %shard_map.196 = (bf16[1536,768]{1,0:T(8,128)(2,1)S(1)}, bf16[1536,768]{1,0:T(8,128)(2,1)S(1)}, bf16[1536,192]{1,0:T(8,128)(2,1)S(1)}, bf16[1536,192]{1,0:T(8,12...) custom-call(bf16[192,1536]{1,0:T(8,128)(2,1)} %pad_maximum_fusion.2., ...), custom_call_target="tpu_custom_call" | custom-call | flops 1000 | bytes 1000 | tf_op jit(solution)/shard_map/pallas_call | solution.py:190
  140.7 10.1 %collective-permute-done.19.refs_3_ = bf16[192,1536]{1,0:T(8,128)(2,1)S(1)} collective-permute-done((bf16[192,1536]{1,0:T(8,128)(2,1)}, bf16[192,1536]{1,0:T(8,128)(2,1)S(1)}, u32[]{:S(2)}, u32[]{:S(2)}) %collective-permute-start.19) | collective-permute-done | bytes 589856 | tf_op jit(solution)/shard_map/ppermute | solution.py:28
  155.2 12.2 %collective-permute-done.21.refs_3_ = bf16[192,1536]{1,0:T(8,128)(2,1)S(1)} collective-permute-done((bf16[192,1536]{1,0:T(8,128)(2,1)S(1)}, bf16[192,1536]{1,0:T(8,128)(2,1)S(1)}, u32[]{:S(2)}, u32[]{:S(2)}) %collective-permute-start.21) | collective-permute-done | bytes 589856 | tf_op jit(solution)/shard_map/ppermute | solution.py:28
  170.6 5.7 %collective-permute-done.22.refs_2_ = bf16[96,1536]{1,0:T(8,128)(2,1)S(1)} collective-permute-done((bf16[96,1536]{1,0:T(8,128)(2,1)S(1)}, bf16[96,1536]{1,0:T(8,128)(2,1)S(1)}, u32[]{:S(2)}, u32[]{:S(2)}) %collective-permute-start.22) | collective-permute-done | bytes 294944 | tf_op jit(solution)/shard_map/ppermute | solution.py:28
  180.3 4.6 collective-permute-done.26
  189.8 8.4 %collective-permute-done.27.refs_3_ = bf16[192,1536]{1,0:T(8,128)(2,1)S(1)} collective-permute-done((bf16[192,1536]{1,0:T(8,128)(2,1)S(1)}, bf16[192,1536]{1,0:T(8,128)(2,1)S(1)}, u32[]{:S(2)}, u32[]{:S(2)}) %collective-permute-start.27) | collective-permute-done | bytes 589856 | tf_op jit(solution)/shard_map/ppermute | solution.py:28
  218.0 11.1 %shard_map.205 = (bf16[1536,1536]{1,0:T(8,128)(2,1)S(1)}, bf16[1536,864]{1,0:T(8,128)(2,1)S(1)}, bf16[1536,864]{1,0:T(8,128)(2,1)S(1)}, bf16[1536,864]{1,0:T(8,128)(2,1)S(1)}) custom-call(bf16[192,1536]{1,0:T(8,128)(2,1)S(1)} %copy-done.64, bf16[192,1536]{1,0:T(8,128)(2,1)S(1)} %copy-done.90, bf16[192,1536]{1,0:T(8,128)(2,1)S(1)} %copy-done.66, ...), custom_call_target="tpu_custom_call" | custom-call | flops 1000 | bytes 1000 | tf_op jit(solution)/shard_map/pallas_call | solution.py:190
  234.4 5.5 %shard_map.225 = bf16[1536,864]{1,0:T(8,128)(2,1)S(1)} custom-call(bf16[1536,1536]{1,0:T(8,128)(2,1)S(1)} %copy-done.9, bf16[1536,864]{1,0:T(8,128)(2,1)S(1)} %get-tuple-element.155.refs_0_.latter), custom_call_target="tpu_custom_call" | custom-call | flops 1000 | bytes 1000 | tf_op jit(solution)/shard_map/pallas_call | solution.py:285
  260.7 4.4 shard_map.212
  273.4 4.4 shard_map.214.near
  286.7 9.4 %shard_map.229 = bf16[1536,1728]{1,0:T(8,128)(2,1)S(1)} custom-call(bf16[1536,1536]{1,0:T(8,128)(2,1)S(1)} %copy-done.13, bf16[1536,1728]{1,0:T(8,128)(2,1)S(1)} %shard_map.213.refs_0_.latter), custom_call_target="tpu_custom_call" | custom-call | flops 1000 | bytes 1000 | tf_op jit(solution)/shard_map/pallas_call | solution.py:285
  304.8 6.7 %collective-permute-done.46.refs_2_ = bf16[96,1536]{1,0:T(8,128)(2,1)S(1)} collective-permute-done((bf16[96,1536]{1,0:T(8,128)(2,1)S(1)}, bf16[96,1536]{1,0:T(8,128)(2,1)S(1)}, u32[]{:S(2)}, u32[]{:S(2)}) %collective-permute-start.46) | collective-permute-done | bytes 294944 | tf_op jit(solution)/shard_map/ppermute | solution.py:28
  321.4 4.8 collective-permute-done.48
  332.1 8.8 %collective-permute-done.51.refs_3_ = bf16[192,1536]{1,0:T(8,128)(2,1)} collective-permute-done((bf16[192,1536]{1,0:T(8,128)(2,1)S(1)}, bf16[192,1536]{1,0:T(8,128)(2,1)}, u32[]{:S(2)}, u32[]{:S(2)}) %collective-permute-start.51) | collective-permute-done | bytes 589856 | tf_op jit(solution)/shard_map/ppermute | solution.py:28
  352.9 7.8 %shard_map.220 = (bf16[1536,1536]{1,0:T(8,128)(2,1)S(1)}, bf16[1536,576]{1,0:T(8,128)(2,1)S(1)}, f32[3,192]{1,0:T(4,128)S(1)}, bf16[192,1536]{1,0:T(8,128)(2,1)S(1)}) custom-call(s32[1]{0:T(128)} %bitcast.15.me, bf16[192,1536]{1,0:T(8,128)(2,1)S(1)} %pad_maximum_fusion.4.refs_0_, bf16[192,1536]{1,0:T(8,128)(2,1)} %collective-permute-done.49.refs_1_, ...), custom_call_target="tpu_custom_call" | custom-call | flops 1000 | bytes 1000 | tf_op jit(solution)/shard_map/pallas_call | solution.py:190
  365.0 3.2 shard_map.222
  374.7 3.5 all-to-all-start.3
  380.2 4.9 %convolution_convert_fusion = bf16[768,576]{0,1:T(8,128)(2,1)} fusion(bf16[1536,768]{1,0:T(8,128)(2,1)} %copy-done.112, bf16[1536,576]{1,0:T(8,128)(2,1)} %copy-done.23), kind=kOutput, calls=%fused_computation.2 | convolution fusion | flops 1359396864 | bytes 5013504 | tf_op jit(solution)/shard_map/dot_general | solution.py:17
  399.6 3.5 fusion.24.term
  408.2 4.2 collective-permute-done.65.refs_3_
  417.3 3.9 all-to-all-start.4
  421.2 3.6 convert_add_fusion
  435.1 17.2 %collective-permute-done.70 = bf16[384,576]{0,1:T(8,128)(2,1)S(1)} collective-permute-done((bf16[384,576]{0,1:T(8,128)(2,1)S(1)}, bf16[384,576]{0,1:T(8,128)(2,1)S(1)}, u32[]{:S(2)}, u32[]{:S(2)}) %collective-permute-start.70) | collective-permute-done | bytes 442400 | tf_op jit(solution)/shard_map/ppermute | solution.py:28
  453.4 4.0 all-to-all-start.5
  462.5 4.3 all-to-all-done.5.came
  (526 shorter events, 242.6 us)
Async XLA Ops:
  12.6 25.0 %all-to-all-start = ((bf16[8,48,592]{2,1,0:T(8,128)(2,1)}), bf16[8,48,592]{2,1,0:T(8,128)(2,1)S(1)}, u32[]{:S(2)}, u32[]{:S(2)}) async-start(bf16[8,48,592]{2,1,0:T(8,128)(2,1)} %pad_maximum_fusion.6), calls=%async_computation | async-start | bytes 983040 | tf_op jit(solution)/shard_map/all_to_all | solution.py:593
  33.8 26.9 %collective-permute-start.4 = (bf16[192,1536]{1,0:T(8,128)(2,1)S(1)}, bf16[192,1536]{1,0:T(8,128)(2,1)}, u32[]{:S(2)}, u32[]{:S(2)}) collective-permute-start(bf16[192,1536]{1,0:T(8,128)(2,1)S(1)} %pad_maximum_fusion.3.refs_2_), channel_id=1, source_target_pairs={{0,2},{1,3},{2,0},{3,1},{4,6},{5,7},{6,4},{7,5},{8,10},{9,11},{10,... | collective-permute-start | bytes 1769480 | tf_op jit(solution)/shard_map/ppermute | solution.py:28
  37.2 23.6 %collective-permute-start.2 = (bf16[192,1536]{1,0:T(8,128)(2,1)}, bf16[192,1536]{1,0:T(8,128)(2,1)}, u32[]{:S(2)}, u32[]{:S(2)}) collective-permute-start(bf16[192,1536]{1,0:T(8,128)(2,1)} %pad_maximum_fusion.2.refs_0_), channel_id=1, source_target_pairs={{0,4},{1,5},{2,6},{3,7},{4,0},{5,1},{6,2},{7,3},{8,12},{9,13},{10,... | collective-permute-start | bytes 1769480 | tf_op jit(solution)/shard_map/ppermute | solution.py:28
  38.0 22.7 %collective-permute-start.9 = (bf16[592,384]{1,0:T(8,128)(2,1)S(1)}, bf16[592,384]{1,0:T(8,128)(2,1)}, u32[]{:S(2)}, u32[]{:S(2)}) collective-permute-start(bf16[592,384]{1,0:T(8,128)(2,1)S(1)} %convolution_convert_fusion.4), channel_id=1, source_target_pairs={{0,16},{8,24},{16,0},{24,8},{1,17},{9,25},{17,1},{25,9},{2,18},{10... | collective-permute-start | bytes 1363976 | tf_op jit(solution)/shard_map/ppermute | solution.py:28
  41.6 24.5 %collective-permute-start.10 = (bf16[96,1664]{1,0:T(8,128)(2,1)S(1)}, bf16[96,1664]{1,0:T(8,128)(2,1)S(1)}, u32[]{:S(2)}, u32[]{:S(2)}) collective-permute-start(bf16[96,1664]{1,0:T(8,128)(2,1)S(1)} %pad_maximum_fusion.7.first), channel_id=1, source_target_pairs={{0,8},{8,0},{16,24},{24,16},{1,9},{9,1},{17,25},{25,17},{2,10},{10... | collective-permute-start | bytes 958472 | tf_op jit(solution)/shard_map/ppermute | solution.py:28
  43.3 24.5 %collective-permute-start.7 = (bf16[192,1536]{1,0:T(8,128)(2,1)S(1)}, bf16[192,1536]{1,0:T(8,128)(2,1)}, u32[]{:S(2)}, u32[]{:S(2)}) collective-permute-start(bf16[192,1536]{1,0:T(8,128)(2,1)S(1)} %pad_maximum_fusion.3.refs_2_), channel_id=1, source_target_pairs={{0,1},{1,0},{2,3},{3,2},{4,5},{5,4},{6,7},{7,6},{8,9},{9,8},{10,11... | collective-permute-start | bytes 1769480 | tf_op jit(solution)/shard_map/ppermute | solution.py:28
  60.7 23.2 %all-to-all-start.1 = ((bf16[8,96,864]{2,1,0:T(8,128)(2,1)}), bf16[8,96,864]{2,1,0:T(8,128)(2,1)}, u32[]{:S(2)}, u32[]{:S(2)}) async-start(bf16[8,96,864]{2,1,0:T(8,128)(2,1)} %shard_map.201), calls=%async_computation.1 | async-start | bytes 2752512 | tf_op jit(solution)/shard_map/all_to_all | solution.py:593
  65.0 141.9 %all-gather.3.cloned.1.call-start = ((), (), s32[]{:S(2)}) async-start(), calls=%async_computation.8 | async-start | bytes 6635520 | tf_op jit(solution)/shard_map/all_gather | solution.py:679
  68.6 22.6 %collective-permute-start.11 = (bf16[592,768]{1,0:T(8,128)(2,1)S(1)}, bf16[592,768]{1,0:T(8,128)(2,1)}, u32[]{:S(2)}, u32[]{:S(2)}) collective-permute-start(bf16[592,768]{1,0:T(8,128)(2,1)S(1)} %pad_maximum_fusion.1.refs_8_), channel_id=1, source_target_pairs={{0,8},{8,0},{16,24},{24,16},{1,9},{9,1},{17,25},{25,17},{2,10},{10... | collective-permute-start | bytes 2727944 | tf_op jit(solution)/shard_map/ppermute | solution.py:28
  95.6 34.6 %all-to-all-start.2 = ((bf16[8,48,864]{2,1,0:T(8,128)(2,1)}), bf16[8,48,864]{2,1,0:T(8,128)(2,1)}, u32[]{:S(2)}, u32[]{:S(2)}) async-start(bf16[8,48,864]{2,1,0:T(8,128)(2,1)} %shard_map.202), calls=%async_computation.2 | async-start | bytes 1376256 | tf_op jit(solution)/shard_map/all_to_all | solution.py:593
  99.8 147.6 %all-gather.5.cloned.1.call-start = ((), (), s32[]{:S(2)}) async-start(), calls=%async_computation.9 | async-start | bytes 3317760 | tf_op jit(solution)/shard_map/all_gather | solution.py:712
  102.5 30.6 %collective-permute-start.18 = (bf16[96,1536]{1,0:T(8,128)(2,1)}, bf16[96,1536]{1,0:T(8,128)(2,1)}, u32[]{:S(2)}, u32[]{:S(2)}) collective-permute-start(bf16[96,1536]{1,0:T(8,128)(2,1)} %get-tuple-element.142), channel_id=1, source_target_pairs={{0,4},{1,5},{2,6},{3,7},{4,0},{5,1},{6,2},{7,3},{8,12},{9,13},{10,... | collective-permute-start | bytes 884744 | tf_op jit(solution)/shard_map/ppermute | solution.py:28
  107.9 27.9 %collective-permute-start.16 = (bf16[96,1536]{1,0:T(8,128)(2,1)}, bf16[96,1536]{1,0:T(8,128)(2,1)}, u32[]{:S(2)}, u32[]{:S(2)}) collective-permute-start(bf16[96,1536]{1,0:T(8,128)(2,1)} %get-tuple-element.141), channel_id=1, source_target_pairs={{0,2},{1,3},{2,0},{3,1},{4,6},{5,7},{6,4},{7,5},{8,10},{9,11},{10,... | collective-permute-start | bytes 884744 | tf_op jit(solution)/shard_map/ppermute | solution.py:28
  132.8 241.9 %reduce-scatter.3.cloned.1.call-start = ((), (), s32[]{:S(2)}) async-start(), calls=%async_computation.10 | async-start | bytes 3440640 | tf_op jit(solution)/shard_map/reduce_scatter | solution.py:741
  154.7 34.5 %collective-permute-start.38 = (bf16[192,1536]{1,0:T(8,128)(2,1)S(1)}, bf16[192,1536]{1,0:T(8,128)(2,1)S(1)}, u32[]{:S(2)}, u32[]{:S(2)}) collective-permute-start(bf16[192,1536]{1,0:T(8,128)(2,1)S(1)} %copy-done.62), channel_id=1, source_target_pairs={{0,1},{1,0},{2,3},{3,2},{4,5},{5,4},{6,7},{7,6},{8,9},{9,8},{10,11... | collective-permute-start | bytes 1769480 | tf_op jit(solution)/shard_map/ppermute | solution.py:28
  154.7 34.5 %collective-permute-start.36 = (bf16[192,1536]{1,0:T(8,128)(2,1)S(1)}, bf16[192,1536]{1,0:T(8,128)(2,1)S(1)}, u32[]{:S(2)}, u32[]{:S(2)}) collective-permute-start(bf16[192,1536]{1,0:T(8,128)(2,1)S(1)} %constant_dynamic-update-slice_fusion.refs_0_), channel_id=1, source_target_pairs={{0,1},{1,0},{2,3},{3,2},{4,5},{5,4},{6,7},{7,6},{8,9},{9,8},{10,11... | collective-permute-start | bytes 1769480 | tf_op jit(solution)/shard_map/ppermute | solution.py:28
  170.6 19.2 %collective-permute-start.39 = (bf16[192,1536]{1,0:T(8,128)(2,1)S(1)}, bf16[192,1536]{1,0:T(8,128)(2,1)S(1)}, u32[]{:S(2)}, u32[]{:S(2)}) collective-permute-start(bf16[192,1536]{1,0:T(8,128)(2,1)S(1)} %collective-permute-done.19.refs_3_), channel_id=1, source_target_pairs={{0,1},{1,0},{2,3},{3,2},{4,5},{5,4},{6,7},{7,6},{8,9},{9,8},{10,11... | collective-permute-start | bytes 1769480 | tf_op jit(solution)/shard_map/ppermute | solution.py:28
  241.6 175.7 %reduce-scatter.5.cloned.1.call-start = ((), (), s32[]{:S(2)}) async-start(), calls=%async_computation.11 | async-start | bytes 6881280 | tf_op jit(solution)/shard_map/reduce_scatter | solution.py:741
  281.3 17.2 %collective-permute-start.44 = (bf16[192,1536]{1,0:T(8,128)(2,1)}, bf16[192,1536]{1,0:T(8,128)(2,1)}, u32[]{:S(2)}, u32[]{:S(2)}) collective-permute-start(bf16[192,1536]{1,0:T(8,128)(2,1)} %get-tuple-element.177), channel_id=1, source_target_pairs={{0,4},{1,5},{2,6},{3,7},{4,0},{5,1},{6,2},{7,3},{8,12},{9,13},{10,... | collective-permute-start | bytes 1769480 | tf_op jit(solution)/shard_map/ppermute | solution.py:28
  342.2 21.5 %collective-permute-start.53 = (bf16[192,1536]{1,0:T(8,128)(2,1)}, bf16[192,1536]{1,0:T(8,128)(2,1)}, u32[]{:S(2)}, u32[]{:S(2)}) collective-permute-start(bf16[192,1536]{1,0:T(8,128)(2,1)} %get-tuple-element.189), channel_id=1, source_target_pairs={{0,2},{1,3},{2,0},{3,1},{4,6},{5,7},{6,4},{7,5},{8,10},{9,11},{10,... | collective-permute-start | bytes 1769480 | tf_op jit(solution)/shard_map/ppermute | solution.py:28
  344.1 19.6 %collective-permute-start.52 = (bf16[192,1536]{1,0:T(8,128)(2,1)}, bf16[192,1536]{1,0:T(8,128)(2,1)}, u32[]{:S(2)}, u32[]{:S(2)}) collective-permute-start(bf16[192,1536]{1,0:T(8,128)(2,1)} %get-tuple-element.187), channel_id=1, source_target_pairs={{0,4},{1,5},{2,6},{3,7},{4,0},{5,1},{6,2},{7,3},{8,12},{9,13},{10,... | collective-permute-start | bytes 1769480 | tf_op jit(solution)/shard_map/ppermute | solution.py:28
  368.2 16.9 %collective-permute-start.61 = (bf16[192,1536]{1,0:T(8,128)(2,1)}, bf16[192,1536]{1,0:T(8,128)(2,1)}, u32[]{:S(2)}, u32[]{:S(2)}) collective-permute-start(bf16[192,1536]{1,0:T(8,128)(2,1)} %get-tuple-element.203), channel_id=1, source_target_pairs={{0,1},{1,0},{2,3},{3,2},{4,5},{5,4},{6,7},{7,6},{8,9},{9,8},{10,11... | collective-permute-start | bytes 1769480 | tf_op jit(solution)/shard_map/ppermute | solution.py:28
  368.7 21.4 %collective-permute-start.62 = (bf16[192,1536]{1,0:T(8,128)(2,1)}, bf16[192,1536]{1,0:T(8,128)(2,1)}, u32[]{:S(2)}, u32[]{:S(2)}) collective-permute-start(bf16[192,1536]{1,0:T(8,128)(2,1)} %get-tuple-element.204), channel_id=1, source_target_pairs={{0,1},{1,0},{2,3},{3,2},{4,5},{5,4},{6,7},{7,6},{8,9},{9,8},{10,11... | collective-permute-start | bytes 1769480 | tf_op jit(solution)/shard_map/ppermute | solution.py:28
  368.7 21.4 %collective-permute-start.63 = (bf16[192,1536]{1,0:T(8,128)(2,1)}, bf16[192,1536]{1,0:T(8,128)(2,1)}, u32[]{:S(2)}, u32[]{:S(2)}) collective-permute-start(bf16[192,1536]{1,0:T(8,128)(2,1)} %get-tuple-element.205), channel_id=1, source_target_pairs={{0,1},{1,0},{2,3},{3,2},{4,5},{5,4},{6,7},{7,6},{8,9},{9,8},{10,11... | collective-permute-start | bytes 1769480 | tf_op jit(solution)/shard_map/ppermute | solution.py:28
  373.7 23.6 %collective-permute-start.54 = (bf16[96,1536]{1,0:T(8,128)(2,1)}, bf16[96,1536]{1,0:T(8,128)(2,1)S(1)}, u32[]{:S(2)}, u32[]{:S(2)}) collective-permute-start(bf16[96,1536]{1,0:T(8,128)(2,1)} %get-tuple-element.192), channel_id=1, source_target_pairs={{0,2},{1,3},{2,0},{3,1},{4,6},{5,7},{6,4},{7,5},{8,10},{9,11},{10,... | collective-permute-start | bytes 884744 | tf_op jit(solution)/shard_map/ppermute | solution.py:28
  374.7 22.7 %all-to-all-start.3 = ((bf16[8,48,864]{2,1,0:T(8,128)(2,1)}), bf16[8,48,864]{2,1,0:T(8,128)(2,1)S(1)}, u32[]{:S(2)}, u32[]{:S(2)}) async-start(bf16[8,48,864]{2,1,0:T(8,128)(2,1)} %bitcast.123), calls=%async_computation.4 | async-start | bytes 1376256 | tf_op jit(solution)/shard_map/all_to_all | solution.py:593
  378.2 19.1 %collective-permute-start.55 = (bf16[96,1536]{1,0:T(8,128)(2,1)}, bf16[96,1536]{1,0:T(8,128)(2,1)}, u32[]{:S(2)}, u32[]{:S(2)}) collective-permute-start(bf16[96,1536]{1,0:T(8,128)(2,1)} %copy-done.116), channel_id=1, source_target_pairs={{0,4},{1,5},{2,6},{3,7},{4,0},{5,1},{6,2},{7,3},{8,12},{9,13},{10,... | collective-permute-start | bytes 884744 | tf_op jit(solution)/shard_map/ppermute | solution.py:28
  385.1 36.1 %collective-permute-start.68 = (bf16[768,576]{0,1:T(8,128)(2,1)}, bf16[768,576]{0,1:T(8,128)(2,1)}, u32[]{:S(2)}, u32[]{:S(2)}) collective-permute-start(bf16[768,576]{0,1:T(8,128)(2,1)} %convolution_convert_fusion), channel_id=1, source_target_pairs={{0,8},{8,0},{16,24},{24,16},{1,9},{9,1},{17,25},{25,17},{2,10},{10... | collective-permute-start | bytes 2654216 | tf_op jit(solution)/shard_map/ppermute | solution.py:28
  404.8 21.5 %collective-permute-start.69 = (bf16[96,1664]{1,0:T(8,128)(2,1)}, bf16[96,1664]{1,0:T(8,128)(2,1)}, u32[]{:S(2)}, u32[]{:S(2)}) collective-permute-start(bf16[96,1664]{1,0:T(8,128)(2,1)} %get-tuple-element.221), channel_id=1, source_target_pairs={{0,8},{8,0},{16,24},{24,16},{1,9},{9,1},{17,25},{25,17},{2,10},{10... | collective-permute-start | bytes 958472 | tf_op jit(solution)/shard_map/ppermute | solution.py:28
  417.3 36.1 %all-to-all-start.4 = ((bf16[8,48,1728]{2,1,0:T(8,128)(2,1)}), bf16[8,48,1728]{2,1,0:T(8,128)(2,1)S(1)}, u32[]{:S(2)}, u32[]{:S(2)}) async-start(bf16[8,48,1728]{2,1,0:T(8,128)(2,1)} %bitcast.121), calls=%async_computation.6 | async-start | bytes 2752512 | tf_op jit(solution)/shard_map/all_to_all | solution.py:593
  426.3 26.0 %collective-permute-start.70 = (bf16[384,576]{0,1:T(8,128)(2,1)S(1)}, bf16[384,576]{0,1:T(8,128)(2,1)S(1)}, u32[]{:S(2)}, u32[]{:S(2)}) collective-permute-start(bf16[384,576]{0,1:T(8,128)(2,1)S(1)} %slice.186), channel_id=1, source_target_pairs={{0,16},{8,24},{16,0},{24,8},{1,17},{9,25},{17,1},{25,9},{2,18},{10... | collective-permute-start | bytes 1327112 | tf_op jit(solution)/shard_map/ppermute | solution.py:28
  432.5 24.9 %collective-permute-start.71 = (bf16[48,1664]{1,0:T(8,128)(2,1)}, bf16[48,1664]{1,0:T(8,128)(2,1)S(1)}, u32[]{:S(2)}, u32[]{:S(2)}) collective-permute-start(bf16[48,1664]{1,0:T(8,128)(2,1)} %split.13), channel_id=1, source_target_pairs={{0,16},{8,24},{16,0},{24,8},{1,17},{9,25},{17,1},{25,9},{2,18},{10... | collective-permute-start | bytes 479240 | tf_op jit(solution)/shard_map/ppermute | solution.py:28
  (177 other events, 1256.1 us)
Sparse Core Ops, SparseCore 0:
  91.3 100.2 all-gather.2
  193.2 53.5 all-gather.4
  249.1 52.8 reduce-scatter.2
  304.1 108.3 reduce-scatter.4
